TPU v7x, 256 devices: a whole 4x4x8 slice. The times are simulated.
256 devices in a mesh: ctx: 32 (over x, y, core), tp: 8 (over z).
Axes of the slice: x: 4, y: 4, z: 8, core: 2. Of those that a mesh axis runs over, the one named last changes fastest.
Arguments:
- queries: bfloat16 [8192, 4096], P('ctx', 'tp'), may hold values from -8 to 8
- key_rows: bfloat16 [8192, 4096], P('ctx', 'tp'), may hold values from -8 to 8
- value_rows: bfloat16 [8192, 4096], P('ctx', 'tp'), may hold values from -6 to 6
- log_decay: float32 [32, 8192], P('tp', 'ctx'), may hold values from -1 to 0, as said below
- write_rate: float32 [32, 8192], P('tp', 'ctx'), may hold values from 0 to 1, as said below
- gate_input: bfloat16 [8192, 4096], P('ctx', 'tp'), may hold values from -6 to 6
- norm_gain: float32 [128], replicated, may hold values from 0.1 to 1.9
- out_weight: bfloat16 [4096, 2048], P('tp'), may hold values from -0.09375 to 0.09375
Outputs:
- mixed: bfloat16 [8192, 2048], P(('ctx', 'tp'))
Inputs may be any that keep to these rules, and one draw needn't show every extreme that they name: `log_decay`: strictly negative. `write_rate`: strictly between 0 and 1.
All inputs are finite; a program needn't handle non-finite values.
Results may differ from a plain program's by a relative error of at most 0.02.
Values may be sent and summed in bfloat16 or wider, within the bound.
No kernel may reach another device: no remote copies, remote signals or barrier semaphores. Data moves between devices by JAX's collectives and lax.ppermute only.
A program may use at most 128 MiB of HBM per device.

v0:
```python
import jax
import jax.numpy as jnp
from jax import lax
from jax.sharding import PartitionSpec as P

DK = 128
DV = 128


highest = lax.Precision.HIGHEST
block_rows = 64
epsilon = 1e-06


def entering_2(value, axis, combine, identity):
    count, mine = (lax.axis_size(axis), lax.axis_index(axis))
    everything = jax.tree.map(
        lambda part, kind: lax.all_gather(part.astype(kind), axis),
        value,
        (jnp.bfloat16, jnp.bfloat16),
    )
    start = jax.tree.map(
        lambda part, zero: jnp.broadcast_to(jnp.asarray(zero, part.dtype), part.shape),
        value,
        identity,
    )

    def hop(k, before):
        reached = k < mine
        new = combine(
            before, jax.tree.map(lambda part, own: part[k].astype(own.dtype), everything, value)
        )
        return jax.tree.map(lambda a, b: jnp.where(reached, a, b), new, before)

    return lax.fori_loop(0, count, hop, start)


def unit_rows(values):
    return values / jnp.sqrt(jnp.sum(values * values, axis=-1, keepdims=True) + epsilon)


def block_terms(query_raw, key_raw, value_raw, log_steps, write_steps):
    key_width = key_raw.shape[-1]
    query_rows = unit_rows(query_raw.astype(jnp.float32)) * key_width ** (-0.5)
    key_rows = unit_rows(key_raw.astype(jnp.float32))
    value_rows = value_raw.astype(jnp.float32)
    length = query_rows.shape[-2]
    log_gamma = jnp.cumsum(log_steps, axis=-1)
    decays = jnp.exp(log_gamma)
    later_pos = jnp.arange(length)[:, None]
    earlier_pos = jnp.arange(length)[None, :]
    inclusive = later_pos >= earlier_pos
    strictly = later_pos > earlier_pos
    spread = log_gamma[..., :, None] - log_gamma[..., None, :]
    weights = jnp.where(inclusive, jnp.exp(jnp.where(inclusive, spread, 0.0)), 0.0)
    key_intersection = jnp.einsum("...cd,...sd->...cs", key_rows, key_rows, precision=highest)
    system = jnp.eye(length, dtype=jnp.float32) + write_steps[..., :, None] * jnp.where(
        strictly, weights * key_intersection, 0.0
    )
    right_side = jnp.concatenate(
        [write_steps[..., None] * value_rows, (write_steps * decays)[..., None] * key_rows], axis=-1
    )
    solved = lax.linalg.triangular_solve(
        system, right_side, left_side=True, lower=True, unit_diagonal=True
    )
    value_width = value_rows.shape[-1]
    new_values = solved[..., :value_width]
    erasers = solved[..., value_width:]
    scores = weights * jnp.einsum("...cd,...sd->...cs", query_rows, key_rows, precision=highest)
    local_out = jnp.einsum("...cs,...se->...ce", scores, new_values, precision=highest)
    query_map = decays[..., None] * query_rows - jnp.einsum(
        "...cs,...sd->...cd", scores, erasers, precision=highest
    )
    weighted = jnp.exp(log_gamma[..., -1:] - log_gamma)[..., None] * key_rows
    transit = decays[..., -1][..., None, None] * jnp.eye(key_width, dtype=jnp.float32) - jnp.einsum(
        "...cd,...ce->...de", weighted, erasers, precision=highest
    )
    state_add = jnp.einsum("...cd,...ce->...de", weighted, new_values, precision=highest)
    return (local_out, query_map, transit, state_add)


def to_blocks(values, heads):
    total = values.shape[0]
    return values.reshape(
        total // block_rows, block_rows, heads, values.shape[1] // heads
    ).transpose(0, 2, 1, 3)


def rates_to_blocks(values):
    heads, total = values.shape
    return values.reshape(heads, total // block_rows, block_rows).transpose(1, 0, 2)


def gated_rows(core, gate_input, norm_gain):
    total, heads, width = core.shape
    normed = core / jnp.sqrt(jnp.mean(core * core, axis=-1, keepdims=True) + epsilon)
    gate_values = gate_input.astype(jnp.float32).reshape(total, heads, width)
    return (
        (normed * norm_gain * jax.nn.silu(gate_values))
        .astype(jnp.bfloat16)
        .reshape(total, heads * width)
    )


def apply_map(step_map, state_in):
    return jnp.einsum("hde,hef->hdf", step_map, state_in, precision=highest)


def on_device(
    queries, key_rows, value_rows, log_decay, write_rate, gate_input, norm_gain, out_weight
):
    heads_here = log_decay.shape[0]
    tok_rows = queries.shape[0]
    local_out, query_map, transit, state_add = block_terms(
        to_blocks(queries, heads_here),
        to_blocks(key_rows, heads_here),
        to_blocks(value_rows, heads_here),
        rates_to_blocks(log_decay),
        rates_to_blocks(write_rate),
    )
    identity = jnp.broadcast_to(jnp.eye(DK, dtype=jnp.float32), (heads_here, DK, DK))
    zero_state = jnp.zeros((heads_here, DK, DV), jnp.float32)

    def advance_ends(carried, block):
        reach, local_state = carried
        step_map, step_add = block
        return ((apply_map(step_map, reach), apply_map(step_map, local_state) + step_add), None)

    (reach_end, local_end), _ = lax.scan(advance_ends, (identity, zero_state), (transit, state_add))

    def combine(earlier_pair, later_pair):
        return (
            apply_map(later_pair[0], earlier_pair[0]),
            apply_map(later_pair[0], earlier_pair[1]) + later_pair[1],
        )

    _, entering = entering_2((reach_end, local_end), "ctx", combine, (identity, zero_state))

    def replay(state_in, block):
        step_map, step_add = block
        return (apply_map(step_map, state_in) + step_add, state_in)

    _, block_starts = lax.scan(replay, entering, (transit, state_add))
    core_blocks = local_out + jnp.einsum(
        "nhcd,nhde->nhce", query_map, block_starts, precision=highest
    )
    core = core_blocks.transpose(0, 2, 1, 3).reshape(tok_rows, heads_here, DV)
    gated = gated_rows(core, gate_input, norm_gain)
    return lax.psum_scatter(
        jnp.dot(gated, out_weight, preferred_element_type=jnp.float32).astype(jnp.bfloat16),
        "tp",
        scatter_dimension=0,
        tiled=True,
    )


def solution(mesh):
    in_specs = (
        P("ctx", "tp"),
        P("ctx", "tp"),
        P("ctx", "tp"),
        P("tp", "ctx"),
        P("tp", "ctx"),
        P("ctx", "tp"),
        P(),
        P("tp", None),
    )
    out_specs = P(("ctx", "tp"), None)
    return jax.shard_map(
        on_device, mesh=mesh, in_specs=in_specs, out_specs=out_specs, check_vma=False
    )
```

profile of v0, /device:TPU:24, one launch (start us, length us, event | category | flops | bytes accessed | tf_op | source)
XLA Modules:
  0.0 338.4 jit_solution(16980302029617682247)
XLA Ops:
  12.4 1.9 reshape.94
  14.8 2.0 bitcast_multiply_fusion
  16.8 2.1 fusion.28
  18.9 80.0 %custom-call.3 = f32[4,4,1,64,64]{3,4,2,1,0:T(8,128)} custom-call(f32[4,4,1,64,64]{4,3,2,1,0:T(8,128)} %fusion.28), custom_call_target="InvertDiagBlocksLowerTriangular" | custom-call | tf_op jit(solution)/shard_map/triangular_solve | solution.py:63
  99.1 2.2 fusion.29
  101.3 3.2 fusion.45
  104.5 3.2 convolution_subtract_fusion
  108.4 20.2 %while.40 = (s32[]{:T(128)}, f32[4,128,128]{2,1,0:T(8,128)}, f32[4,128,128]{2,1,0:T(8,128)}, f32[4,4,128,128]{3,2,1,0:T(8,128)S(1)}, f32[4,4,128,128]{3,2,1,0:T(8,128)}, /*index=5*/s32[]{:T(128)}, s32[]{:T(128)}) while((s32[]{:T(128)}, f32[4,128,128]{2,1,0:T(8,128)}, f32[4,128,128]{2,1,0:T(8,128)}, ...), condition=%wide.region_4.5_spmd.clone, body=%wide.region_3.4_spmd.clone.sunk | while | flops 201457664 | bytes 2885218 | solution.py:129
  111.4 2.1 convolution_add_fusion.7
  116.5 2.1 convolution_add_fusion.7
  121.5 2.1 convolution_add_fusion.7
  126.6 2.1 convolution_add_fusion.7
  128.6 1.8 convert_element_type.84
  130.5 1.6 convert_element_type.85
  132.5 2.5 convolution_multiply_fusion.1
  134.9 1.5 fusion.47
  136.4 1.5 convolution_subtract_fusion.1
  137.9 46.1 %all-gather.5.cloned.1.call-done = bf16[128,128,128]{2,1,0:T(8,128)(2,1)} async-done(((bf16[4,128,128]{2,1,0:T(8,128)(2,1)}), bf16[128,128,128]{2,1,0:T(8,128)(2,1)}) %all-gather.5.cloned.1.call-update) | async-done | bytes 4194320 | tf_op jit(solution)/shard_map/all_gather | solution.py:18
  184.0 53.1 %all-gather.7.cloned.1.call-done = bf16[128,128,128]{2,1,0:T(8,128)(2,1)} async-done(((bf16[4,128,128]{2,1,0:T(8,128)(2,1)}), bf16[128,128,128]{2,1,0:T(8,128)(2,1)}) %all-gather.7.cloned.1.call-update) | async-done | bytes 4194320 | tf_op jit(solution)/shard_map/all_gather | solution.py:18
  237.1 42.1 %while.41 = (s32[]{:T(128)}, f32[4,128,128]{2,1,0:T(8,128)S(1)}, s32[]{:T(128)}, bf16[32,4,128,128]{3,2,1,0:T(8,128)(2,1)}, bf16[32,4,128,128]{3,2,1,0:T(8,128)(2,1)}, /*index=5*/s32[]{:T(128)}, s32[]{:T(128)}) while((s32[]{:T(128)}, f32[4,128,128]{2,1,0:T(8,128)S(1)}, s32[]{:T(128)}, bf16[32,4,128,128]{3,2,1,0:T(8,128)(2,1)}, ...), condition=%wide.region_6.7_spmd.clone, body=%wide.region_5.6_spmd.clone.sunk | while | flops 100990976 | bytes 1575527 | solution.py:35
  279.3 8.8 %while.39 = (s32[]{:T(128)}, f32[4,128,128]{2,1,0:T(8,128)S(1)}, f32[4,4,128,128]{3,2,1,0:T(8,128)}, f32[4,4,128,128]{3,2,1,0:T(8,128)}, f32[4,4,128,128]{3,2,1,0:T(8,128)}, /*index=5*/s32[]{:T(128)}) while((s32[]{:T(128)}, f32[4,128,128]{2,1,0:T(8,128)S(1)}, f32[4,4,128,128]{3,2,1,0:T(8,128)}, f32[4,4,128,128]{3,2,1,0:T(8,128)}, ...), condition=%wide.region_8.9_spmd, body=%wide.region_7.8_spmd.sunk | while | flops 100728832 | bytes 2098257 | solution.py:143
  288.1 2.6 multiply_reduce_fusion
  291.5 1.8 convolution_convert_fusion
  293.3 38.6 %reduce-scatter.2.cloned.1.call-done = bf16[32,2048]{1,0:T(8,128)(2,1)} async-done(((bf16[256,2048]{1,0:T(8,128)(2,1)}), bf16[32,2048]{1,0:T(8,128)(2,1)}) %reduce-scatter.2.cloned.1.call-update) | async-done | bytes 131088 | tf_op jit(solution)/shard_map/reduce_scatter | solution.py:149
  (142 shorter events, 69.7 us)
Async XLA Ops:
  6.5 284.9 %copy-start = (bf16[512,2048]{1,0:T(8,128)(2,1)S(1)}, bf16[512,2048]{1,0:T(8,128)(2,1)}, u32[]{:S(2)}) copy-start(bf16[512,2048]{1,0:T(8,128)(2,1)} %param.21) | copy-start | bytes 6291460
  6.5 177.5 %all-gather.5.cloned.1.call-start = ((), (), s32[]{:S(2)}) async-start(), calls=%async_computation.2 | async-start | bytes 4325376 | tf_op jit(solution)/shard_map/all_gather | solution.py:18
  8.6 5.8 %copy-start.6 = (f32[4,64,4,128]{3,2,1,0:T(4,128)}, f32[4,64,4,128]{3,2,1,0:T(4,128)S(1)}, u32[]{:S(2)}) copy-start(f32[4,64,4,128]{3,2,1,0:T(4,128)S(1)} %reshape.92) | copy-start | bytes 1572868
  10.0 91.4 %copy-start.2 = (f32[4,64,4,128]{3,2,1,0:T(4,128)}, f32[4,64,4,128]{3,2,1,0:T(4,128)S(1)}, u32[]{:S(2)}) copy-start(f32[4,64,4,128]{3,2,1,0:T(4,128)S(1)} %reshape.93) | copy-start | bytes 1572868
  101.3 3.2 copy-start.3
  108.4 24.0 %copy-start.8 = (f32[128]{0:T(128)S(1)}, f32[128]{0:T(128)}, u32[]{:S(2)}) copy-start(f32[128]{0:T(128)} %param.20) | copy-start | bytes 1540
  128.6 9.3 %copy-start.1 = (f32[4,4,128,128]{3,2,1,0:T(8,128)}, f32[4,4,128,128]{3,2,1,0:T(8,128)S(1)}, u32[]{:S(2)}) copy-start(f32[4,4,128,128]{3,2,1,0:T(8,128)S(1)} %get-tuple-element.392) | copy-start | bytes 3145732
  130.5 106.7 %all-gather.7.cloned.1.call-start = ((), (), s32[]{:S(2)}) async-start(), calls=%async_computation.3 | async-start | bytes 4325376 | tf_op jit(solution)/shard_map/all_gather | solution.py:18
  132.2 199.7 %reduce-scatter.2.cloned.1.call-start = ((), (), s32[]{:S(2)}) async-start(), calls=%async_computation.1 | async-start | bytes 1179648 | tf_op jit(solution)/shard_map/reduce_scatter | solution.py:149
  132.4 2.5 copy-start.4
  132.4 4.0 %copy-start.7 = (f32[4,64,4,128]{3,2,1,0:T(4,128)S(1)}, f32[4,64,4,128]{3,2,1,0:T(4,128)}, u32[]{:S(2)}) copy-start(f32[4,64,4,128]{3,2,1,0:T(4,128)} %copy-done.6) | copy-start | bytes 1572868
  279.2 8.8 %copy-start.5 = (f32[4,4,64,128]{3,2,1,0:T(8,128)S(1)}, f32[4,4,64,128]{3,2,1,0:T(8,128)}, u32[]{:S(2)}) copy-start(f32[4,4,64,128]{3,2,1,0:T(8,128)} %fusion.47) | copy-start | bytes 1572868
  288.0 3.4 %copy-start.9 = (bf16[256,512]{1,0:T(8,128)(2,1)S(1)}, bf16[256,512]{1,0:T(8,128)(2,1)}, u32[]{:S(2)}) copy-start(bf16[256,512]{1,0:T(8,128)(2,1)} %param.19) | copy-start | bytes 786436
Sparse Core Ops, SparseCore 0:
  130.6 53.3 all-gather.4
  186.6 50.5 all-gather.6
  293.4 38.4 reduce-scatter.1
where the time goes:
time: 340 us; the launch traced here: 338 us
  waiting for transfers between devices  138 us (41%)
  other arithmetic  87.4 us (26%)
  matrix products  79 us (23%)
  local copies, waits for them, and re-layouts  19.1 us (6%)
  between operations  13.4 us (4%)
    all_gather x2, waiting for transfers between devices, entering_2(): lax.all_gather(part.astype(kind), axis)  99.2 us
    another operation x3, other arithmetic, block_terms(): lax.linalg.triangular_solve(system, right_side, left_side=True, lower=Tru...  80 us
    dot_general x44, matrix products, apply_map(): return jnp.einsum('hde,hef->hdf', step_map, state_in, precision=highest)  58.5 us
    reduce_scatter x1, waiting for transfers between devices, on_device(): lax.psum_scatter(jnp.dot(gated, out_weight, preferred_element_type=jnp.fl...  38.6 us
    while x44, local copies, waits for them, and re-layouts  8.29 us
  transfers between devices with their start and end apart: 3, of which 3 were waited for; matrix products, arithmetic and copies ran while one was open for 2% of the time, Pallas kernels for 0%

commit v1 on v0

v1 whole, which is shorter than its diff:
```python
import jax
import jax.numpy as jnp
from jax import lax
from jax.experimental import pallas as pl
from jax.experimental.pallas import tpu as pltpu
from jax.sharding import PartitionSpec as P

F32 = jnp.float32
BF16 = jnp.bfloat16
EPS = 1e-6
HD = 128
C = 128
HPC = 2
NC = 4
NP = HPC * NC
SUB = 16


def dot(a, b):
    return lax.dot_general(a, b, (((1,), (0,)), ((), ())), preferred_element_type=F32)


def dot_nt(a, b):
    return lax.dot_general(a, b, (((1,), (1,)), ((), ())), preferred_element_type=F32)


def dot_tn(a, b):
    return lax.dot_general(a, b, (((0,), (0,)), ((), ())), preferred_element_type=F32)


def split(a):
    hi = a.astype(BF16)
    lo = (a - hi.astype(F32)).astype(BF16)
    return hi, lo


def lanes(*parts):
    return jnp.concatenate(parts, axis=1)


def rows(*parts):
    return jnp.concatenate(parts, axis=0)


def dot_sq(a, b):
    ah, al = split(a)
    bh, bl = split(b)
    out = dot(lanes(ah, al), rows(lanes(bh, bl), lanes(bh, jnp.zeros_like(bl))))
    return out[:, :C] + out[:, C:]


def dot_wide(a, b):
    ah, al = split(a)
    bh, bl = split(b)
    return dot(lanes(ah, al), rows(bh, bh)) + dot(ah, bl)


def dot_exact_left(a, b):
    bh, bl = split(b)
    out = dot(a, lanes(bh, bl))
    return out[:, :HD] + out[:, HD:]


def iota2(shape, dim):
    return lax.broadcasted_iota(jnp.int32, shape, dim)


def put_tokens(core, own, other, dst):
    half = own.shape[0]
    width = HPC * HD

    @pl.when(core == 0)
    def _():
        dst[:half, :] = own[:, :width]
        dst[half:, :] = other[:, :width]

    @pl.when(core != 0)
    def _():
        dst[:half, :] = other[:, width:]
        dst[half:, :] = own[:, width:]


def put_rates(core, own, other, dst):
    for h in range(HPC):
        for n in range(NC):
            p = h * NC + n
            s = slice((n % 2) * C, (n % 2) * C + C)

            @pl.when(core == 0)
            def _(h=h, n=n, p=p, s=s):
                src = own if n < 2 else other
                dst[p : p + 1, :] = src[h : h + 1, s]

            @pl.when(core != 0)
            def _(h=h, n=n, p=p, s=s):
                src = other if n < 2 else own
                dst[p : p + 1, :] = src[HPC + h : HPC + h + 1, s]


def maps_kernel(
    k_ref, ko_ref, v_ref, vo_ref, ld_ref, ldo_ref, wr_ref, wro_ref,
    ks_ref, wu_ref, vec_ref, vect_ref, map_ref, total_ref,
    vs, lds, wrs, xs, ts,
):
    core = lax.rem(lax.axis_index("ctx"), 2)
    put_tokens(core, k_ref, ko_ref, ks_ref)
    put_tokens(core, v_ref, vo_ref, vs)
    put_rates(core, ld_ref, ldo_ref, lds)
    put_rates(core, wr_ref, wro_ref, wrs)
    row = iota2((C, C), 0)
    col = iota2((C, C), 1)
    eye = row == col
    strict = row > col
    upper = (row <= col).astype(BF16)

    def keys(p):
        h, n = divmod(p, NC)
        return ks_ref[n * C : n * C + C, h * HD : h * HD + HD]

    def values(p):
        h, n = divmod(p, NC)
        return vs[n * C : n * C + C, h * HD : h * HD + HD]

    steps = lds[...]
    beta = wrs[...]
    s0 = steps.astype(BF16)
    r1 = steps - s0.astype(F32)
    s1 = r1.astype(BF16)
    s2 = (r1 - s1.astype(F32)).astype(BF16)
    g = dot(s0, upper) + (dot(s1, upper) + dot(s2, upper))
    gram = []
    norms = []
    for p in range(NP):
        kp = keys(p)
        kk = dot_nt(kp, kp)
        gram.append(kk)
        norms.append(jnp.sum(jnp.where(eye, kk, 0.0), axis=0, keepdims=True))
    rn = 1.0 / jnp.sqrt(rows(*norms) + EPS)
    eg = jnp.exp(g)
    gend = g[:, C - 1 : C]
    tail = jnp.exp(gend - g) * rn
    vec = rows(g, beta * rn, tail, rn, eg, beta * eg * rn, beta, beta)
    vec_ref[...] = vec
    vect = rows(vec, vec).T
    vect_ref[...] = vect[:, : NP * 8]

    def column(kind, p):
        i = kind * NP + p
        return vect[:, i : i + 1]

    lower = []
    for p in range(NP):
        spread = column(0, p) - g[p : p + 1, :]
        w = jnp.exp(jnp.where(strict, spread, 0.0))
        w = w * (column(1, p) * rn[p : p + 1, :]) * gram[p]
        lower.append(jnp.where(strict, w, 0.0))
    lane_block = lax.div(iota2((SUB, C), 1), SUB)
    for p in range(NP):
        acc = jnp.zeros((SUB, C), F32)
        for b in range(C // SUB):
            acc = acc + jnp.where(lane_block == b, lower[p][b * SUB : b * SUB + SUB, :], 0.0)
        xs[pl.ds(p, SUB, stride=NP), :] = acc
    base = row - SUB * lax.div(col, SUB)
    select = lanes(*[(base == j).astype(BF16) for j in range(SUB)])
    xh, xl = split(xs[...])
    spread_coef = dot(lanes(xh, xl), rows(select, select))
    lane_in = lax.rem(iota2((NP, C), 1), SUB)
    solved = []
    for i in range(SUB):
        acc = (lane_in == i).astype(F32)
        for j in range(i):
            acc = acc - spread_coef[i * NP : i * NP + NP, j * C : j * C + C] * solved[j]
        solved.append(acc)
        ts[i * NP : i * NP + NP, :] = acc
    inverse = []
    for p in range(NP):
        tp = ts[pl.ds(p, SUB, stride=NP), :]
        inverse.append(rows(*[jnp.where(lane_block == b, tp, 0.0) for b in range(C // SUB)]))
    size = SUB
    while size < C:
        rb = lax.div(row, size)
        cb = lax.div(col, size)
        mask = (rb == cb + 1) & (lax.rem(rb, 2) == 1)
        mids = [dot_sq(jnp.where(mask, lower[p], 0.0), inverse[p]) for p in range(NP)]
        inverse = [inverse[p] - dot_sq(inverse[p], mids[p]) for p in range(NP)]
        size *= 2
    maps = []
    for p in range(NP):
        h, n = divmod(p, NC)
        kp = keys(p)
        vp = values(p)
        eh, el = split(inverse[p] * vec[5 * NP + p : 5 * NP + p + 1, :])
        uh, ul = split(inverse[p] * beta[p : p + 1, :])
        erase = dot(lanes(eh, el), rows(kp, kp))
        write = dot(lanes(uh, ul), rows(vp, vp))
        both = lanes(erase, write)
        wu_ref[p] = both.astype(BF16)
        wh, wl = split(both * column(2, p))
        out = dot_tn(rows(kp, kp), rows(wh, wl))
        decay = jnp.where(eye, jnp.exp(gend[p : p + 1, :]), 0.0)
        m = lanes(decay - out[:, :HD], out[:, HD:])
        map_ref[p] = m
        maps.append(m)

    def follow(later, earlier):
        out = dot_wide(later[:, :HD], earlier)
        return lanes(out[:, :HD], out[:, HD:] + later[:, HD:])

    for h in range(HPC):
        m0, m1, m2, m3 = maps[h * NC : h * NC + NC]
        total_ref[h] = follow(follow(m3, m2), follow(m1, m0)).astype(BF16)


def reads_kernel(
    q_ref, qo_ref, ks_ref, wu_ref, vec_ref, vect_ref, map_ref, qeff_ref, local_ref, qs
):
    core = lax.rem(lax.axis_index("ctx"), 2)
    put_tokens(core, q_ref, qo_ref, qs)
    row = iota2((C, C), 0)
    col = iota2((C, C), 1)
    incl = row >= col
    scale = HD**-0.5
    vec = vec_ref[...]
    vect = vect_ref[...]

    def column(kind, p):
        i = kind * NP + p
        return vect[:, i : i + 1]

    def follow(later, earlier):
        out = dot_wide(later[:, :HD], earlier)
        return lanes(out[:, :HD], out[:, HD:] + later[:, HD:])

    for h in range(HPC):
        prefix = None
        for n in range(NC):
            p = h * NC + n
            qp = qs[n * C : n * C + C, h * HD : h * HD + HD]
            kp = ks_ref[n * C : n * C + C, h * HD : h * HD + HD]
            qf = qp.astype(F32)
            rq = scale / jnp.sqrt(jnp.sum(qf * qf, axis=1, keepdims=True) + EPS)
            w = jnp.exp(jnp.where(incl, column(0, p) - vec[p : p + 1, :], 0.0))
            scores = w * (rq * vec[3 * NP + p : 3 * NP + p + 1, :]) * dot_nt(qp, kp)
            sh, sl = split(jnp.where(incl, scores, 0.0))
            wu = wu_ref[p]
            out = dot(lanes(sh, sl), rows(wu, wu))
            qeff = (column(4, p) * rq) * qf - out[:, :HD]
            local = out[:, HD:]
            if n > 0:
                out = dot_wide(qeff, prefix)
                qeff = out[:, :HD]
                local = local + out[:, HD:]
            prefix = map_ref[p] if n == 0 else follow(map_ref[p], prefix)
            qeff_ref[h, n * C : n * C + C, :] = qeff.astype(BF16)
            local_ref[h, n * C : n * C + C, :] = local


def row_kernel(m_ref, r1_ref, r2_ref, r3_ref, total_ref, prefix_ref, slots):
    y = lax.rem(lax.div(lax.axis_index("ctx"), 2), 4)
    for d, ref in enumerate((m_ref, r1_ref, r2_ref, r3_ref)):
        slots[lax.rem(y + 4 - d, 4)] = ref[...]
    eye = (iota2((HD, 2 * HD), 0) == iota2((HD, 2 * HD), 1)).astype(F32)
    for h in range(HPC):
        m0, m1, m2, m3 = (slots[i, h] for i in range(4))
        b1, b2, b3 = (m[:, HD:].astype(F32) for m in (m1, m2, m3))
        t01 = dot(m1[:, :HD], m0)
        t01 = lanes(t01[:, :HD], t01[:, HD:] + b1)
        t23 = dot(m3[:, :HD], m2)
        t23 = lanes(t23[:, :HD], t23[:, HD:] + b3)
        th, tl = split(t01)
        t012 = dot(m2[:, :HD], th) + dot(m2[:, :HD], tl)
        t012 = lanes(t012[:, :HD], t012[:, HD:] + b2)
        total = dot_wide(t23[:, :HD], t01)
        total_ref[h] = lanes(total[:, :HD], total[:, HD:] + t23[:, HD:]).astype(BF16)
        prefix_ref[h] = jnp.where(
            y == 0, eye, jnp.where(y == 1, m0.astype(F32), jnp.where(y == 2, t01, t012))
        )


def gated_kernel(
    r1_ref, r2_ref, r3_ref, prefix_ref, qeff_ref, local_ref, gate_ref, gateo_ref, gain_ref,
    keep_ref, send_ref, gs,
):
    core = lax.rem(lax.axis_index("ctx"), 2)
    put_tokens(core, gate_ref, gateo_ref, gs)
    gain = gain_ref[...]
    half = gate_ref.shape[0]
    entering = []
    for h in range(HPC):
        state = r3_ref[h][:, HD:].astype(F32)
        for ref in (r2_ref, r1_ref):
            m = ref[h]
            state = dot_exact_left(m[:, :HD], state) + m[:, HD:].astype(F32)
        m = prefix_ref[h]
        state = dot_sq(m[:, :HD], state) + m[:, HD:]
        entering.append(split(state))
    for h in range(HPC):
        sh, sl = entering[h]
        out = dot(qeff_ref[h], lanes(sh, sl))
        core_rows = local_ref[h] + out[:, :HD] + out[:, HD:]
        mean = jnp.mean(core_rows * core_rows, axis=1, keepdims=True)
        gate = gs[:, h * HD : h * HD + HD].astype(F32)
        silu = gate / (1.0 + jnp.exp(-gate))
        out = (core_rows / jnp.sqrt(mean + EPS) * gain * silu).astype(BF16)
        s = slice(h * HD, h * HD + HD)

        @pl.when(core == 0)
        def _():
            keep_ref[:, s] = out[:half]
            send_ref[:, s] = out[half:]

        @pl.when(core != 0)
        def _():
            keep_ref[:, s] = out[half:]
            send_ref[:, s] = out[:half]


def project_kernel(keep_ref, recv_ref, w_ref, *refs):
    outs, lhs = refs[:-1], refs[-1]
    core = lax.rem(lax.axis_index("ctx"), 2)
    me = lax.axis_index("tp")
    width = HPC * HD
    chunk = 32
    for d in range(8):
        start = pl.multiple_of(lax.rem(me + d, 8) * chunk, chunk)
        here = slice(d * chunk, d * chunk + chunk)
        kept = keep_ref[pl.ds(start, chunk), :]
        got = recv_ref[pl.ds(start, chunk), :]

        @pl.when(core == 0)
        def _(here=here, kept=kept, got=got):
            lhs[here, :width] = kept
            lhs[here, width:] = got

        @pl.when(core != 0)
        def _(here=here, kept=kept, got=got):
            lhs[here, :width] = got
            lhs[here, width:] = kept

    step = 512
    for j in range(w_ref.shape[1] // step):
        s = slice(j * step, j * step + step)
        out = dot(lhs[...], w_ref[:, s]).astype(BF16)
        for d, ref in zip((0, 1, 2, 3, 5, 6, 7), (outs[0], outs[1], outs[2], outs[3], outs[6], outs[7], outs[8])):
            ref[:, s] = out[d * chunk : d * chunk + chunk]
        ref = outs[4] if j < 2 else outs[5]
        t = slice((j % 2) * step, (j % 2) * step + step)
        ref[:, t] = out[4 * chunk : 5 * chunk]


def partial_kernel(a_ref, a3_ref, a4_ref, b_ref, b3_ref, b4_ref, ao_ref, bo_ref):
    half = a4_ref.shape[1]
    a = a_ref[...].astype(F32) + a3_ref[...].astype(F32)
    b = b_ref[...].astype(F32) + b3_ref[...].astype(F32)
    ao_ref[:, :half] = (a[:, :half] + a4_ref[...].astype(F32)).astype(BF16)
    ao_ref[:, half:] = a[:, half:].astype(BF16)
    bo_ref[:, :half] = b[:, :half].astype(BF16)
    bo_ref[:, half:] = (b[:, half:] + b4_ref[...].astype(F32)).astype(BF16)


def sum_kernel(a_ref, b_ref, c_ref, d_ref, e_ref, out_ref):
    total = a_ref[...].astype(F32)
    for ref in (b_ref, c_ref, d_ref, e_ref):
        total = total + ref[...].astype(F32)
    out_ref[...] = total.astype(BF16)


def call(kernel, outs, args, scratch=(), flops=0, moved=0):
    vmem = pl.BlockSpec(memory_space=pltpu.VMEM)
    return pl.pallas_call(
        kernel,
        out_shape=[jax.ShapeDtypeStruct(s, t) for s, t in outs],
        in_specs=[vmem] * len(args),
        out_specs=[vmem] * len(outs),
        scratch_shapes=list(scratch),
        compiler_params=pltpu.CompilerParams(vmem_limit_bytes=32 * 1024 * 1024),
        cost_estimate=pl.CostEstimate(flops=flops, bytes_accessed=moved, transcendentals=0),
    )(*args)


def on_device(q, k, v, ld, wr, gate, gain, w):
    tokens = q.shape[0]
    chip = 2 * tokens
    ring = lax.axis_size("tp")
    n_ctx = lax.axis_size("ctx")
    cross = [(i, i ^ 1) for i in range(n_ctx)]

    def swap(a):
        return lax.ppermute(a, "ctx", cross)

    def along_y(a, d):
        pairs = []
        for i in range(n_ctx):
            x, y, c = i // 8, i // 2 % 4, i % 2
            pairs.append((i, (x * 4 + (y + d) % 4) * 2 + c))
        return lax.ppermute(a, "ctx", pairs)

    def along_x(a, d):
        return lax.ppermute(a, "ctx", [(i, i + 8 * d) for i in range(n_ctx - 8 * d)])

    def along_z(a, d):
        return lax.ppermute(a, "tp", [(i, (i + d) % ring) for i in range(ring)])

    ko, vo, ldo, wro = swap(k), swap(v), swap(ld), swap(wr)
    qo, gateo = swap(q), swap(gate)
    ks, wu, vec, vect, maps, total = call(
        maps_kernel,
        [
            ((chip, HPC * HD), BF16),
            ((NP, C, 2 * HD), BF16),
            ((8 * NP, C), F32),
            ((C, 8 * NP), F32),
            ((NP, HD, 2 * HD), F32),
            ((HPC, HD, 2 * HD), BF16),
        ],
        (k, ko, v, vo, ld, ldo, wr, wro),
        [
            pltpu.VMEM((chip, HPC * HD), BF16),
            pltpu.VMEM((NP, C), F32),
            pltpu.VMEM((NP, C), F32),
            pltpu.VMEM((SUB * NP, C), F32),
            pltpu.VMEM((SUB * NP, C), F32),
        ],
        flops=10**9,
        moved=2**20,
    )
    around = [along_y(total, d) for d in (1, 2, 3)]
    qeff, local = call(
        reads_kernel,
        [((HPC, chip, HD), BF16), ((HPC, chip, HD), F32)],
        (q, qo, ks, wu, vec, vect, maps),
        [pltpu.VMEM((chip, HPC * HD), BF16)],
        flops=10**9,
        moved=2**20,
    )
    row_total, prefix = call(
        row_kernel,
        [((HPC, HD, 2 * HD), BF16), ((HPC, HD, 2 * HD), F32)],
        (total, *around),
        [pltpu.VMEM((4, HPC, HD, 2 * HD), BF16)],
        flops=10**8,
        moved=2**19,
    )
    before = [along_x(row_total, d) for d in (1, 2, 3)]
    keep, send = call(
        gated_kernel,
        [((tokens, HPC * HD), BF16)] * 2,
        (*before, prefix, qeff, local, gate, gateo, gain.reshape(1, HD)),
        [pltpu.VMEM((chip, HPC * HD), BF16)],
        flops=10**8,
        moved=2**20,
    )
    recv = swap(send)
    width = w.shape[1]
    chunk = tokens // ring
    p0, p1, p2, p3, p4a, p4b, p5, p6, p7 = call(
        project_kernel,
        [((chunk, width), BF16)] * 4 + [((chunk, width // 2), BF16)] * 2 + [((chunk, width), BF16)] * 3,
        (keep, recv, w),
        [pltpu.VMEM((tokens, w.shape[0]), BF16)],
        flops=10**9,
        moved=2**22,
    )
    a3, b3 = along_z(p3, 1), along_z(p5, -1)
    a4, b4 = along_z(p4a, 2), along_z(p4b, -2)
    a1, b1 = along_z(p1, 1), along_z(p7, -1)
    pa, pb = call(partial_kernel, [((chunk, width), BF16)] * 2, (p2, a3, a4, p6, b3, b4))
    a2, b2 = along_z(pa, 2), along_z(pb, -2)
    return call(sum_kernel, [((chunk, width), BF16)], (p0, a1, b1, a2, b2))[0]


def solution(mesh):
    in_specs = (
        P("ctx", "tp"),
        P("ctx", "tp"),
        P("ctx", "tp"),
        P("tp", "ctx"),
        P("tp", "ctx"),
        P("ctx", "tp"),
        P(),
        P("tp", None),
    )
    return jax.shard_map(
        on_device, mesh=mesh, in_specs=in_specs, out_specs=P(("ctx", "tp"), None), check_vma=False
    )
```

time: 340 us -> 66.1 us (0.19)
  the two profiles are of different devices: /device:TPU:24 before, /device:TPU:2 now
where the time goes in v1:
time: 66.1 us; the launch traced here: 65.8 us
  starting transfers between devices  29.6 us (45%)
  waiting for transfers between devices  22 us (33%)
  Pallas kernels  10.7 us (16%)
  local copies, waits for them, and re-layouts  3.29 us (5%)
    ppermute x8, starting transfers between devices, along_z(): return lax.ppermute(a, 'tp', [(i, (i + d) % ring) for i in range(ring)])  16.5 us
    pallas_call x7, Pallas kernels, call(): pl.pallas_call(kernel, out_shape=[jax.ShapeDtypeStruct(s, t) for s, t in...  10.7 us
    ppermute x8, waiting for transfers between devices, along_z(): return lax.ppermute(a, 'tp', [(i, (i + d) % ring) for i in range(ring)])  8.35 us
    ppermute x3, waiting for transfers between devices, along_y(): return lax.ppermute(a, 'ctx', pairs)  8.09 us
    ppermute x3, starting transfers between devices, along_x(): lax.ppermute(a, 'ctx', [(i, i + 8 * d) for i in range(n_ctx - 8 * d)])  7.25 us
    ppermute x3, starting transfers between devices, along_y(): return lax.ppermute(a, 'ctx', pairs)  4.69 us
    unnamed x16, local copies, waits for them, and re-layouts  3.29 us
    ppermute x3, waiting for transfers between devices, along_x(): lax.ppermute(a, 'ctx', [(i, i + 8 * d) for i in range(n_ctx - 8 * d)])  3.22 us
  transfers between devices with their start and end apart: 21, of which 9 were waited for; matrix products, arithmetic and copies ran while one was open for 0% of the time, Pallas kernels for 12%

profile of v1, /device:TPU:2, one launch (start us, length us, event | category | flops | bytes accessed | tf_op | source)
XLA Modules:
  0.0 65.8 jit_solution(6578536550394593557)
XLA Ops:
  1.1 1.0 %collective-permute-done.2.ldo_ref = f32[4,256]{1,0:T(4,128)S(1)} collective-permute-done((f32[4,256]{1,0:T(4,128)}, f32[4,256]{1,0:T(4,128)S(1)}, u32[]{:S(2)}, u32[]{:S(2)}) %collective-permute-start.2) | collective-permute-done | bytes 4128 | tf_op jit(solution)/shard_map/ppermute | solution.py:389
  2.2 0.9 %copy-done.3 = bf16[256,512]{1,0:T(8,128)(2,1)S(1)} copy-done((bf16[256,512]{1,0:T(8,128)(2,1)S(1)}, bf16[256,512]{1,0:T(8,128)(2,1)}, u32[]{:S(2)}) %copy-start.3) | copy-done | bytes 262168
  3.1 0.9 %copy-done.4 = bf16[256,512]{1,0:T(8,128)(2,1)S(1)} copy-done((bf16[256,512]{1,0:T(8,128)(2,1)S(1)}, bf16[256,512]{1,0:T(8,128)(2,1)}, u32[]{:S(2)}) %copy-start.4) | copy-done | bytes 262168
  5.4 4.8 %shard_map.82 = (bf16[512,256]{1,0:T(8,128)(2,1)S(1)}, bf16[8,128,256]{2,1,0:T(8,128)(2,1)S(1)}, f32[64,128]{1,0:T(8,128)S(1)}, f32[128,64]{1,0:T(8,128)S(1)}, f...) custom-call(bf16[256,512]{1,0:T(8,128)(2,1)S(1)} %copy-done.3, ...), custom_call_target="tpu_custom_call" | custom-call | flops 1000000000 | bytes 1048576 | tf_op jit(solution)/shard_map/pallas_call | solution.py:370
  10.3 3.1 %collective-permute-start.6 = (bf16[2,128,256]{2,1,0:T(8,128)(2,1)S(1)}, bf16[2,128,256]{2,1,0:T(8,128)(2,1)S(1)}, u32[]{:S(2)}, u32[]{:S(2)}) collective-permute-start(bf16[2,128,256]{2,1,0:T(8,128)(2,1)S(1)} %get-tuple-element.28.m_ref), channel_id=1, source_target_pairs={{0,48},{8,56},{16,0},{24,8},{32,16},{40,24},{48,32},{56,40},{64,11... | collective-permute-start | bytes 393224 | tf_op jit(solution)/shard_map/ppermute | solution.py:396
  14.0 1.0 %collective-permute-start.4 = (bf16[2,128,256]{2,1,0:T(8,128)(2,1)S(1)}, bf16[2,128,256]{2,1,0:T(8,128)(2,1)S(1)}, u32[]{:S(2)}, u32[]{:S(2)}) collective-permute-start(bf16[2,128,256]{2,1,0:T(8,128)(2,1)S(1)} %get-tuple-element.28.m_ref), channel_id=1, source_target_pairs={{0,16},{8,24},{16,32},{24,40},{32,48},{40,56},{48,0},{56,8},{64,80... | collective-permute-start | bytes 393224 | tf_op jit(solution)/shard_map/ppermute | solution.py:396
  15.0 4.4 %collective-permute-done.6.r3_ref = bf16[2,128,256]{2,1,0:T(8,128)(2,1)S(1)} collective-permute-done((bf16[2,128,256]{2,1,0:T(8,128)(2,1)S(1)}, bf16[2,128,256]{2,1,0:T(8,128)(2,1)S(1)}, u32[]{:S(2)}, u32[]{:S(2)}) %collective-permute-start.6) | collective-permute-done | bytes 131104 | tf_op jit(solution)/shard_map/ppermute | solution.py:396
  19.4 1.9 %collective-permute-done.5.r2_ref = bf16[2,128,256]{2,1,0:T(8,128)(2,1)S(1)} collective-permute-done((bf16[2,128,256]{2,1,0:T(8,128)(2,1)S(1)}, bf16[2,128,256]{2,1,0:T(8,128)(2,1)S(1)}, u32[]{:S(2)}, u32[]{:S(2)}) %collective-permute-start.5) | collective-permute-done | bytes 131104 | tf_op jit(solution)/shard_map/ppermute | solution.py:396
  21.3 1.8 %collective-permute-done.4.r1_ref = bf16[2,128,256]{2,1,0:T(8,128)(2,1)S(1)} collective-permute-done((bf16[2,128,256]{2,1,0:T(8,128)(2,1)S(1)}, bf16[2,128,256]{2,1,0:T(8,128)(2,1)S(1)}, u32[]{:S(2)}, u32[]{:S(2)}) %collective-permute-start.4) | collective-permute-done | bytes 131104 | tf_op jit(solution)/shard_map/ppermute | solution.py:396
  24.4 4.7 %collective-permute-start.8 = (bf16[2,128,256]{2,1,0:T(8,128)(2,1)S(1)}, bf16[2,128,256]{2,1,0:T(8,128)(2,1)S(1)}, u32[]{:S(2)}, u32[]{:S(2)}) collective-permute-start(bf16[2,128,256]{2,1,0:T(8,128)(2,1)S(1)} %get-tuple-element.29), channel_id=1, source_target_pairs={{0,128},{8,136},{16,144},{24,152},{32,160},{40,168},{48,176},{56,1... | collective-permute-start | bytes 393224 | tf_op jit(solution)/shard_map/ppermute | solution.py:399
  29.1 1.9 %collective-permute-start.7 = (bf16[2,128,256]{2,1,0:T(8,128)(2,1)S(1)}, bf16[2,128,256]{2,1,0:T(8,128)(2,1)S(1)}, u32[]{:S(2)}, u32[]{:S(2)}) collective-permute-start(bf16[2,128,256]{2,1,0:T(8,128)(2,1)S(1)} %get-tuple-element.29), channel_id=1, source_target_pairs={{0,64},{8,72},{16,80},{24,88},{32,96},{40,104},{48,112},{56,120},{... | collective-permute-start | bytes 393224 | tf_op jit(solution)/shard_map/ppermute | solution.py:399
  31.0 2.1 %shard_map.84 = (bf16[2,512,128]{2,1,0:T(8,128)(2,1)S(1)}, f32[2,512,128]{2,1,0:T(8,128)S(1)}) custom-call(bf16[256,512]{1,0:T(8,128)(2,1)S(1)} %copy-done.5, bf16[256,512]{1,0:T(8,128)(2,1)S(1)} %collective-permute-done.10.qo_ref, bf16[512,256]{1,0:T(8,128)(2,1)S(1)} %get-tuple-element.31.ks_ref, bf16[8,128,256]{2,1,0:T(8,128)(2,1)S(1)} %get-tuple-element.32.wu_ref, ...), custom_call_target="tpu_custom_call" | custom-call | flops 1000000000 | bytes 1048576 | tf_op jit(solution)/shard_map/pallas_call | solution.py:370
  33.2 3.2 %collective-permute-done.7.r1_ref = bf16[2,128,256]{2,1,0:T(8,128)(2,1)S(1)} collective-permute-done((bf16[2,128,256]{2,1,0:T(8,128)(2,1)S(1)}, bf16[2,128,256]{2,1,0:T(8,128)(2,1)S(1)}, u32[]{:S(2)}, u32[]{:S(2)}) %collective-permute-start.7) | collective-permute-done | bytes 131104 | tf_op jit(solution)/shard_map/ppermute | solution.py:399
  36.4 1.5 %shard_map.85 = (bf16[256,256]{1,0:T(8,128)(2,1)S(1)}, bf16[256,256]{1,0:T(8,128)(2,1)S(1)}) custom-call(bf16[2,128,256]{2,1,0:T(8,128)(2,1)S(1)} %collective-permute-done.7.r1_ref, bf16[2,128,256]{2,1,0:T(8,128)(2,1)S(1)} %collective-permute-done.8.r2_ref, bf16[2,128,256]{2,1,0:T(8,128)(2,1)S(1)} %collective-permute-done.9.r3_ref, ...), custom_call_target="tpu_custom_call" | custom-call | flops 100000000 | bytes 1048576 | tf_op jit(solution)/shard_map/pallas_call | solution.py:370
  38.0 1.3 %collective-permute-done.12.recv_ref = bf16[256,256]{1,0:T(8,128)(2,1)S(1)} collective-permute-done((bf16[256,256]{1,0:T(8,128)(2,1)S(1)}, bf16[256,256]{1,0:T(8,128)(2,1)S(1)}, u32[]{:S(2)}, u32[]{:S(2)}) %collective-permute-start.12) | collective-permute-done | bytes 131104 | tf_op jit(solution)/shard_map/ppermute | solution.py:389
  40.1 2.0 %collective-permute-start.15 = (bf16[32,2048]{1,0:T(8,128)(2,1)S(1)}, bf16[32,2048]{1,0:T(8,128)(2,1)S(1)}, u32[]{:S(2)}, u32[]{:S(2)}) collective-permute-start(bf16[32,2048]{1,0:T(8,128)(2,1)S(1)} %get-tuple-element.44), channel_id=1, source_target_pairs={{0,1},{1,2},{2,3},{3,4},{4,5},{5,6},{6,7},{7,0},{8,9},{9,10},{10,1... | collective-permute-start | bytes 393224 | tf_op jit(solution)/shard_map/ppermute | solution.py:402
  42.1 4.0 %collective-permute-start.17 = (bf16[32,2048]{1,0:T(8,128)(2,1)S(1)}, bf16[32,2048]{1,0:T(8,128)(2,1)S(1)}, u32[]{:S(2)}, u32[]{:S(2)}) collective-permute-start(bf16[32,2048]{1,0:T(8,128)(2,1)S(1)} %get-tuple-element.47), channel_id=1, source_target_pairs={{0,7},{1,0},{2,1},{3,2},{4,3},{5,4},{6,5},{7,6},{8,15},{9,8},{10,9... | collective-permute-start | bytes 393224 | tf_op jit(solution)/shard_map/ppermute | solution.py:402
  46.2 4.1 %collective-permute-start.18 = (bf16[32,1024]{1,0:T(8,128)(2,1)S(1)}, bf16[32,1024]{1,0:T(8,128)(2,1)S(1)}, u32[]{:S(2)}, u32[]{:S(2)}) collective-permute-start(bf16[32,1024]{1,0:T(8,128)(2,1)S(1)} %get-tuple-element.48), channel_id=1, source_target_pairs={{0,6},{1,7},{2,0},{3,1},{4,2},{5,3},{6,4},{7,5},{8,14},{9,15},{10,... | collective-permute-start | bytes 196616 | tf_op jit(solution)/shard_map/ppermute | solution.py:402
  50.3 3.3 %collective-permute-done.16.a4_ref = bf16[32,1024]{1,0:T(8,128)(2,1)S(1)} collective-permute-done((bf16[32,1024]{1,0:T(8,128)(2,1)S(1)}, bf16[32,1024]{1,0:T(8,128)(2,1)S(1)}, u32[]{:S(2)}, u32[]{:S(2)}) %collective-permute-start.16) | collective-permute-done | bytes 65568 | tf_op jit(solution)/shard_map/ppermute | solution.py:402
  53.6 2.1 %collective-permute-start.14 = (bf16[32,2048]{1,0:T(8,128)(2,1)S(1)}, bf16[32,2048]{1,0:T(8,128)(2,1)S(1)}, u32[]{:S(2)}, u32[]{:S(2)}) collective-permute-start(bf16[32,2048]{1,0:T(8,128)(2,1)S(1)} %get-tuple-element.42), channel_id=1, source_target_pairs={{0,7},{1,0},{2,1},{3,2},{4,3},{5,4},{6,5},{7,6},{8,15},{9,8},{10,9... | collective-permute-start | bytes 393224 | tf_op jit(solution)/shard_map/ppermute | solution.py:402
  55.8 2.3 %collective-permute-start.19 = (bf16[32,2048]{1,0:T(8,128)(2,1)S(1)}, bf16[32,2048]{1,0:T(8,128)(2,1)S(1)}, u32[]{:S(2)}, u32[]{:S(2)}) collective-permute-start(bf16[32,2048]{1,0:T(8,128)(2,1)S(1)} %get-tuple-element.49), channel_id=1, source_target_pairs={{0,2},{1,3},{2,4},{3,5},{4,6},{5,7},{6,0},{7,1},{8,10},{9,11},{10,... | collective-permute-start | bytes 393224 | tf_op jit(solution)/shard_map/ppermute | solution.py:402
  58.1 1.9 %collective-permute-start.20 = (bf16[32,2048]{1,0:T(8,128)(2,1)S(1)}, bf16[32,2048]{1,0:T(8,128)(2,1)S(1)}, u32[]{:S(2)}, u32[]{:S(2)}) collective-permute-start(bf16[32,2048]{1,0:T(8,128)(2,1)S(1)} %get-tuple-element.50), channel_id=1, source_target_pairs={{0,6},{1,7},{2,0},{3,1},{4,2},{5,3},{6,4},{7,5},{8,14},{9,15},{10,... | collective-permute-start | bytes 393224 | tf_op jit(solution)/shard_map/ppermute | solution.py:402
  60.0 3.4 %collective-permute-done.19.d_ref = bf16[32,2048]{1,0:T(8,128)(2,1)S(1)} collective-permute-done((bf16[32,2048]{1,0:T(8,128)(2,1)S(1)}, bf16[32,2048]{1,0:T(8,128)(2,1)S(1)}, u32[]{:S(2)}, u32[]{:S(2)}) %collective-permute-start.19) | collective-permute-done | bytes 131104 | tf_op jit(solution)/shard_map/ppermute | solution.py:402
  63.4 1.7 %collective-permute-done.20.e_ref = bf16[32,2048]{1,0:T(8,128)(2,1)S(1)} collective-permute-done((bf16[32,2048]{1,0:T(8,128)(2,1)S(1)}, bf16[32,2048]{1,0:T(8,128)(2,1)S(1)}, u32[]{:S(2)}, u32[]{:S(2)}) %collective-permute-start.20) | collective-permute-done | bytes 131104 | tf_op jit(solution)/shard_map/ppermute | solution.py:402
  (41 shorter events, 6.2 us)
Async XLA Ops:
  0.0 15.0 %copy-start = (bf16[256,512]{1,0:T(8,128)(2,1)S(1)}, bf16[256,512]{1,0:T(8,128)(2,1)}, u32[]{:S(2)}) copy-start(bf16[256,512]{1,0:T(8,128)(2,1)} %gate_ref.1) | copy-start | bytes 786436
  0.0 2.1 %collective-permute-start = (bf16[256,512]{1,0:T(8,128)(2,1)}, bf16[256,512]{1,0:T(8,128)(2,1)S(1)}, u32[]{:S(2)}, u32[]{:S(2)}) collective-permute-start(bf16[256,512]{1,0:T(8,128)(2,1)} %k_ref.1), channel_id=1, source_target_pairs={{0,8},{8,0},{16,24},{24,16},{32,40},{40,32},{48,56},{56,48},{64,72... | collective-permute-start | bytes 786440 | tf_op jit(solution)/shard_map/ppermute | solution.py:389
  0.0 2.1 %collective-permute-start.1 = (bf16[256,512]{1,0:T(8,128)(2,1)}, bf16[256,512]{1,0:T(8,128)(2,1)S(1)}, u32[]{:S(2)}, u32[]{:S(2)}) collective-permute-start(bf16[256,512]{1,0:T(8,128)(2,1)} %v_ref.1), channel_id=1, source_target_pairs={{0,8},{8,0},{16,24},{24,16},{32,40},{40,32},{48,56},{56,48},{64,72... | collective-permute-start | bytes 786440 | tf_op jit(solution)/shard_map/ppermute | solution.py:389
  0.5 1.6 %collective-permute-start.2 = (f32[4,256]{1,0:T(4,128)}, f32[4,256]{1,0:T(4,128)S(1)}, u32[]{:S(2)}, u32[]{:S(2)}) collective-permute-start(f32[4,256]{1,0:T(4,128)} %ld_ref.1), channel_id=1, source_target_pairs={{0,8},{8,0},{16,24},{24,16},{32,40},{40,32},{48,56},{56,48},{64,72... | collective-permute-start | bytes 12296 | tf_op jit(solution)/shard_map/ppermute | solution.py:389
  0.6 1.5 %collective-permute-start.3 = (f32[4,256]{1,0:T(4,128)}, f32[4,256]{1,0:T(4,128)S(1)}, u32[]{:S(2)}, u32[]{:S(2)}) collective-permute-start(f32[4,256]{1,0:T(4,128)} %wr_ref.1), channel_id=1, source_target_pairs={{0,8},{8,0},{16,24},{24,16},{32,40},{40,32},{48,56},{56,48},{64,72... | collective-permute-start | bytes 12296 | tf_op jit(solution)/shard_map/ppermute | solution.py:389
  1.0 30.0 %collective-permute-start.10 = (bf16[256,512]{1,0:T(8,128)(2,1)}, bf16[256,512]{1,0:T(8,128)(2,1)S(1)}, u32[]{:S(2)}, u32[]{:S(2)}) collective-permute-start(bf16[256,512]{1,0:T(8,128)(2,1)} %q_ref.1), channel_id=1, source_target_pairs={{0,8},{8,0},{16,24},{24,16},{32,40},{40,32},{48,56},{56,48},{64,72... | collective-permute-start | bytes 786440 | tf_op jit(solution)/shard_map/ppermute | solution.py:389
  5.4 25.6 %copy-start.5 = (bf16[256,512]{1,0:T(8,128)(2,1)S(1)}, bf16[256,512]{1,0:T(8,128)(2,1)}, u32[]{:S(2)}) copy-start(bf16[256,512]{1,0:T(8,128)(2,1)} %q_ref.1) | copy-start | bytes 786436
  10.3 26.2 %copy-start.1 = (f32[128]{0:T(128)S(1)}, f32[128]{0:T(128)}, u32[]{:S(2)}) copy-start(f32[128]{0:T(128)} %param.14) | copy-start | bytes 1540
  10.3 9.1 %collective-permute-start.6 = (bf16[2,128,256]{2,1,0:T(8,128)(2,1)S(1)}, bf16[2,128,256]{2,1,0:T(8,128)(2,1)S(1)}, u32[]{:S(2)}, u32[]{:S(2)}) collective-permute-start(bf16[2,128,256]{2,1,0:T(8,128)(2,1)S(1)} %get-tuple-element.28.m_ref), channel_id=1, source_target_pairs={{0,48},{8,56},{16,0},{24,8},{32,16},{40,24},{48,32},{56,40},{64,11... | collective-permute-start | bytes 393224 | tf_op jit(solution)/shard_map/ppermute | solution.py:396
  13.4 7.9 %collective-permute-start.5 = (bf16[2,128,256]{2,1,0:T(8,128)(2,1)S(1)}, bf16[2,128,256]{2,1,0:T(8,128)(2,1)S(1)}, u32[]{:S(2)}, u32[]{:S(2)}) collective-permute-start(bf16[2,128,256]{2,1,0:T(8,128)(2,1)S(1)} %get-tuple-element.28.m_ref), channel_id=1, source_target_pairs={{0,32},{8,40},{16,48},{24,56},{32,0},{40,8},{48,16},{56,24},{64,96... | collective-permute-start | bytes 393224 | tf_op jit(solution)/shard_map/ppermute | solution.py:396
  14.0 9.1 %collective-permute-start.4 = (bf16[2,128,256]{2,1,0:T(8,128)(2,1)S(1)}, bf16[2,128,256]{2,1,0:T(8,128)(2,1)S(1)}, u32[]{:S(2)}, u32[]{:S(2)}) collective-permute-start(bf16[2,128,256]{2,1,0:T(8,128)(2,1)S(1)} %get-tuple-element.28.m_ref), channel_id=1, source_target_pairs={{0,16},{8,24},{16,32},{24,40},{32,48},{40,56},{48,0},{56,8},{64,80... | collective-permute-start | bytes 393224 | tf_op jit(solution)/shard_map/ppermute | solution.py:396
  15.0 18.2 %collective-permute-start.11 = (bf16[256,512]{1,0:T(8,128)(2,1)S(1)}, bf16[256,512]{1,0:T(8,128)(2,1)S(1)}, u32[]{:S(2)}, u32[]{:S(2)}) collective-permute-start(bf16[256,512]{1,0:T(8,128)(2,1)S(1)} %copy-done), channel_id=1, source_target_pairs={{0,8},{8,0},{16,24},{24,16},{32,40},{40,32},{48,56},{56,48},{64,72... | collective-permute-start | bytes 786440 | tf_op jit(solution)/shard_map/ppermute | solution.py:389
  23.7 9.5 %collective-permute-start.9 = (bf16[2,128,256]{2,1,0:T(8,128)(2,1)S(1)}, bf16[2,128,256]{2,1,0:T(8,128)(2,1)S(1)}, u32[]{:S(2)}, u32[]{:S(2)}) collective-permute-start(bf16[2,128,256]{2,1,0:T(8,128)(2,1)S(1)} %get-tuple-element.29), channel_id=1, source_target_pairs={{0,192},{8,200},{16,208},{24,216},{32,224},{40,232},{48,240},{56,2... | collective-permute-start | bytes 393224 | tf_op jit(solution)/shard_map/ppermute | solution.py:399
  24.4 8.8 %collective-permute-start.8 = (bf16[2,128,256]{2,1,0:T(8,128)(2,1)S(1)}, bf16[2,128,256]{2,1,0:T(8,128)(2,1)S(1)}, u32[]{:S(2)}, u32[]{:S(2)}) collective-permute-start(bf16[2,128,256]{2,1,0:T(8,128)(2,1)S(1)} %get-tuple-element.29), channel_id=1, source_target_pairs={{0,128},{8,136},{16,144},{24,152},{32,160},{40,168},{48,176},{56,1... | collective-permute-start | bytes 393224 | tf_op jit(solution)/shard_map/ppermute | solution.py:399
  29.1 7.3 %collective-permute-start.7 = (bf16[2,128,256]{2,1,0:T(8,128)(2,1)S(1)}, bf16[2,128,256]{2,1,0:T(8,128)(2,1)S(1)}, u32[]{:S(2)}, u32[]{:S(2)}) collective-permute-start(bf16[2,128,256]{2,1,0:T(8,128)(2,1)S(1)} %get-tuple-element.29), channel_id=1, source_target_pairs={{0,64},{8,72},{16,80},{24,88},{32,96},{40,104},{48,112},{56,120},{... | collective-permute-start | bytes 393224 | tf_op jit(solution)/shard_map/ppermute | solution.py:399
  37.9 1.4 %collective-permute-start.12 = (bf16[256,256]{1,0:T(8,128)(2,1)S(1)}, bf16[256,256]{1,0:T(8,128)(2,1)S(1)}, u32[]{:S(2)}, u32[]{:S(2)}) collective-permute-start(bf16[256,256]{1,0:T(8,128)(2,1)S(1)} %get-tuple-element.39), channel_id=1, source_target_pairs={{0,8},{8,0},{16,24},{24,16},{32,40},{40,32},{48,56},{56,48},{64,72... | collective-permute-start | bytes 393224 | tf_op jit(solution)/shard_map/ppermute | solution.py:389
  40.1 15.6 %collective-permute-start.15 = (bf16[32,2048]{1,0:T(8,128)(2,1)S(1)}, bf16[32,2048]{1,0:T(8,128)(2,1)S(1)}, u32[]{:S(2)}, u32[]{:S(2)}) collective-permute-start(bf16[32,2048]{1,0:T(8,128)(2,1)S(1)} %get-tuple-element.44), channel_id=1, source_target_pairs={{0,1},{1,2},{2,3},{3,4},{4,5},{5,6},{6,7},{7,0},{8,9},{9,10},{10,1... | collective-permute-start | bytes 393224 | tf_op jit(solution)/shard_map/ppermute | solution.py:402
  42.1 13.6 %collective-permute-start.17 = (bf16[32,2048]{1,0:T(8,128)(2,1)S(1)}, bf16[32,2048]{1,0:T(8,128)(2,1)S(1)}, u32[]{:S(2)}, u32[]{:S(2)}) collective-permute-start(bf16[32,2048]{1,0:T(8,128)(2,1)S(1)} %get-tuple-element.47), channel_id=1, source_target_pairs={{0,7},{1,0},{2,1},{3,2},{4,3},{5,4},{6,5},{7,6},{8,15},{9,8},{10,9... | collective-permute-start | bytes 393224 | tf_op jit(solution)/shard_map/ppermute | solution.py:402
  46.2 7.4 %collective-permute-start.16 = (bf16[32,1024]{1,0:T(8,128)(2,1)S(1)}, bf16[32,1024]{1,0:T(8,128)(2,1)S(1)}, u32[]{:S(2)}, u32[]{:S(2)}) collective-permute-start(bf16[32,1024]{1,0:T(8,128)(2,1)S(1)} %get-tuple-element.45), channel_id=1, source_target_pairs={{0,2},{1,3},{2,4},{3,5},{4,6},{5,7},{6,0},{7,1},{8,10},{9,11},{10,... | collective-permute-start | bytes 196616 | tf_op jit(solution)/shard_map/ppermute | solution.py:402
  46.2 9.5 %collective-permute-start.18 = (bf16[32,1024]{1,0:T(8,128)(2,1)S(1)}, bf16[32,1024]{1,0:T(8,128)(2,1)S(1)}, u32[]{:S(2)}, u32[]{:S(2)}) collective-permute-start(bf16[32,1024]{1,0:T(8,128)(2,1)S(1)} %get-tuple-element.48), channel_id=1, source_target_pairs={{0,6},{1,7},{2,0},{3,1},{4,2},{5,3},{6,4},{7,5},{8,14},{9,15},{10,... | collective-permute-start | bytes 196616 | tf_op jit(solution)/shard_map/ppermute | solution.py:402
  50.3 9.7 %collective-permute-start.13 = (bf16[32,2048]{1,0:T(8,128)(2,1)S(1)}, bf16[32,2048]{1,0:T(8,128)(2,1)S(1)}, u32[]{:S(2)}, u32[]{:S(2)}) collective-permute-start(bf16[32,2048]{1,0:T(8,128)(2,1)S(1)} %get-tuple-element.41), channel_id=1, source_target_pairs={{0,1},{1,2},{2,3},{3,4},{4,5},{5,6},{6,7},{7,0},{8,9},{9,10},{10,1... | collective-permute-start | bytes 393224 | tf_op jit(solution)/shard_map/ppermute | solution.py:402
  53.6 6.4 %collective-permute-start.14 = (bf16[32,2048]{1,0:T(8,128)(2,1)S(1)}, bf16[32,2048]{1,0:T(8,128)(2,1)S(1)}, u32[]{:S(2)}, u32[]{:S(2)}) collective-permute-start(bf16[32,2048]{1,0:T(8,128)(2,1)S(1)} %get-tuple-element.42), channel_id=1, source_target_pairs={{0,7},{1,0},{2,1},{3,2},{4,3},{5,4},{6,5},{7,6},{8,15},{9,8},{10,9... | collective-permute-start | bytes 393224 | tf_op jit(solution)/shard_map/ppermute | solution.py:402
  55.8 7.6 %collective-permute-start.19 = (bf16[32,2048]{1,0:T(8,128)(2,1)S(1)}, bf16[32,2048]{1,0:T(8,128)(2,1)S(1)}, u32[]{:S(2)}, u32[]{:S(2)}) collective-permute-start(bf16[32,2048]{1,0:T(8,128)(2,1)S(1)} %get-tuple-element.49), channel_id=1, source_target_pairs={{0,2},{1,3},{2,4},{3,5},{4,6},{5,7},{6,0},{7,1},{8,10},{9,11},{10,... | collective-permute-start | bytes 393224 | tf_op jit(solution)/shard_map/ppermute | solution.py:402
  58.1 7.0 %collective-permute-start.20 = (bf16[32,2048]{1,0:T(8,128)(2,1)S(1)}, bf16[32,2048]{1,0:T(8,128)(2,1)S(1)}, u32[]{:S(2)}, u32[]{:S(2)}) collective-permute-start(bf16[32,2048]{1,0:T(8,128)(2,1)S(1)} %get-tuple-element.50), channel_id=1, source_target_pairs={{0,6},{1,7},{2,0},{3,1},{4,2},{5,3},{6,4},{7,5},{8,14},{9,15},{10,... | collective-permute-start | bytes 393224 | tf_op jit(solution)/shard_map/ppermute | solution.py:402
  (5 other events, 11.6 us)

commit v2 on v1

v2 whole, which is shorter than its diff:
```python
import jax
import jax.numpy as jnp
from jax import lax
from jax.experimental import pallas as pl
from jax.experimental.pallas import tpu as pltpu
from jax.sharding import PartitionSpec as P

F32 = jnp.float32
BF16 = jnp.bfloat16
EPS = 1e-6
HD = 128
C = 128
HEADS = 4
OWN = 2
NC = 2
NP = HEADS * NC
SUB = 16
TP = 8


def dot(a, b):
    return lax.dot_general(a, b, (((1,), (0,)), ((), ())), preferred_element_type=F32)


def dot_nt(a, b):
    return lax.dot_general(a, b, (((1,), (1,)), ((), ())), preferred_element_type=F32)


def dot_tn(a, b):
    return lax.dot_general(a, b, (((0,), (0,)), ((), ())), preferred_element_type=F32)


def split(a):
    hi = a.astype(BF16)
    lo = (a - hi.astype(F32)).astype(BF16)
    return hi, lo


def lanes(*parts):
    return jnp.concatenate(parts, axis=1)


def rows(*parts):
    return jnp.concatenate(parts, axis=0)


def dot_sq(a, b):
    ah, al = split(a)
    bh, bl = split(b)
    out = dot(lanes(ah, al), rows(lanes(bh, bl), lanes(bh, jnp.zeros_like(bl))))
    return out[:, :C] + out[:, C:]


def dot_wide(a, b):
    ah, al = split(a)
    bh, bl = split(b)
    return dot(lanes(ah, al), rows(bh, bh)) + dot(ah, bl)


def dot_exact_left(a, b):
    bh, bl = split(b)
    out = dot(a, lanes(bh, bl))
    return out[:, :HD] + out[:, HD:]


def follow(later, earlier):
    out = dot_wide(later[:, :HD], earlier)
    return lanes(out[:, :HD], out[:, HD:] + later[:, HD:])


def iota2(shape, dim):
    return lax.broadcasted_iota(jnp.int32, shape, dim)


def core_index():
    return lax.rem(lax.axis_index("ctx"), 2)


def part(ref, p):
    n, h = divmod(p, HEADS)
    return ref[n * C : n * C + C, h * HD : h * HD + HD]


def maps_kernel(
    k_hbm, v_hbm, ld_hbm, wr_hbm,
    wu_ref, vec_ref, vect_ref, first_ref, keep_ref, send_ref,
    k_ref, v_ref, ld_ref, wr_ref, xs, ts, sems,
):
    copies = [
        pltpu.make_async_copy(src, dst, sems.at[i])
        for i, (src, dst) in enumerate(
            ((ld_hbm, ld_ref), (wr_hbm, wr_ref), (k_hbm, k_ref), (v_hbm, v_ref))
        )
    ]
    for copy in copies:
        copy.start()
    core = core_index()
    row = iota2((C, C), 0)
    col = iota2((C, C), 1)
    eye = row == col
    strict = row > col
    upper = (row <= col).astype(BF16)
    base = row - SUB * lax.div(col, SUB)
    select = lanes(*[(base == j).astype(BF16) for j in range(SUB)])
    for copy in copies[:3]:
        copy.wait()
    steps = rows(ld_ref[:, :C], ld_ref[:, C:])
    beta = rows(wr_ref[:, :C], wr_ref[:, C:])
    s0 = steps.astype(BF16)
    r1 = steps - s0.astype(F32)
    s1 = r1.astype(BF16)
    s2 = (r1 - s1.astype(F32)).astype(BF16)
    g = dot(s0, upper) + (dot(s1, upper) + dot(s2, upper))
    gram = []
    norms = []
    for p in range(NP):
        kp = part(k_ref, p)
        kk = dot_nt(kp, kp)
        gram.append(kk)
        norms.append(jnp.sum(jnp.where(eye, kk, 0.0), axis=0, keepdims=True))
    rn = 1.0 / jnp.sqrt(rows(*norms) + EPS)
    eg = jnp.exp(g)
    gend = g[:, C - 1 : C]
    tail = jnp.exp(gend - g) * rn
    vec = rows(g, beta * rn, tail, rn, eg, beta * eg * rn, beta, beta)
    vec_ref[...] = vec
    vect = rows(vec, vec).T
    vect_ref[...] = vect[:, : NP * 8]

    def column(kind, p):
        i = kind * NP + p
        return vect[:, i : i + 1]

    lower = []
    for p in range(NP):
        spread = column(0, p) - g[p : p + 1, :]
        w = jnp.exp(jnp.where(strict, spread, 0.0))
        w = w * (column(1, p) * rn[p : p + 1, :]) * gram[p]
        lower.append(jnp.where(strict, w, 0.0))
    lane_block = lax.div(iota2((SUB, C), 1), SUB)
    for p in range(NP):
        acc = jnp.zeros((SUB, C), F32)
        for b in range(C // SUB):
            acc = acc + jnp.where(lane_block == b, lower[p][b * SUB : b * SUB + SUB, :], 0.0)
        xs[pl.ds(p, SUB, stride=NP), :] = acc
    xh, xl = split(xs[...])
    coef = dot(lanes(xh, xl), rows(select, select))
    lane_in = lax.rem(iota2((NP, C), 1), SUB)
    solved = []
    for i in range(SUB):
        acc = (lane_in == i).astype(F32)
        for j in range(i):
            acc = acc - coef[i * NP : i * NP + NP, j * C : j * C + C] * solved[j]
        solved.append(acc)
        ts[i * NP : i * NP + NP, :] = acc
    inverse = []
    for p in range(NP):
        tp = ts[pl.ds(p, SUB, stride=NP), :]
        inverse.append(rows(*[jnp.where(lane_block == b, tp, 0.0) for b in range(C // SUB)]))
    size = SUB
    while size < C:
        rb = lax.div(row, size)
        cb = lax.div(col, size)
        mask = (rb == cb + 1) & (lax.rem(rb, 2) == 1)
        mids = [dot_sq(jnp.where(mask, lower[p], 0.0), inverse[p]) for p in range(NP)]
        inverse = [inverse[p] - dot_sq(inverse[p], mids[p]) for p in range(NP)]
        size *= 2
    copies[3].wait()
    maps = []
    for p in range(NP):
        kp = part(k_ref, p)
        vp = part(v_ref, p)
        eh, el = split(inverse[p] * vec[5 * NP + p : 5 * NP + p + 1, :])
        uh, ul = split(inverse[p] * beta[p : p + 1, :])
        erase = dot(lanes(eh, el), rows(kp, kp))
        write = dot(lanes(uh, ul), rows(vp, vp))
        both = lanes(erase, write)
        wu_ref[p] = both.astype(BF16)
        wh, wl = split(both * column(2, p))
        out = dot_tn(rows(kp, kp), rows(wh, wl))
        decay = jnp.where(eye, jnp.exp(gend[p : p + 1, :]), 0.0)
        maps.append(lanes(decay - out[:, :HD], out[:, HD:]))
    whole = []
    for h in range(HEADS):
        first_ref[h] = maps[h]
        whole.append(follow(maps[HEADS + h], maps[h]))
    for h in range(OWN):
        keep_ref[h] = jnp.where(core == 0, whole[h], whole[OWN + h])
        send_ref[h] = jnp.where(core == 0, whole[OWN + h], whole[h]).astype(BF16)


def pair_kernel(keep_ref, recv_ref, total_ref, early_ref):
    core = core_index()
    for h in range(OWN):
        mine = keep_ref[h]
        other = recv_ref[h].astype(F32)
        early = jnp.where(core == 0, mine, other)
        late = jnp.where(core == 0, other, mine)
        early_ref[h] = early
        total_ref[h] = follow(late, early).astype(BF16)


def reads_kernel(q_ref, k_ref, wu_ref, vec_ref, vect_ref, first_ref, qeff_ref, local_ref):
    row = iota2((C, C), 0)
    col = iota2((C, C), 1)
    incl = row >= col
    scale = HD**-0.5
    vec = vec_ref[...]
    vect = vect_ref[...]

    def column(kind, p):
        i = kind * NP + p
        return vect[:, i : i + 1]

    for p in range(NP):
        n, h = divmod(p, HEADS)
        qp = part(q_ref, p)
        qf = qp.astype(F32)
        rq = scale / jnp.sqrt(jnp.sum(qf * qf, axis=1, keepdims=True) + EPS)
        w = jnp.exp(jnp.where(incl, column(0, p) - vec[p : p + 1, :], 0.0))
        scores = w * (rq * vec[3 * NP + p : 3 * NP + p + 1, :]) * dot_nt(qp, part(k_ref, p))
        sh, sl = split(jnp.where(incl, scores, 0.0))
        wu = wu_ref[p]
        out = dot(lanes(sh, sl), rows(wu, wu))
        qeff = (column(4, p) * rq) * qf - out[:, :HD]
        local = out[:, HD:]
        if n > 0:
            out = dot_wide(qeff, first_ref[h])
            qeff = out[:, :HD]
            local = local + out[:, HD:]
        qeff_ref[h, n * C : n * C + C, :] = qeff.astype(BF16)
        local_ref[h, n * C : n * C + C, :] = local


def y_index():
    return lax.rem(lax.div(lax.axis_index("ctx"), 2), 4)


def x_index():
    return lax.div(lax.axis_index("ctx"), 8)


def follow_sent(later, earlier):
    out = dot(later[:, :HD], earlier)
    return lanes(out[:, :HD], out[:, HD:] + later[:, HD:].astype(F32))


def two_kernel(m_ref, recv_ref, after, two_ref):
    del after
    odd = lax.rem(y_index(), 2) == 1
    for h in range(OWN):
        mine, other = m_ref[h], recv_ref[h]
        early = jnp.where(odd, other, mine)
        late = jnp.where(odd, mine, other)
        two_ref[h] = follow_sent(late, early).astype(BF16)


def row_kernel(recv_ref, two_ref, recv_two_ref, total_ref, prefix_ref):
    y = y_index()
    eye = (iota2((HD, 2 * HD), 0) == iota2((HD, 2 * HD), 1)).astype(F32)
    for h in range(OWN):
        mine, other = two_ref[h], recv_two_ref[h]
        early = jnp.where(y >= 2, other, mine)
        late = jnp.where(y >= 2, mine, other)
        total_ref[h] = follow_sent(late, early).astype(BF16)
        before = recv_ref[h]
        prefix_ref[h] = jnp.where(
            y == 0,
            eye,
            jnp.where(
                y == 1,
                before.astype(F32),
                jnp.where(y == 2, early.astype(F32), follow_sent(before, early)),
            ),
        )


def half_kernel(m_ref, recv_ref, add_ref):
    odd = lax.rem(x_index(), 2) == 1
    for h in range(OWN):
        mine, other = m_ref[h], recv_ref[h]
        early = jnp.where(odd, other, mine)
        late = jnp.where(odd, mine, other)
        out = dot(late[:, :HD], early[:, HD:]) + late[:, HD:].astype(F32)
        add_ref[h] = out.astype(BF16)


def state_kernel(recv_ref, half_ref, prefix_ref, early_ref, keep_ref, send_ref):
    core = core_index()
    x = x_index()
    for h in range(OWN):
        m = recv_ref[h]
        half = half_ref[h]
        through = dot(m[:, :HD], half)
        state = jnp.where(x >= 2, half.astype(F32), 0.0)
        state = jnp.where(x == 3, through, state)
        state = state + jnp.where(lax.rem(x, 2) == 1, m[:, HD:].astype(F32), 0.0)
        for_cores = []
        for ref in (prefix_ref, early_ref):
            m = ref[h]
            state = dot_sq(m[:, :HD], state) + m[:, HD:]
            for_cores.append(state)
        hi, lo = split(jnp.where(core == 0, for_cores[0], for_cores[1]))
        keep_ref[h] = lanes(hi, lo)
        send_ref[h] = jnp.where(core == 0, for_cores[1], for_cores[0]).astype(BF16)


def gated_rows(state, head, qeff_ref, local_ref, gate_ref, gain):
    out = dot(qeff_ref[head], state)
    core_rows = local_ref[head] + out[:, :HD]
    if state.shape[1] > HD:
        core_rows = core_rows + out[:, HD:]
    mean = jnp.mean(core_rows * core_rows, axis=1, keepdims=True)
    gate = gate_ref[:, pl.ds(pl.multiple_of(head * HD, HD), HD)].astype(F32)
    silu = gate / (1.0 + jnp.exp(-gate))
    return (core_rows / jnp.sqrt(mean + EPS) * gain * silu).astype(BF16)


def gather_rows(state_ref, first, qeff_ref, local_ref, gate_ref, gain_ref, gs, lhs):
    for h in range(OWN):
        gs[:, h * HD : h * HD + HD] = gated_rows(
            state_ref[h], first + h, qeff_ref, local_ref, gate_ref, gain_ref[...]
        )
    me = lax.axis_index("tp")
    chunk = gs.shape[0] // TP
    for d in range(TP):
        start = pl.multiple_of(lax.rem(me + d, TP) * chunk, chunk)
        lhs[d * chunk : d * chunk + chunk, :] = gs[pl.ds(start, chunk), :]


def weight_rows(w_ref, first, s):
    return w_ref[pl.ds(pl.multiple_of(first * HD, OWN * HD), OWN * HD), s]


STEP = 512


def own_kernel(state_ref, qeff_ref, local_ref, gate_ref, gain_ref, w_ref, acc_ref, gs, lhs):
    first = OWN * core_index()
    gather_rows(state_ref, first, qeff_ref, local_ref, gate_ref, gain_ref, gs, lhs)
    for j in range(w_ref.shape[1] // STEP):
        s = slice(j * STEP, j * STEP + STEP)
        acc_ref[:, s] = dot(lhs[...], weight_rows(w_ref, first, s))


def other_kernel(
    state_ref, acc_ref, qeff_ref, local_ref, gate_ref, gain_ref, w_ref, *refs
):
    outs, (gs, lhs) = refs[:-2], refs[-2:]
    first = OWN * (1 - core_index())
    gather_rows(state_ref, first, qeff_ref, local_ref, gate_ref, gain_ref, gs, lhs)
    chunk = gs.shape[0] // TP
    for j in range(w_ref.shape[1] // STEP):
        s = slice(j * STEP, j * STEP + STEP)
        out = (acc_ref[:, s] + dot(lhs[...], weight_rows(w_ref, first, s))).astype(BF16)
        for d, ref in zip((0, 1, 2, 3, 5, 6, 7), outs):
            ref[:, s] = out[d * chunk : d * chunk + chunk]
        ref = outs[7 + j // 2]
        t = slice(j % 2 * STEP, j % 2 * STEP + STEP)
        ref[:, t] = out[4 * chunk : 5 * chunk]


def partial_kernel(a_ref, a3_ref, a4_ref, b_ref, b3_ref, b4_ref, ao_ref, bo_ref):
    half = a4_ref.shape[1]
    a = a_ref[...].astype(F32) + a3_ref[...].astype(F32)
    b = b_ref[...].astype(F32) + b3_ref[...].astype(F32)
    ao_ref[:, :half] = (a[:, :half] + a4_ref[...].astype(F32)).astype(BF16)
    ao_ref[:, half:] = a[:, half:].astype(BF16)
    bo_ref[:, :half] = b[:, :half].astype(BF16)
    bo_ref[:, half:] = (b[:, half:] + b4_ref[...].astype(F32)).astype(BF16)


def sum_kernel(*refs):
    total = refs[0][...].astype(F32)
    for ref in refs[1:-1]:
        total = total + ref[...].astype(F32)
    refs[-1][...] = total.astype(BF16)


def call(kernel, outs, args, scratch=(), hbm=(), flops=10**8, moved=2**20, vmem_mib=32):
    vmem = pl.BlockSpec(memory_space=pltpu.VMEM)
    stay = pl.BlockSpec(memory_space=pltpu.HBM)
    loose = pl.BlockSpec(memory_space=pl.ANY)
    specs = [{"hbm": stay, "any": loose}.get(dict(hbm).get(i), vmem) for i in range(len(args))]
    return pl.pallas_call(
        kernel,
        out_shape=[jax.ShapeDtypeStruct(s, t) for s, t in outs],
        in_specs=specs,
        out_specs=[vmem] * len(outs),
        scratch_shapes=list(scratch),
        compiler_params=pltpu.CompilerParams(vmem_limit_bytes=vmem_mib * 2**20),
        cost_estimate=pl.CostEstimate(flops=flops, bytes_accessed=moved, transcendentals=0),
    )(*args)


def on_device(q, k, v, ld, wr, gate, gain, w):
    tokens = q.shape[0]
    n_ctx = lax.axis_size("ctx")

    def swap(a):
        return lax.ppermute(a, "ctx", [(i, i ^ 1) for i in range(n_ctx)])

    def across_y(a, m):
        pairs = [(i, (i // 8 * 4 + (i // 2 % 4 ^ m)) * 2 + i % 2) for i in range(n_ctx)]
        return lax.ppermute(a, "ctx", pairs)

    def across_x(a, m):
        return lax.ppermute(a, "ctx", [(i, (i // 8 ^ m) * 8 + i % 8) for i in range(n_ctx)])

    def along_z(a, d):
        return lax.ppermute(a, "tp", [(i, (i + d) % TP) for i in range(TP)])

    pair = (OWN, HD, 2 * HD)
    wu, vec, vect, first, keep, send = call(
        maps_kernel,
        [
            ((NP, C, 2 * HD), BF16),
            ((8 * NP, C), F32),
            ((C, 8 * NP), F32),
            ((HEADS, HD, 2 * HD), F32),
            (pair, F32),
            (pair, BF16),
        ],
        tuple(pltpu.with_memory_space_constraint(a, pltpu.HBM) for a in (k, v, ld, wr)),
        [
            pltpu.VMEM(k.shape, BF16),
            pltpu.VMEM(v.shape, BF16),
            pltpu.VMEM(ld.shape, F32),
            pltpu.VMEM(wr.shape, F32),
            pltpu.VMEM((SUB * NP, C), F32),
            pltpu.VMEM((SUB * NP, C), F32),
            pltpu.SemaphoreType.DMA((4,)),
        ],
        hbm={0: "hbm", 1: "hbm", 2: "hbm", 3: "hbm"},
        flops=10**9,
        vmem_mib=32,
    )
    total, early = call(pair_kernel, [(pair, BF16), (pair, F32)], (keep, swap(send)))
    beside = across_y(total, 1)
    qeff, local = call(
        reads_kernel,
        [((HEADS, tokens, HD), BF16), ((HEADS, tokens, HD), F32)],
        (q, k, wu, vec, vect, first),
        flops=10**9,
    )
    (two,) = call(two_kernel, [(pair, BF16)], (total, beside, local), hbm={2: "any"})
    row_total, prefix = call(
        row_kernel, [(pair, BF16), (pair, F32)], (beside, two, across_y(two, 3))
    )
    beside_row = across_x(row_total, 1)
    (half,) = call(half_kernel, [((OWN, HD, HD), BF16)], (row_total, beside_row))
    own_state, send_state = call(
        state_kernel,
        [(pair, BF16), ((OWN, HD, HD), BF16)],
        (beside_row, across_x(half, 3), prefix, early),
    )
    other_state = swap(send_state)
    gain = gain.reshape(1, HD)
    rows_scratch = [pltpu.VMEM((tokens, OWN * HD), BF16)] * 2
    width = w.shape[1]
    (acc,) = call(
        own_kernel,
        [((tokens, width), F32)],
        (own_state, qeff, local, gate, gain, w),
        rows_scratch,
        flops=10**9,
    )
    rows_here = tokens // TP
    block = ((rows_here, width), BF16)
    p0, p1, p2, p3, p5, p6, p7, p4a, p4b = call(
        other_kernel,
        [block] * 7 + [((rows_here, width // 2), BF16)] * 2,
        (other_state, acc, qeff, local, gate, gain, w),
        rows_scratch,
        flops=10**9,
    )
    a3, b3 = along_z(p3, 1), along_z(p5, -1)
    a4, b4 = along_z(p4a, 2), along_z(p4b, -2)
    a1, b1 = along_z(p1, 1), along_z(p7, -1)
    pa, pb = call(partial_kernel, [block] * 2, (p2, a3, a4, p6, b3, b4))
    a2, b2 = along_z(pa, 2), along_z(pb, -2)
    return call(sum_kernel, [block], (p0, a1, b1, a2, b2))[0]


def solution(mesh):
    in_specs = (
        P("ctx", "tp"),
        P("ctx", "tp"),
        P("ctx", "tp"),
        P("tp", "ctx"),
        P("tp", "ctx"),
        P("ctx", "tp"),
        P(),
        P("tp", None),
    )
    return jax.shard_map(
        on_device, mesh=mesh, in_specs=in_specs, out_specs=P(("ctx", "tp"), None), check_vma=False
    )
```

time: 66.1 us -> 59.1 us (0.89)
  the two profiles are of different devices: /device:TPU:2 before, /device:TPU:24 now
where the time goes in v2:
time: 59.1 us; the launch traced here: 59 us
  waiting for transfers between devices  24 us (41%)
  starting transfers between devices  23.9 us (40%)
  Pallas kernels  10.9 us (18%)
    ppermute x8, starting transfers between devices, along_z(): return lax.ppermute(a, 'tp', [(i, (i + d) % TP) for i in range(TP)])  16.5 us
    pallas_call x11, Pallas kernels, call(): pl.pallas_call(kernel, out_shape=[jax.ShapeDtypeStruct(s, t) for s, t in...  10.9 us
    ppermute x8, waiting for transfers between devices, along_z(): return lax.ppermute(a, 'tp', [(i, (i + d) % TP) for i in range(TP)])  8.38 us
    ppermute x2, waiting for transfers between devices, across_y(): return lax.ppermute(a, 'ctx', pairs)  7.68 us
    ppermute x2, waiting for transfers between devices, across_x(): lax.ppermute(a, 'ctx', [(i, (i // 8 ^ m) * 8 + i % 8) for i in range(n_ct...  6.19 us
    ppermute x2, starting transfers between devices, across_x(): lax.ppermute(a, 'ctx', [(i, (i // 8 ^ m) * 8 + i % 8) for i in range(n_ct...  4.42 us
    ppermute x2, starting transfers between devices, across_y(): return lax.ppermute(a, 'ctx', pairs)  2.87 us
    ppermute x2, waiting for transfers between devices, swap(): return lax.ppermute(a, 'ctx', [(i, i ^ 1) for i in range(n_ctx)])  1.75 us
  transfers between devices with their start and end apart: 14, of which 9 were waited for; matrix products, arithmetic and copies ran while one was open for 0% of the time, Pallas kernels for 4%

profile of v2, /device:TPU:24, one launch (start us, length us, event | category | flops | bytes accessed | tf_op | source)
XLA Modules:
  0.0 59.0 jit_solution(4833478724328303144)
XLA Ops:
  0.0 5.6 %shard_map.82 = (bf16[8,128,256]{2,1,0:T(8,128)(2,1)S(1)}, f32[64,128]{1,0:T(8,128)S(1)}, f32[128,64]{1,0:T(8,128)S(1)}, f32[4,128,256]{2,1,0:T(8,128)S(1)}, f32...) custom-call(bf16[256,512]{1,0:T(8,128)(2,1)} %k_ref.1, bf16[256,512]{1,0:T(8,128)(2,1)} %v_hbm.1, ...), custom_call_target="tpu_custom_call" | custom-call | flops 1000000000 | bytes 1048576 | tf_op jit(solution)/shard_map/pallas_call | solution.py:385
  5.7 1.3 %collective-permute-done.recv_ref = bf16[2,128,256]{2,1,0:T(8,128)(2,1)S(1)} collective-permute-done((bf16[2,128,256]{2,1,0:T(8,128)(2,1)S(1)}, bf16[2,128,256]{2,1,0:T(8,128)(2,1)S(1)}, u32[]{:S(2)}, u32[]{:S(2)}) %collective-permute-start) | collective-permute-done | bytes 131104 | tf_op jit(solution)/shard_map/ppermute | solution.py:401
  7.3 0.8 %collective-permute-start.1 = (bf16[2,128,256]{2,1,0:T(8,128)(2,1)S(1)}, bf16[2,128,256]{2,1,0:T(8,128)(2,1)S(1)}, u32[]{:S(2)}, u32[]{:S(2)}) collective-permute-start(bf16[2,128,256]{2,1,0:T(8,128)(2,1)S(1)} %get-tuple-element.32.m_ref), channel_id=1, source_target_pairs={{0,16},{8,24},{16,0},{24,8},{32,48},{40,56},{48,32},{56,40},{64,80... | collective-permute-start | bytes 393224 | tf_op jit(solution)/shard_map/ppermute | solution.py:405
  8.2 1.3 %shard_map.84 = (bf16[4,256,128]{2,1,0:T(8,128)(2,1)S(1)}, f32[4,256,128]{2,1,0:T(8,128)S(1)}) custom-call(bf16[256,512]{1,0:T(8,128)(2,1)S(1)} %copy-done.4, bf16[256,512]{1,0:T(8,128)(2,1)S(1)} %copy-done.3, bf16[8,128,256]{2,1,0:T(8,128)(2,1)S(1)} %get-tuple-element.33.wu_ref, f32[64,128]{1,0:T(8,128)S(1)} %get-tuple-element.34.vec_ref, ...), custom_call_target="tpu_custom_call" | custom-call | flops 1000000000 | bytes 1048576 | tf_op jit(solution)/shard_map/pallas_call | solution.py:385
  9.5 3.5 %collective-permute-done.1.recv_ref = bf16[2,128,256]{2,1,0:T(8,128)(2,1)S(1)} collective-permute-done((bf16[2,128,256]{2,1,0:T(8,128)(2,1)S(1)}, bf16[2,128,256]{2,1,0:T(8,128)(2,1)S(1)}, u32[]{:S(2)}, u32[]{:S(2)}) %collective-permute-start.1) | collective-permute-done | bytes 131104 | tf_op jit(solution)/shard_map/ppermute | solution.py:405
  13.2 2.0 %collective-permute-start.2 = (bf16[2,128,256]{2,1,0:T(8,128)(2,1)S(1)}, bf16[2,128,256]{2,1,0:T(8,128)(2,1)S(1)}, u32[]{:S(2)}, u32[]{:S(2)}) collective-permute-start(bf16[2,128,256]{2,1,0:T(8,128)(2,1)S(1)} %shard_map.85.two_ref), channel_id=1, source_target_pairs={{0,48},{8,56},{16,32},{24,40},{32,16},{40,24},{48,0},{56,8},{64,11... | collective-permute-start | bytes 393224 | tf_op jit(solution)/shard_map/ppermute | solution.py:405
  15.2 4.2 %collective-permute-done.2.recv_two_ref = bf16[2,128,256]{2,1,0:T(8,128)(2,1)S(1)} collective-permute-done((bf16[2,128,256]{2,1,0:T(8,128)(2,1)S(1)}, bf16[2,128,256]{2,1,0:T(8,128)(2,1)S(1)}, u32[]{:S(2)}, u32[]{:S(2)}) %collective-permute-start.2) | collective-permute-done | bytes 131104 | tf_op jit(solution)/shard_map/ppermute | solution.py:405
  19.7 1.6 %collective-permute-start.3 = (bf16[2,128,256]{2,1,0:T(8,128)(2,1)S(1)}, bf16[2,128,256]{2,1,0:T(8,128)(2,1)S(1)}, u32[]{:S(2)}, u32[]{:S(2)}) collective-permute-start(bf16[2,128,256]{2,1,0:T(8,128)(2,1)S(1)} %get-tuple-element.38.m_ref), channel_id=1, source_target_pairs={{0,64},{8,72},{16,80},{24,88},{32,96},{40,104},{48,112},{56,120},{... | collective-permute-start | bytes 393224 | tf_op jit(solution)/shard_map/ppermute | solution.py:408
  21.2 3.5 %collective-permute-done.3.recv_ref = bf16[2,128,256]{2,1,0:T(8,128)(2,1)S(1)} collective-permute-done((bf16[2,128,256]{2,1,0:T(8,128)(2,1)S(1)}, bf16[2,128,256]{2,1,0:T(8,128)(2,1)S(1)}, u32[]{:S(2)}, u32[]{:S(2)}) %collective-permute-start.3) | collective-permute-done | bytes 131104 | tf_op jit(solution)/shard_map/ppermute | solution.py:408
  24.9 2.8 %collective-permute-start.4 = (bf16[2,128,128]{2,1,0:T(8,128)(2,1)S(1)}, bf16[2,128,128]{2,1,0:T(8,128)(2,1)S(1)}, u32[]{:S(2)}, u32[]{:S(2)}) collective-permute-start(bf16[2,128,128]{2,1,0:T(8,128)(2,1)S(1)} %shard_map.87), channel_id=1, source_target_pairs={{0,192},{8,200},{16,208},{24,216},{32,224},{40,232},{48,240},{56,2... | collective-permute-start | bytes 196616 | tf_op jit(solution)/shard_map/ppermute | solution.py:408
  27.7 2.7 %collective-permute-done.4.half_ref = bf16[2,128,128]{2,1,0:T(8,128)(2,1)S(1)} collective-permute-done((bf16[2,128,128]{2,1,0:T(8,128)(2,1)S(1)}, bf16[2,128,128]{2,1,0:T(8,128)(2,1)S(1)}, u32[]{:S(2)}, u32[]{:S(2)}) %collective-permute-start.4) | collective-permute-done | bytes 65568 | tf_op jit(solution)/shard_map/ppermute | solution.py:408
  30.4 0.7 %shard_map.88 = (bf16[2,128,256]{2,1,0:T(8,128)(2,1)S(1)}, bf16[2,128,128]{2,1,0:T(8,128)(2,1)S(1)}) custom-call(bf16[2,128,256]{2,1,0:T(8,128)(2,1)S(1)} %collective-permute-done.3.recv_ref, bf16[2,128,128]{2,1,0:T(8,128)(2,1)S(1)} %collective-permute-done.4.half_ref, f32[2,128,256]{2,1,0:T(8,128)S(1)} %get-tuple-element.39.prefix_ref, ...), custom_call_target="tpu_custom_call" | custom-call | flops 100000000 | bytes 1048576 | tf_op jit(solution)/shard_map/pallas_call | solution.py:385
  31.3 0.8 %shard_map.89.acc_ref = f32[256,2048]{1,0:T(8,128)S(1)} custom-call(bf16[2,128,256]{2,1,0:T(8,128)(2,1)S(1)} %get-tuple-element.42.state_ref, bf16[4,256,128]{2,1,0:T(8,128)(2,1)S(1)} %get-tuple-element.43.qeff_ref, f32[4,256,128]{2,1,0:T(8,128)S(1)} %get-tuple-element.37.after.local_ref, bf16[256,512]{1,0:T(8,128)(2,1)S(1)} %copy-done.1, ...), custom_call_target="tpu_custom_call" | custom-call | flops 1000000000 | bytes 1048576 | tf_op jit(solution)/shard_map/pallas_call | solution.py:385
  32.5 0.8 %shard_map.90 = (bf16[32,2048]{1,0:T(8,128)(2,1)S(1)}, bf16[32,2048]{1,0:T(8,128)(2,1)S(1)}, bf16[32,2048]{1,0:T(8,128)(2,1)S(1)}, bf16[32,2048]{1,0:T(8,128)(2,...) custom-call(bf16[2,128,128]{2,1,0:T(8,128)(2,1)S(1)} %collective-per, ...), custom_call_target="tpu_custom_call" | custom-call | flops 1000000000 | bytes 1048576 | tf_op jit(solution)/shard_map/pallas_call | solution.py:385
  33.3 2.0 %collective-permute-start.8 = (bf16[32,2048]{1,0:T(8,128)(2,1)S(1)}, bf16[32,2048]{1,0:T(8,128)(2,1)S(1)}, u32[]{:S(2)}, u32[]{:S(2)}) collective-permute-start(bf16[32,2048]{1,0:T(8,128)(2,1)S(1)} %get-tuple-element.48), channel_id=1, source_target_pairs={{0,1},{1,2},{2,3},{3,4},{4,5},{5,6},{6,7},{7,0},{8,9},{9,10},{10,1... | collective-permute-start | bytes 393224 | tf_op jit(solution)/shard_map/ppermute | solution.py:411
  35.3 4.0 %collective-permute-start.10 = (bf16[32,2048]{1,0:T(8,128)(2,1)S(1)}, bf16[32,2048]{1,0:T(8,128)(2,1)S(1)}, u32[]{:S(2)}, u32[]{:S(2)}) collective-permute-start(bf16[32,2048]{1,0:T(8,128)(2,1)S(1)} %get-tuple-element.51), channel_id=1, source_target_pairs={{0,7},{1,0},{2,1},{3,2},{4,3},{5,4},{6,5},{7,6},{8,15},{9,8},{10,9... | collective-permute-start | bytes 393224 | tf_op jit(solution)/shard_map/ppermute | solution.py:411
  39.3 4.1 %collective-permute-start.11 = (bf16[32,1024]{1,0:T(8,128)(2,1)S(1)}, bf16[32,1024]{1,0:T(8,128)(2,1)S(1)}, u32[]{:S(2)}, u32[]{:S(2)}) collective-permute-start(bf16[32,1024]{1,0:T(8,128)(2,1)S(1)} %get-tuple-element.52), channel_id=1, source_target_pairs={{0,6},{1,7},{2,0},{3,1},{4,2},{5,3},{6,4},{7,5},{8,14},{9,15},{10,... | collective-permute-start | bytes 196616 | tf_op jit(solution)/shard_map/ppermute | solution.py:411
  43.4 3.3 %collective-permute-done.9.a4_ref = bf16[32,1024]{1,0:T(8,128)(2,1)S(1)} collective-permute-done((bf16[32,1024]{1,0:T(8,128)(2,1)S(1)}, bf16[32,1024]{1,0:T(8,128)(2,1)S(1)}, u32[]{:S(2)}, u32[]{:S(2)}) %collective-permute-start.9) | collective-permute-done | bytes 65568 | tf_op jit(solution)/shard_map/ppermute | solution.py:411
  46.7 2.1 %collective-permute-start.7 = (bf16[32,2048]{1,0:T(8,128)(2,1)S(1)}, bf16[32,2048]{1,0:T(8,128)(2,1)S(1)}, u32[]{:S(2)}, u32[]{:S(2)}) collective-permute-start(bf16[32,2048]{1,0:T(8,128)(2,1)S(1)} %get-tuple-element.46), channel_id=1, source_target_pairs={{0,7},{1,0},{2,1},{3,2},{4,3},{5,4},{6,5},{7,6},{8,15},{9,8},{10,9... | collective-permute-start | bytes 393224 | tf_op jit(solution)/shard_map/ppermute | solution.py:411
  48.9 2.3 %collective-permute-start.12 = (bf16[32,2048]{1,0:T(8,128)(2,1)S(1)}, bf16[32,2048]{1,0:T(8,128)(2,1)S(1)}, u32[]{:S(2)}, u32[]{:S(2)}) collective-permute-start(bf16[32,2048]{1,0:T(8,128)(2,1)S(1)} %get-tuple-element.53), channel_id=1, source_target_pairs={{0,2},{1,3},{2,4},{3,5},{4,6},{5,7},{6,0},{7,1},{8,10},{9,11},{10,... | collective-permute-start | bytes 393224 | tf_op jit(solution)/shard_map/ppermute | solution.py:411
  51.2 1.9 %collective-permute-start.13 = (bf16[32,2048]{1,0:T(8,128)(2,1)S(1)}, bf16[32,2048]{1,0:T(8,128)(2,1)S(1)}, u32[]{:S(2)}, u32[]{:S(2)}) collective-permute-start(bf16[32,2048]{1,0:T(8,128)(2,1)S(1)} %get-tuple-element.54), channel_id=1, source_target_pairs={{0,6},{1,7},{2,0},{3,1},{4,2},{5,3},{6,4},{7,5},{8,14},{9,15},{10,... | collective-permute-start | bytes 393224 | tf_op jit(solution)/shard_map/ppermute | solution.py:411
  53.1 3.4 %collective-permute-done.12.refs_3_ = bf16[32,2048]{1,0:T(8,128)(2,1)S(1)} collective-permute-done((bf16[32,2048]{1,0:T(8,128)(2,1)S(1)}, bf16[32,2048]{1,0:T(8,128)(2,1)S(1)}, u32[]{:S(2)}, u32[]{:S(2)}) %collective-permute-start.12) | collective-permute-done | bytes 131104 | tf_op jit(solution)/shard_map/ppermute | solution.py:411
  56.5 1.7 %collective-permute-done.13.refs_4_ = bf16[32,2048]{1,0:T(8,128)(2,1)S(1)} collective-permute-done((bf16[32,2048]{1,0:T(8,128)(2,1)S(1)}, bf16[32,2048]{1,0:T(8,128)(2,1)S(1)}, u32[]{:S(2)}, u32[]{:S(2)}) %collective-permute-start.13) | collective-permute-done | bytes 131104 | tf_op jit(solution)/shard_map/ppermute | solution.py:411
  58.2 0.7 %shard_map.92 = bf16[32,2048]{1,0:T(8,128)(2,1)} custom-call(bf16[32,2048]{1,0:T(8,128)(2,1)S(1)} %get-tuple-element.44.refs_0_, bf16[32,2048]{1,0:T(8,128)(2,1)S(1)} %collective-permute-done.6.refs_1_, bf16[32,2048]{1,0:T(8,128)(2,1)S(1)} %collective-permute-done.7.refs_2_, bf16[32,2048]{1,0:T(8,128)(2,1)S(1)} %collective-permute-done.12.refs_3_, ...), custom_call_target="tpu_custom_call" | custom-call | flops 100000000 | bytes 1048576 | tf_op jit(solution)/shard_map/pallas_call | solution.py:385
  (25 shorter events, 1.6 us)
Async XLA Ops:
  0.0 8.2 %copy-start.3 = (bf16[256,512]{1,0:T(8,128)(2,1)S(1)}, bf16[256,512]{1,0:T(8,128)(2,1)}, u32[]{:S(2)}) copy-start(bf16[256,512]{1,0:T(8,128)(2,1)} %k_ref.1) | copy-start | bytes 786436
  0.0 8.2 %copy-start.4 = (bf16[256,512]{1,0:T(8,128)(2,1)S(1)}, bf16[256,512]{1,0:T(8,128)(2,1)}, u32[]{:S(2)}) copy-start(bf16[256,512]{1,0:T(8,128)(2,1)} %q_ref.1) | copy-start | bytes 786436
  5.6 1.4 %collective-permute-start = (bf16[2,128,256]{2,1,0:T(8,128)(2,1)S(1)}, bf16[2,128,256]{2,1,0:T(8,128)(2,1)S(1)}, u32[]{:S(2)}, u32[]{:S(2)}) collective-permute-start(bf16[2,128,256]{2,1,0:T(8,128)(2,1)S(1)} %get-tuple-element.31), channel_id=1, source_target_pairs={{0,8},{8,0},{16,24},{24,16},{32,40},{40,32},{48,56},{56,48},{64,72... | collective-permute-start | bytes 393224 | tf_op jit(solution)/shard_map/ppermute | solution.py:401
  7.3 5.6 %collective-permute-start.1 = (bf16[2,128,256]{2,1,0:T(8,128)(2,1)S(1)}, bf16[2,128,256]{2,1,0:T(8,128)(2,1)S(1)}, u32[]{:S(2)}, u32[]{:S(2)}) collective-permute-start(bf16[2,128,256]{2,1,0:T(8,128)(2,1)S(1)} %get-tuple-element.32.m_ref), channel_id=1, source_target_pairs={{0,16},{8,24},{16,0},{24,8},{32,48},{40,56},{48,32},{56,40},{64,80... | collective-permute-start | bytes 393224 | tf_op jit(solution)/shard_map/ppermute | solution.py:405
  9.5 21.8 %copy-start = (bf16[512,2048]{1,0:T(8,128)(2,1)S(1)}, bf16[512,2048]{1,0:T(8,128)(2,1)}, u32[]{:S(2)}) copy-start(bf16[512,2048]{1,0:T(8,128)(2,1)} %w_ref.3) | copy-start | bytes 6291460
  9.5 21.8 %copy-start.1 = (bf16[256,512]{1,0:T(8,128)(2,1)S(1)}, bf16[256,512]{1,0:T(8,128)(2,1)}, u32[]{:S(2)}) copy-start(bf16[256,512]{1,0:T(8,128)(2,1)} %gate_ref.3) | copy-start | bytes 786436
  9.5 21.8 %copy-start.2 = (f32[128]{0:T(128)S(1)}, f32[128]{0:T(128)}, u32[]{:S(2)}) copy-start(f32[128]{0:T(128)} %param.14) | copy-start | bytes 1540
  13.2 6.3 %collective-permute-start.2 = (bf16[2,128,256]{2,1,0:T(8,128)(2,1)S(1)}, bf16[2,128,256]{2,1,0:T(8,128)(2,1)S(1)}, u32[]{:S(2)}, u32[]{:S(2)}) collective-permute-start(bf16[2,128,256]{2,1,0:T(8,128)(2,1)S(1)} %shard_map.85.two_ref), channel_id=1, source_target_pairs={{0,48},{8,56},{16,32},{24,40},{32,16},{40,24},{48,0},{56,8},{64,11... | collective-permute-start | bytes 393224 | tf_op jit(solution)/shard_map/ppermute | solution.py:405
  19.7 5.1 %collective-permute-start.3 = (bf16[2,128,256]{2,1,0:T(8,128)(2,1)S(1)}, bf16[2,128,256]{2,1,0:T(8,128)(2,1)S(1)}, u32[]{:S(2)}, u32[]{:S(2)}) collective-permute-start(bf16[2,128,256]{2,1,0:T(8,128)(2,1)S(1)} %get-tuple-element.38.m_ref), channel_id=1, source_target_pairs={{0,64},{8,72},{16,80},{24,88},{32,96},{40,104},{48,112},{56,120},{... | collective-permute-start | bytes 393224 | tf_op jit(solution)/shard_map/ppermute | solution.py:408
  24.9 5.6 %collective-permute-start.4 = (bf16[2,128,128]{2,1,0:T(8,128)(2,1)S(1)}, bf16[2,128,128]{2,1,0:T(8,128)(2,1)S(1)}, u32[]{:S(2)}, u32[]{:S(2)}) collective-permute-start(bf16[2,128,128]{2,1,0:T(8,128)(2,1)S(1)} %shard_map.87), channel_id=1, source_target_pairs={{0,192},{8,200},{16,208},{24,216},{32,224},{40,232},{48,240},{56,2... | collective-permute-start | bytes 196616 | tf_op jit(solution)/shard_map/ppermute | solution.py:408
  31.1 1.3 %collective-permute-start.5 = (bf16[2,128,128]{2,1,0:T(8,128)(2,1)S(1)}, bf16[2,128,128]{2,1,0:T(8,128)(2,1)S(1)}, u32[]{:S(2)}, u32[]{:S(2)}) collective-permute-start(bf16[2,128,128]{2,1,0:T(8,128)(2,1)S(1)} %get-tuple-element.41), channel_id=1, source_target_pairs={{0,8},{8,0},{16,24},{24,16},{32,40},{40,32},{48,56},{56,48},{64,72... | collective-permute-start | bytes 196616 | tf_op jit(solution)/shard_map/ppermute | solution.py:401
  33.3 15.5 %collective-permute-start.8 = (bf16[32,2048]{1,0:T(8,128)(2,1)S(1)}, bf16[32,2048]{1,0:T(8,128)(2,1)S(1)}, u32[]{:S(2)}, u32[]{:S(2)}) collective-permute-start(bf16[32,2048]{1,0:T(8,128)(2,1)S(1)} %get-tuple-element.48), channel_id=1, source_target_pairs={{0,1},{1,2},{2,3},{3,4},{4,5},{5,6},{6,7},{7,0},{8,9},{9,10},{10,1... | collective-permute-start | bytes 393224 | tf_op jit(solution)/shard_map/ppermute | solution.py:411
  35.3 13.6 %collective-permute-start.10 = (bf16[32,2048]{1,0:T(8,128)(2,1)S(1)}, bf16[32,2048]{1,0:T(8,128)(2,1)S(1)}, u32[]{:S(2)}, u32[]{:S(2)}) collective-permute-start(bf16[32,2048]{1,0:T(8,128)(2,1)S(1)} %get-tuple-element.51), channel_id=1, source_target_pairs={{0,7},{1,0},{2,1},{3,2},{4,3},{5,4},{6,5},{7,6},{8,15},{9,8},{10,9... | collective-permute-start | bytes 393224 | tf_op jit(solution)/shard_map/ppermute | solution.py:411
  39.3 7.4 %collective-permute-start.9 = (bf16[32,1024]{1,0:T(8,128)(2,1)S(1)}, bf16[32,1024]{1,0:T(8,128)(2,1)S(1)}, u32[]{:S(2)}, u32[]{:S(2)}) collective-permute-start(bf16[32,1024]{1,0:T(8,128)(2,1)S(1)} %get-tuple-element.49), channel_id=1, source_target_pairs={{0,2},{1,3},{2,4},{3,5},{4,6},{5,7},{6,0},{7,1},{8,10},{9,11},{10,... | collective-permute-start | bytes 196616 | tf_op jit(solution)/shard_map/ppermute | solution.py:411
  39.3 9.5 %collective-permute-start.11 = (bf16[32,1024]{1,0:T(8,128)(2,1)S(1)}, bf16[32,1024]{1,0:T(8,128)(2,1)S(1)}, u32[]{:S(2)}, u32[]{:S(2)}) collective-permute-start(bf16[32,1024]{1,0:T(8,128)(2,1)S(1)} %get-tuple-element.52), channel_id=1, source_target_pairs={{0,6},{1,7},{2,0},{3,1},{4,2},{5,3},{6,4},{7,5},{8,14},{9,15},{10,... | collective-permute-start | bytes 196616 | tf_op jit(solution)/shard_map/ppermute | solution.py:411
  43.4 9.7 %collective-permute-start.6 = (bf16[32,2048]{1,0:T(8,128)(2,1)S(1)}, bf16[32,2048]{1,0:T(8,128)(2,1)S(1)}, u32[]{:S(2)}, u32[]{:S(2)}) collective-permute-start(bf16[32,2048]{1,0:T(8,128)(2,1)S(1)} %get-tuple-element.45), channel_id=1, source_target_pairs={{0,1},{1,2},{2,3},{3,4},{4,5},{5,6},{6,7},{7,0},{8,9},{9,10},{10,1... | collective-permute-start | bytes 393224 | tf_op jit(solution)/shard_map/ppermute | solution.py:411
  46.7 6.4 %collective-permute-start.7 = (bf16[32,2048]{1,0:T(8,128)(2,1)S(1)}, bf16[32,2048]{1,0:T(8,128)(2,1)S(1)}, u32[]{:S(2)}, u32[]{:S(2)}) collective-permute-start(bf16[32,2048]{1,0:T(8,128)(2,1)S(1)} %get-tuple-element.46), channel_id=1, source_target_pairs={{0,7},{1,0},{2,1},{3,2},{4,3},{5,4},{6,5},{7,6},{8,15},{9,8},{10,9... | collective-permute-start | bytes 393224 | tf_op jit(solution)/shard_map/ppermute | solution.py:411
  48.9 7.6 %collective-permute-start.12 = (bf16[32,2048]{1,0:T(8,128)(2,1)S(1)}, bf16[32,2048]{1,0:T(8,128)(2,1)S(1)}, u32[]{:S(2)}, u32[]{:S(2)}) collective-permute-start(bf16[32,2048]{1,0:T(8,128)(2,1)S(1)} %get-tuple-element.53), channel_id=1, source_target_pairs={{0,2},{1,3},{2,4},{3,5},{4,6},{5,7},{6,0},{7,1},{8,10},{9,11},{10,... | collective-permute-start | bytes 393224 | tf_op jit(solution)/shard_map/ppermute | solution.py:411
  51.2 7.0 %collective-permute-start.13 = (bf16[32,2048]{1,0:T(8,128)(2,1)S(1)}, bf16[32,2048]{1,0:T(8,128)(2,1)S(1)}, u32[]{:S(2)}, u32[]{:S(2)}) collective-permute-start(bf16[32,2048]{1,0:T(8,128)(2,1)S(1)} %get-tuple-element.54), channel_id=1, source_target_pairs={{0,6},{1,7},{2,0},{3,1},{4,2},{5,3},{6,4},{7,5},{8,14},{9,15},{10,... | collective-permute-start | bytes 393224 | tf_op jit(solution)/shard_map/ppermute | solution.py:411

commit v3 on v2

--- a/solution.py
+++ b/solution.py
@@ -66,6 +66,25 @@
 def follow(later, earlier):
     out = dot_wide(later[:, :HD], earlier)
     return lanes(out[:, :HD], out[:, HD:] + later[:, HD:])
+
+
+def odd_rows(a, size):
+    return rows(*[a[i : i + size] for i in range(size, C, 2 * size)])
+
+
+def at_odd_rows(a, size):
+    zero = jnp.zeros((size, a.shape[1]), a.dtype)
+    out = []
+    for i in range(0, C // 2, size):
+        out += [zero, a[i : i + size]]
+    return rows(*out)
+
+
+def minus_odd_rows(a, b, size):
+    out = []
+    for i in range(0, C // 2, size):
+        out += [a[2 * i : 2 * i + size], a[2 * i + size : 2 * i + 2 * size] - b[i : i + size]]
+    return rows(*out)
 
 
 def iota2(shape, dim):
@@ -157,13 +176,22 @@
     for p in range(NP):
         tp = ts[pl.ds(p, SUB, stride=NP), :]
         inverse.append(rows(*[jnp.where(lane_block == b, tp, 0.0) for b in range(C // SUB)]))
+    system = [split(lower[p]) for p in range(NP)]
     size = SUB
     while size < C:
-        rb = lax.div(row, size)
-        cb = lax.div(col, size)
-        mask = (rb == cb + 1) & (lax.rem(rb, 2) == 1)
-        mids = [dot_sq(jnp.where(mask, lower[p], 0.0), inverse[p]) for p in range(NP)]
-        inverse = [inverse[p] - dot_sq(inverse[p], mids[p]) for p in range(NP)]
+        mask = lax.div(odd_rows(row, size), size) == lax.div(odd_rows(col, size), size) + 1
+        parts = [split(inverse[p]) for p in range(NP)]
+        mids = []
+        for p in range(NP):
+            th, tl = parts[p]
+            nh, nl = (odd_rows(a, size) for a in system[p])
+            out = dot(lanes(nh, nl), rows(lanes(th, tl), lanes(th, jnp.zeros_like(tl))))
+            mids.append(split(jnp.where(mask, out[:, :C] + out[:, C:], 0.0)))
+        for p in range(NP):
+            th, tl = (odd_rows(a, size) for a in parts[p])
+            mh, ml = (at_odd_rows(a, size) for a in mids[p])
+            out = dot(lanes(th, tl), rows(lanes(mh, ml), lanes(mh, jnp.zeros_like(ml))))
+            inverse[p] = minus_odd_rows(inverse[p], out[:, :C] + out[:, C:], size)
         size *= 2
     copies[3].wait()
     maps = []
@@ -175,7 +203,7 @@
         erase = dot(lanes(eh, el), rows(kp, kp))
         write = dot(lanes(uh, ul), rows(vp, vp))
         both = lanes(erase, write)
-        wu_ref[p] = both.astype(BF16)
+        wu_ref[p] = rows(*split(both))
         wh, wl = split(both * column(2, p))
         out = dot_tn(rows(kp, kp), rows(wh, wl))
         decay = jnp.where(eye, jnp.exp(gend[p : p + 1, :]), 0.0)
@@ -220,8 +248,8 @@
         w = jnp.exp(jnp.where(incl, column(0, p) - vec[p : p + 1, :], 0.0))
         scores = w * (rq * vec[3 * NP + p : 3 * NP + p + 1, :]) * dot_nt(qp, part(k_ref, p))
         sh, sl = split(jnp.where(incl, scores, 0.0))
-        wu = wu_ref[p]
-        out = dot(lanes(sh, sl), rows(wu, wu))
+        wh, wl = wu_ref[p, :C], wu_ref[p, C:]
+        out = dot(lanes(sh, sl), rows(wh, wh)) + dot(sh, wl)
         qeff = (column(4, p) * rq) * qf - out[:, :HD]
         local = out[:, HD:]
         if n > 0:
@@ -245,64 +273,50 @@
     return lanes(out[:, :HD], out[:, HD:] + later[:, HD:].astype(F32))
 
 
-def two_kernel(m_ref, recv_ref, after, two_ref):
+def row_kernel(m_ref, r1_ref, r2_ref, r3_ref, after, total_ref, slots):
     del after
-    odd = lax.rem(y_index(), 2) == 1
+    y = y_index()
+    for d, ref in enumerate((m_ref, r1_ref, r2_ref, r3_ref)):
+        slots[jnp.bitwise_xor(y, d)] = ref[...]
     for h in range(OWN):
-        mine, other = m_ref[h], recv_ref[h]
-        early = jnp.where(odd, other, mine)
-        late = jnp.where(odd, mine, other)
-        two_ref[h] = follow_sent(late, early).astype(BF16)
-
-
-def row_kernel(recv_ref, two_ref, recv_two_ref, total_ref, prefix_ref):
+        m0, m1, m2, m3 = (slots[i, h] for i in range(4))
+        total_ref[h] = follow(follow_sent(m3, m2), follow_sent(m1, m0)).astype(BF16)
+
+
+def prefix_kernel(m_ref, r1_ref, r2_ref, r3_ref, early_ref, own_ref, other_ref, slots):
+    core = core_index()
     y = y_index()
+    for d, ref in enumerate((m_ref, r1_ref, r2_ref, r3_ref)):
+        slots[jnp.bitwise_xor(y, d)] = ref[...]
     eye = (iota2((HD, 2 * HD), 0) == iota2((HD, 2 * HD), 1)).astype(F32)
     for h in range(OWN):
-        mine, other = two_ref[h], recv_two_ref[h]
-        early = jnp.where(y >= 2, other, mine)
-        late = jnp.where(y >= 2, mine, other)
-        total_ref[h] = follow_sent(late, early).astype(BF16)
-        before = recv_ref[h]
-        prefix_ref[h] = jnp.where(
-            y == 0,
-            eye,
-            jnp.where(
-                y == 1,
-                before.astype(F32),
-                jnp.where(y == 2, early.astype(F32), follow_sent(before, early)),
-            ),
+        m0, m1, m2 = (slots[i, h] for i in range(3))
+        t01 = follow_sent(m1, m0)
+        th, tl = split(t01)
+        t012 = dot(m2[:, :HD], th) + dot(m2[:, :HD], tl)
+        t012 = lanes(t012[:, :HD], t012[:, HD:] + m2[:, HD:].astype(F32))
+        first = jnp.where(
+            y == 0, eye, jnp.where(y == 1, m0.astype(F32), jnp.where(y == 2, t01, t012))
         )
-
-
-def half_kernel(m_ref, recv_ref, add_ref):
-    odd = lax.rem(x_index(), 2) == 1
+        second = follow(early_ref[h], first)
+        own_ref[h] = jnp.where(core == 0, first, second)
+        other_ref[h] = jnp.where(core == 0, second, first)
+
+
+def state_kernel(m_ref, r1_ref, r2_ref, r3_ref, own_ref, other_ref, keep_ref, send_ref, slots):
+    x = x_index()
+    for d, ref in enumerate((m_ref, r1_ref, r2_ref, r3_ref)):
+        slots[jnp.bitwise_xor(x, d)] = ref[...]
     for h in range(OWN):
-        mine, other = m_ref[h], recv_ref[h]
-        early = jnp.where(odd, other, mine)
-        late = jnp.where(odd, mine, other)
-        out = dot(late[:, :HD], early[:, HD:]) + late[:, HD:].astype(F32)
-        add_ref[h] = out.astype(BF16)
-
-
-def state_kernel(recv_ref, half_ref, prefix_ref, early_ref, keep_ref, send_ref):
-    core = core_index()
-    x = x_index()
-    for h in range(OWN):
-        m = recv_ref[h]
-        half = half_ref[h]
-        through = dot(m[:, :HD], half)
-        state = jnp.where(x >= 2, half.astype(F32), 0.0)
-        state = jnp.where(x == 3, through, state)
-        state = state + jnp.where(lax.rem(x, 2) == 1, m[:, HD:].astype(F32), 0.0)
-        for_cores = []
-        for ref in (prefix_ref, early_ref):
-            m = ref[h]
-            state = dot_sq(m[:, :HD], state) + m[:, HD:]
-            for_cores.append(state)
-        hi, lo = split(jnp.where(core == 0, for_cores[0], for_cores[1]))
+        state = jnp.where(x > 0, slots[0, h][:, HD:].astype(F32), 0.0)
+        for i in (1, 2):
+            m = slots[i, h]
+            step = dot_exact_left(m[:, :HD], state) + m[:, HD:].astype(F32)
+            state = jnp.where(x > i, step, state)
+        own, other = own_ref[h], other_ref[h]
+        hi, lo = split(dot_sq(own[:, :HD], state) + own[:, HD:])
         keep_ref[h] = lanes(hi, lo)
-        send_ref[h] = jnp.where(core == 0, for_cores[1], for_cores[0]).astype(BF16)
+        send_ref[h] = (dot_sq(other[:, :HD], state) + other[:, HD:]).astype(BF16)
 
 
 def gated_rows(state, head, qeff_ref, local_ref, gate_ref, gain):
@@ -333,6 +347,7 @@
 
 
 STEP = 512
+ORDER_Y = (1, 2, 3)
 
 
 def own_kernel(state_ref, qeff_ref, local_ref, gate_ref, gain_ref, w_ref, acc_ref, gs, lhs):
@@ -414,7 +429,7 @@
     wu, vec, vect, first, keep, send = call(
         maps_kernel,
         [
-            ((NP, C, 2 * HD), BF16),
+            ((NP, 2 * C, 2 * HD), BF16),
             ((8 * NP, C), F32),
             ((C, 8 * NP), F32),
             ((HEADS, HD, 2 * HD), F32),
@@ -436,23 +451,33 @@
         vmem_mib=32,
     )
     total, early = call(pair_kernel, [(pair, BF16), (pair, F32)], (keep, swap(send)))
-    beside = across_y(total, 1)
+    around = [across_y(total, m) for m in ORDER_Y]
+    around = [around[ORDER_Y.index(m)] for m in (1, 2, 3)]
     qeff, local = call(
         reads_kernel,
         [((HEADS, tokens, HD), BF16), ((HEADS, tokens, HD), F32)],
         (q, k, wu, vec, vect, first),
         flops=10**9,
     )
-    (two,) = call(two_kernel, [(pair, BF16)], (total, beside, local), hbm={2: "any"})
-    row_total, prefix = call(
-        row_kernel, [(pair, BF16), (pair, F32)], (beside, two, across_y(two, 3))
-    )
-    beside_row = across_x(row_total, 1)
-    (half,) = call(half_kernel, [((OWN, HD, HD), BF16)], (row_total, beside_row))
+    (row_total,) = call(
+        row_kernel,
+        [(pair, BF16)],
+        (total, *around, local),
+        [pltpu.VMEM((4, *pair), BF16)],
+        hbm={4: "any"},
+    )
+    own, other = call(
+        prefix_kernel,
+        [(pair, F32)] * 2,
+        (total, *around, early),
+        [pltpu.VMEM((4, *pair), BF16)],
+    )
+    rows_around = [across_x(row_total, m) for m in (1, 2, 3)]
     own_state, send_state = call(
         state_kernel,
         [(pair, BF16), ((OWN, HD, HD), BF16)],
-        (beside_row, across_x(half, 3), prefix, early),
+        (row_total, *rows_around, own, other),
+        [pltpu.VMEM((4, *pair), BF16)],
     )
     other_state = swap(send_state)
     gain = gain.reshape(1, HD)

time: 59.1 us -> 57.1 us (0.966)
  waiting for transfers between devices: 24 us -> 19.5 us
  starting transfers between devices: 23.9 us -> 25.2 us
  Pallas kernels: 10.9 us -> 12.2 us
    ppermute x2 -> x3, waiting for transfers between devices: 7.68 us -> 4.43 us  [across_y(): return lax.ppermute(a, 'ctx', pairs)]
    ppermute x2 -> x3, starting transfers between devices: 2.87 us -> 4.18 us  [across_y(): return lax.ppermute(a, 'ctx', pairs)]
    pallas_call x11 -> x10, Pallas kernels: 10.9 us -> 12.2 us  [call(): pl.pallas_call(kernel, out_shape=[jax.ShapeDtypeStruct(s, t) for s, t in...]
    ppermute x2 -> x3, waiting for transfers between devices: 6.19 us -> 4.92 us  [across_x(): lax.ppermute(a, 'ctx', [(i, (i // 8 ^ m) * 8 + i % 8) for i in range(n_ct...]
    ppermute x2 -> x3, starting transfers between devices: 4.42 us -> 4.18 us  [across_x(): lax.ppermute(a, 'ctx', [(i, (i // 8 ^ m) * 8 + i % 8) for i in range(n_ct...]
  transfers between devices with their start and end apart: 14 -> 16, of which waited for: 9 -> 10; matrix products, arithmetic and copies ran while one was open for 0% -> 0% of each run, Pallas kernels for 4% -> 6%
where the time goes in v3:
time: 57.1 us; the launch traced here: 57 us
  starting transfers between devices  25.2 us (44%)
  waiting for transfers between devices  19.5 us (34%)
  Pallas kernels  12.2 us (21%)
    ppermute x8, starting transfers between devices, along_z(): return lax.ppermute(a, 'tp', [(i, (i + d) % TP) for i in range(TP)])  16.7 us
    pallas_call x10, Pallas kernels, call(): pl.pallas_call(kernel, out_shape=[jax.ShapeDtypeStruct(s, t) for s, t in...  12.2 us
    ppermute x8, waiting for transfers between devices, along_z(): return lax.ppermute(a, 'tp', [(i, (i + d) % TP) for i in range(TP)])  8.38 us
    ppermute x3, waiting for transfers between devices, across_x(): lax.ppermute(a, 'ctx', [(i, (i // 8 ^ m) * 8 + i % 8) for i in range(n_ct...  4.92 us
    ppermute x3, waiting for transfers between devices, across_y(): return lax.ppermute(a, 'ctx', pairs)  4.43 us
    ppermute x3, starting transfers between devices, across_x(): lax.ppermute(a, 'ctx', [(i, (i // 8 ^ m) * 8 + i % 8) for i in range(n_ct...  4.18 us
    ppermute x3, starting transfers between devices, across_y(): return lax.ppermute(a, 'ctx', pairs)  4.18 us
    ppermute x2, waiting for transfers between devices, swap(): return lax.ppermute(a, 'ctx', [(i, i ^ 1) for i in range(n_ctx)])  1.75 us
  transfers between devices with their start and end apart: 16, of which 10 were waited for; matrix products, arithmetic and copies ran while one was open for 0% of the time, Pallas kernels for 6%

profile of v3, /device:TPU:24, one launch (start us, length us, event | category | flops | bytes accessed | tf_op | source)
XLA Modules:
  0.0 57.0 jit_solution(2521432966310380746)
XLA Ops:
  0.0 5.6 %shard_map.82 = (bf16[8,256,256]{2,1,0:T(8,128)(2,1)S(1)}, f32[64,128]{1,0:T(8,128)S(1)}, f32[128,64]{1,0:T(8,128)S(1)}, f32[4,128,256]{2,1,0:T(8,128)S(1)}, f32...) custom-call(bf16[256,512]{1,0:T(8,128)(2,1)} %k_ref.1, bf16[256,512]{1,0:T(8,128)(2,1)} %v_hbm.1, ...), custom_call_target="tpu_custom_call" | custom-call | flops 1000000000 | bytes 1048576 | tf_op jit(solution)/shard_map/pallas_call | solution.py:400
  5.7 1.3 %collective-permute-done.recv_ref = bf16[2,128,256]{2,1,0:T(8,128)(2,1)S(1)} collective-permute-done((bf16[2,128,256]{2,1,0:T(8,128)(2,1)S(1)}, bf16[2,128,256]{2,1,0:T(8,128)(2,1)S(1)}, u32[]{:S(2)}, u32[]{:S(2)}) %collective-permute-start) | collective-permute-done | bytes 131104 | tf_op jit(solution)/shard_map/ppermute | solution.py:416
  7.3 2.0 %collective-permute-start.3 = (bf16[2,128,256]{2,1,0:T(8,128)(2,1)S(1)}, bf16[2,128,256]{2,1,0:T(8,128)(2,1)S(1)}, u32[]{:S(2)}, u32[]{:S(2)}) collective-permute-start(bf16[2,128,256]{2,1,0:T(8,128)(2,1)S(1)} %get-tuple-element.32.m_ref), channel_id=1, source_target_pairs={{0,48},{8,56},{16,32},{24,40},{32,16},{40,24},{48,0},{56,8},{64,11... | collective-permute-start | bytes 393224 | tf_op jit(solution)/shard_map/ppermute | solution.py:420
  9.4 0.8 %collective-permute-start.2 = (bf16[2,128,256]{2,1,0:T(8,128)(2,1)S(1)}, bf16[2,128,256]{2,1,0:T(8,128)(2,1)S(1)}, u32[]{:S(2)}, u32[]{:S(2)}) collective-permute-start(bf16[2,128,256]{2,1,0:T(8,128)(2,1)S(1)} %get-tuple-element.32.m_ref), channel_id=1, source_target_pairs={{0,32},{8,40},{16,48},{24,56},{32,0},{40,8},{48,16},{56,24},{64,96... | collective-permute-start | bytes 393224 | tf_op jit(solution)/shard_map/ppermute | solution.py:420
  10.2 1.3 %collective-permute-start.1 = (bf16[2,128,256]{2,1,0:T(8,128)(2,1)S(1)}, bf16[2,128,256]{2,1,0:T(8,128)(2,1)S(1)}, u32[]{:S(2)}, u32[]{:S(2)}) collective-permute-start(bf16[2,128,256]{2,1,0:T(8,128)(2,1)S(1)} %get-tuple-element.32.m_ref), channel_id=1, source_target_pairs={{0,16},{8,24},{16,0},{24,8},{32,48},{40,56},{48,32},{56,40},{64,80... | collective-permute-start | bytes 393224 | tf_op jit(solution)/shard_map/ppermute | solution.py:420
  11.5 1.6 %shard_map.84 = (bf16[4,256,128]{2,1,0:T(8,128)(2,1)S(1)}, f32[4,256,128]{2,1,0:T(8,128)S(1)}) custom-call(bf16[256,512]{1,0:T(8,128)(2,1)S(1)} %copy-done.4, bf16[256,512]{1,0:T(8,128)(2,1)S(1)} %copy-done.3, bf16[8,256,256]{2,1,0:T(8,128)(2,1)S(1)} %get-tuple-element.33.wu_ref, f32[64,128]{1,0:T(8,128)S(1)} %get-tuple-element.34.vec_ref, ...), custom_call_target="tpu_custom_call" | custom-call | flops 1000000000 | bytes 1048576 | tf_op jit(solution)/shard_map/pallas_call | solution.py:400
  13.2 3.5 %collective-permute-done.3.r3_ref = bf16[2,128,256]{2,1,0:T(8,128)(2,1)S(1)} collective-permute-done((bf16[2,128,256]{2,1,0:T(8,128)(2,1)S(1)}, bf16[2,128,256]{2,1,0:T(8,128)(2,1)S(1)}, u32[]{:S(2)}, u32[]{:S(2)}) %collective-permute-start.3) | collective-permute-done | bytes 131104 | tf_op jit(solution)/shard_map/ppermute | solution.py:420
  18.1 2.8 %collective-permute-start.6 = (bf16[2,128,256]{2,1,0:T(8,128)(2,1)S(1)}, bf16[2,128,256]{2,1,0:T(8,128)(2,1)S(1)}, u32[]{:S(2)}, u32[]{:S(2)}) collective-permute-start(bf16[2,128,256]{2,1,0:T(8,128)(2,1)S(1)} %shard_map.85.m_ref), channel_id=1, source_target_pairs={{0,192},{8,200},{16,208},{24,216},{32,224},{40,232},{48,240},{56,2... | collective-permute-start | bytes 393224 | tf_op jit(solution)/shard_map/ppermute | solution.py:423
  20.9 0.8 %collective-permute-start.5 = (bf16[2,128,256]{2,1,0:T(8,128)(2,1)S(1)}, bf16[2,128,256]{2,1,0:T(8,128)(2,1)S(1)}, u32[]{:S(2)}, u32[]{:S(2)}) collective-permute-start(bf16[2,128,256]{2,1,0:T(8,128)(2,1)S(1)} %shard_map.85.m_ref), channel_id=1, source_target_pairs={{0,128},{8,136},{16,144},{24,152},{32,160},{40,168},{48,176},{56,1... | collective-permute-start | bytes 393224 | tf_op jit(solution)/shard_map/ppermute | solution.py:423
  22.3 0.9 %shard_map.86 = (f32[2,128,256]{2,1,0:T(8,128)S(1)}, f32[2,128,256]{2,1,0:T(8,128)S(1)}) custom-call(bf16[2,128,256]{2,1,0:T(8,128)(2,1)S(1)} %get-tuple-element.32.m_ref, bf16[2,128,256]{2,1,0:T(8,128)(2,1)S(1)} %collective-permute-done.1.r1_ref, bf16[2,128,256]{2,1,0:T(8,128)(2,1)S(1)} %collective-permute-done.2.r2_ref, ...), custom_call_target="tpu_custom_call" | custom-call | flops 100000000 | bytes 1048576 | tf_op jit(solution)/shard_map/pallas_call | solution.py:400
  23.1 2.6 %collective-permute-done.6.r3_ref = bf16[2,128,256]{2,1,0:T(8,128)(2,1)S(1)} collective-permute-done((bf16[2,128,256]{2,1,0:T(8,128)(2,1)S(1)}, bf16[2,128,256]{2,1,0:T(8,128)(2,1)S(1)}, u32[]{:S(2)}, u32[]{:S(2)}) %collective-permute-start.6) | collective-permute-done | bytes 131104 | tf_op jit(solution)/shard_map/ppermute | solution.py:423
  25.8 2.3 %collective-permute-done.5.r2_ref = bf16[2,128,256]{2,1,0:T(8,128)(2,1)S(1)} collective-permute-done((bf16[2,128,256]{2,1,0:T(8,128)(2,1)S(1)}, bf16[2,128,256]{2,1,0:T(8,128)(2,1)S(1)}, u32[]{:S(2)}, u32[]{:S(2)}) %collective-permute-start.5) | collective-permute-done | bytes 131104 | tf_op jit(solution)/shard_map/ppermute | solution.py:423
  28.1 0.9 %shard_map.87 = (bf16[2,128,256]{2,1,0:T(8,128)(2,1)S(1)}, bf16[2,128,128]{2,1,0:T(8,128)(2,1)S(1)}) custom-call(bf16[2,128,256]{2,1,0:T(8,128)(2,1)S(1)} %shard_map.85.m_ref, bf16[2,128,256]{2,1,0:T(8,128)(2,1)S(1)} %collective-permute-done.4.r1_ref, bf16[2,128,256]{2,1,0:T(8,128)(2,1)S(1)} %collective-permute-done.5.r2_ref, ...), custom_call_target="tpu_custom_call" | custom-call | flops 100000000 | bytes 1048576 | tf_op jit(solution)/shard_map/pallas_call | solution.py:400
  29.1 0.8 %shard_map.88.acc_ref = f32[256,2048]{1,0:T(8,128)S(1)} custom-call(bf16[2,128,256]{2,1,0:T(8,128)(2,1)S(1)} %get-tuple-element.42.state_ref, bf16[4,256,128]{2,1,0:T(8,128)(2,1)S(1)} %get-tuple-element.43.qeff_ref, f32[4,256,128]{2,1,0:T(8,128)S(1)} %get-tuple-element.37.after.local_ref, bf16[256,512]{1,0:T(8,128)(2,1)S(1)} %copy-done.1, ...), custom_call_target="tpu_custom_call" | custom-call | flops 1000000000 | bytes 1048576 | tf_op jit(solution)/shard_map/pallas_call | solution.py:400
  30.3 0.8 %shard_map.89 = (bf16[32,2048]{1,0:T(8,128)(2,1)S(1)}, bf16[32,2048]{1,0:T(8,128)(2,1)S(1)}, bf16[32,2048]{1,0:T(8,128)(2,1)S(1)}, bf16[32,2048]{1,0:T(8,128)(2,...) custom-call(bf16[2,128,128]{2,1,0:T(8,128)(2,1)S(1)} %collective-per, ...), custom_call_target="tpu_custom_call" | custom-call | flops 1000000000 | bytes 1048576 | tf_op jit(solution)/shard_map/pallas_call | solution.py:400
  31.1 2.2 %collective-permute-start.10 = (bf16[32,2048]{1,0:T(8,128)(2,1)S(1)}, bf16[32,2048]{1,0:T(8,128)(2,1)S(1)}, u32[]{:S(2)}, u32[]{:S(2)}) collective-permute-start(bf16[32,2048]{1,0:T(8,128)(2,1)S(1)} %get-tuple-element.48), channel_id=1, source_target_pairs={{0,1},{1,2},{2,3},{3,4},{4,5},{5,6},{6,7},{7,0},{8,9},{9,10},{10,1... | collective-permute-start | bytes 393224 | tf_op jit(solution)/shard_map/ppermute | solution.py:426
  33.3 4.0 %collective-permute-start.12 = (bf16[32,2048]{1,0:T(8,128)(2,1)S(1)}, bf16[32,2048]{1,0:T(8,128)(2,1)S(1)}, u32[]{:S(2)}, u32[]{:S(2)}) collective-permute-start(bf16[32,2048]{1,0:T(8,128)(2,1)S(1)} %get-tuple-element.51), channel_id=1, source_target_pairs={{0,7},{1,0},{2,1},{3,2},{4,3},{5,4},{6,5},{7,6},{8,15},{9,8},{10,9... | collective-permute-start | bytes 393224 | tf_op jit(solution)/shard_map/ppermute | solution.py:426
  37.3 4.1 %collective-permute-start.13 = (bf16[32,1024]{1,0:T(8,128)(2,1)S(1)}, bf16[32,1024]{1,0:T(8,128)(2,1)S(1)}, u32[]{:S(2)}, u32[]{:S(2)}) collective-permute-start(bf16[32,1024]{1,0:T(8,128)(2,1)S(1)} %get-tuple-element.52), channel_id=1, source_target_pairs={{0,6},{1,7},{2,0},{3,1},{4,2},{5,3},{6,4},{7,5},{8,14},{9,15},{10,... | collective-permute-start | bytes 196616 | tf_op jit(solution)/shard_map/ppermute | solution.py:426
  41.5 3.3 %collective-permute-done.11.a4_ref = bf16[32,1024]{1,0:T(8,128)(2,1)S(1)} collective-permute-done((bf16[32,1024]{1,0:T(8,128)(2,1)S(1)}, bf16[32,1024]{1,0:T(8,128)(2,1)S(1)}, u32[]{:S(2)}, u32[]{:S(2)}) %collective-permute-start.11) | collective-permute-done | bytes 65568 | tf_op jit(solution)/shard_map/ppermute | solution.py:426
  44.7 2.1 %collective-permute-start.9 = (bf16[32,2048]{1,0:T(8,128)(2,1)S(1)}, bf16[32,2048]{1,0:T(8,128)(2,1)S(1)}, u32[]{:S(2)}, u32[]{:S(2)}) collective-permute-start(bf16[32,2048]{1,0:T(8,128)(2,1)S(1)} %get-tuple-element.46), channel_id=1, source_target_pairs={{0,7},{1,0},{2,1},{3,2},{4,3},{5,4},{6,5},{7,6},{8,15},{9,8},{10,9... | collective-permute-start | bytes 393224 | tf_op jit(solution)/shard_map/ppermute | solution.py:426
  47.0 2.3 %collective-permute-start.14 = (bf16[32,2048]{1,0:T(8,128)(2,1)S(1)}, bf16[32,2048]{1,0:T(8,128)(2,1)S(1)}, u32[]{:S(2)}, u32[]{:S(2)}) collective-permute-start(bf16[32,2048]{1,0:T(8,128)(2,1)S(1)} %get-tuple-element.53), channel_id=1, source_target_pairs={{0,2},{1,3},{2,4},{3,5},{4,6},{5,7},{6,0},{7,1},{8,10},{9,11},{10,... | collective-permute-start | bytes 393224 | tf_op jit(solution)/shard_map/ppermute | solution.py:426
  49.3 1.9 %collective-permute-start.15 = (bf16[32,2048]{1,0:T(8,128)(2,1)S(1)}, bf16[32,2048]{1,0:T(8,128)(2,1)S(1)}, u32[]{:S(2)}, u32[]{:S(2)}) collective-permute-start(bf16[32,2048]{1,0:T(8,128)(2,1)S(1)} %get-tuple-element.54), channel_id=1, source_target_pairs={{0,6},{1,7},{2,0},{3,1},{4,2},{5,3},{6,4},{7,5},{8,14},{9,15},{10,... | collective-permute-start | bytes 393224 | tf_op jit(solution)/shard_map/ppermute | solution.py:426
  51.2 3.4 %collective-permute-done.14.refs_3_ = bf16[32,2048]{1,0:T(8,128)(2,1)S(1)} collective-permute-done((bf16[32,2048]{1,0:T(8,128)(2,1)S(1)}, bf16[32,2048]{1,0:T(8,128)(2,1)S(1)}, u32[]{:S(2)}, u32[]{:S(2)}) %collective-permute-start.14) | collective-permute-done | bytes 131104 | tf_op jit(solution)/shard_map/ppermute | solution.py:426
  54.5 1.7 %collective-permute-done.15.refs_4_ = bf16[32,2048]{1,0:T(8,128)(2,1)S(1)} collective-permute-done((bf16[32,2048]{1,0:T(8,128)(2,1)S(1)}, bf16[32,2048]{1,0:T(8,128)(2,1)S(1)}, u32[]{:S(2)}, u32[]{:S(2)}) %collective-permute-start.15) | collective-permute-done | bytes 131104 | tf_op jit(solution)/shard_map/ppermute | solution.py:426
  (28 shorter events, 3.7 us)
Async XLA Ops:
  0.0 11.5 %copy-start.3 = (bf16[256,512]{1,0:T(8,128)(2,1)S(1)}, bf16[256,512]{1,0:T(8,128)(2,1)}, u32[]{:S(2)}) copy-start(bf16[256,512]{1,0:T(8,128)(2,1)} %k_ref.1) | copy-start | bytes 786436
  0.0 11.5 %copy-start.4 = (bf16[256,512]{1,0:T(8,128)(2,1)S(1)}, bf16[256,512]{1,0:T(8,128)(2,1)}, u32[]{:S(2)}) copy-start(bf16[256,512]{1,0:T(8,128)(2,1)} %q_ref.1) | copy-start | bytes 786436
  5.6 1.4 %collective-permute-start = (bf16[2,128,256]{2,1,0:T(8,128)(2,1)S(1)}, bf16[2,128,256]{2,1,0:T(8,128)(2,1)S(1)}, u32[]{:S(2)}, u32[]{:S(2)}) collective-permute-start(bf16[2,128,256]{2,1,0:T(8,128)(2,1)S(1)} %get-tuple-element.31), channel_id=1, source_target_pairs={{0,8},{8,0},{16,24},{24,16},{32,40},{40,32},{48,56},{56,48},{64,72... | collective-permute-start | bytes 393224 | tf_op jit(solution)/shard_map/ppermute | solution.py:416
  7.3 9.4 %collective-permute-start.3 = (bf16[2,128,256]{2,1,0:T(8,128)(2,1)S(1)}, bf16[2,128,256]{2,1,0:T(8,128)(2,1)S(1)}, u32[]{:S(2)}, u32[]{:S(2)}) collective-permute-start(bf16[2,128,256]{2,1,0:T(8,128)(2,1)S(1)} %get-tuple-element.32.m_ref), channel_id=1, source_target_pairs={{0,48},{8,56},{16,32},{24,40},{32,16},{40,24},{48,0},{56,8},{64,11... | collective-permute-start | bytes 393224 | tf_op jit(solution)/shard_map/ppermute | solution.py:420
  9.4 7.9 %collective-permute-start.2 = (bf16[2,128,256]{2,1,0:T(8,128)(2,1)S(1)}, bf16[2,128,256]{2,1,0:T(8,128)(2,1)S(1)}, u32[]{:S(2)}, u32[]{:S(2)}) collective-permute-start(bf16[2,128,256]{2,1,0:T(8,128)(2,1)S(1)} %get-tuple-element.32.m_ref), channel_id=1, source_target_pairs={{0,32},{8,40},{16,48},{24,56},{32,0},{40,8},{48,16},{56,24},{64,96... | collective-permute-start | bytes 393224 | tf_op jit(solution)/shard_map/ppermute | solution.py:420
  10.2 7.4 %collective-permute-start.1 = (bf16[2,128,256]{2,1,0:T(8,128)(2,1)S(1)}, bf16[2,128,256]{2,1,0:T(8,128)(2,1)S(1)}, u32[]{:S(2)}, u32[]{:S(2)}) collective-permute-start(bf16[2,128,256]{2,1,0:T(8,128)(2,1)S(1)} %get-tuple-element.32.m_ref), channel_id=1, source_target_pairs={{0,16},{8,24},{16,0},{24,8},{32,48},{40,56},{48,32},{56,40},{64,80... | collective-permute-start | bytes 393224 | tf_op jit(solution)/shard_map/ppermute | solution.py:420
  13.1 16.0 %copy-start = (bf16[512,2048]{1,0:T(8,128)(2,1)S(1)}, bf16[512,2048]{1,0:T(8,128)(2,1)}, u32[]{:S(2)}) copy-start(bf16[512,2048]{1,0:T(8,128)(2,1)} %w_ref.3) | copy-start | bytes 6291460
  13.1 16.0 %copy-start.1 = (bf16[256,512]{1,0:T(8,128)(2,1)S(1)}, bf16[256,512]{1,0:T(8,128)(2,1)}, u32[]{:S(2)}) copy-start(bf16[256,512]{1,0:T(8,128)(2,1)} %gate_ref.3) | copy-start | bytes 786436
  13.1 16.0 %copy-start.2 = (f32[128]{0:T(128)S(1)}, f32[128]{0:T(128)}, u32[]{:S(2)}) copy-start(f32[128]{0:T(128)} %param.14) | copy-start | bytes 1540
  18.1 7.7 %collective-permute-start.6 = (bf16[2,128,256]{2,1,0:T(8,128)(2,1)S(1)}, bf16[2,128,256]{2,1,0:T(8,128)(2,1)S(1)}, u32[]{:S(2)}, u32[]{:S(2)}) collective-permute-start(bf16[2,128,256]{2,1,0:T(8,128)(2,1)S(1)} %shard_map.85.m_ref), channel_id=1, source_target_pairs={{0,192},{8,200},{16,208},{24,216},{32,224},{40,232},{48,240},{56,2... | collective-permute-start | bytes 393224 | tf_op jit(solution)/shard_map/ppermute | solution.py:423
  20.9 7.2 %collective-permute-start.5 = (bf16[2,128,256]{2,1,0:T(8,128)(2,1)S(1)}, bf16[2,128,256]{2,1,0:T(8,128)(2,1)S(1)}, u32[]{:S(2)}, u32[]{:S(2)}) collective-permute-start(bf16[2,128,256]{2,1,0:T(8,128)(2,1)S(1)} %shard_map.85.m_ref), channel_id=1, source_target_pairs={{0,128},{8,136},{16,144},{24,152},{32,160},{40,168},{48,176},{56,1... | collective-permute-start | bytes 393224 | tf_op jit(solution)/shard_map/ppermute | solution.py:423
  21.7 6.4 %collective-permute-start.4 = (bf16[2,128,256]{2,1,0:T(8,128)(2,1)S(1)}, bf16[2,128,256]{2,1,0:T(8,128)(2,1)S(1)}, u32[]{:S(2)}, u32[]{:S(2)}) collective-permute-start(bf16[2,128,256]{2,1,0:T(8,128)(2,1)S(1)} %shard_map.85.m_ref), channel_id=1, source_target_pairs={{0,64},{8,72},{16,80},{24,88},{32,96},{40,104},{48,112},{56,120},{... | collective-permute-start | bytes 393224 | tf_op jit(solution)/shard_map/ppermute | solution.py:423
  29.0 1.3 %collective-permute-start.7 = (bf16[2,128,128]{2,1,0:T(8,128)(2,1)S(1)}, bf16[2,128,128]{2,1,0:T(8,128)(2,1)S(1)}, u32[]{:S(2)}, u32[]{:S(2)}) collective-permute-start(bf16[2,128,128]{2,1,0:T(8,128)(2,1)S(1)} %get-tuple-element.41), channel_id=1, source_target_pairs={{0,8},{8,0},{16,24},{24,16},{32,40},{40,32},{48,56},{56,48},{64,72... | collective-permute-start | bytes 196616 | tf_op jit(solution)/shard_map/ppermute | solution.py:416
  31.1 15.7 %collective-permute-start.10 = (bf16[32,2048]{1,0:T(8,128)(2,1)S(1)}, bf16[32,2048]{1,0:T(8,128)(2,1)S(1)}, u32[]{:S(2)}, u32[]{:S(2)}) collective-permute-start(bf16[32,2048]{1,0:T(8,128)(2,1)S(1)} %get-tuple-element.48), channel_id=1, source_target_pairs={{0,1},{1,2},{2,3},{3,4},{4,5},{5,6},{6,7},{7,0},{8,9},{9,10},{10,1... | collective-permute-start | bytes 393224 | tf_op jit(solution)/shard_map/ppermute | solution.py:426
  33.3 13.5 %collective-permute-start.12 = (bf16[32,2048]{1,0:T(8,128)(2,1)S(1)}, bf16[32,2048]{1,0:T(8,128)(2,1)S(1)}, u32[]{:S(2)}, u32[]{:S(2)}) collective-permute-start(bf16[32,2048]{1,0:T(8,128)(2,1)S(1)} %get-tuple-element.51), channel_id=1, source_target_pairs={{0,7},{1,0},{2,1},{3,2},{4,3},{5,4},{6,5},{7,6},{8,15},{9,8},{10,9... | collective-permute-start | bytes 393224 | tf_op jit(solution)/shard_map/ppermute | solution.py:426
  37.3 7.4 %collective-permute-start.11 = (bf16[32,1024]{1,0:T(8,128)(2,1)S(1)}, bf16[32,1024]{1,0:T(8,128)(2,1)S(1)}, u32[]{:S(2)}, u32[]{:S(2)}) collective-permute-start(bf16[32,1024]{1,0:T(8,128)(2,1)S(1)} %get-tuple-element.49), channel_id=1, source_target_pairs={{0,2},{1,3},{2,4},{3,5},{4,6},{5,7},{6,0},{7,1},{8,10},{9,11},{10,... | collective-permute-start | bytes 196616 | tf_op jit(solution)/shard_map/ppermute | solution.py:426
  37.3 9.5 %collective-permute-start.13 = (bf16[32,1024]{1,0:T(8,128)(2,1)S(1)}, bf16[32,1024]{1,0:T(8,128)(2,1)S(1)}, u32[]{:S(2)}, u32[]{:S(2)}) collective-permute-start(bf16[32,1024]{1,0:T(8,128)(2,1)S(1)} %get-tuple-element.52), channel_id=1, source_target_pairs={{0,6},{1,7},{2,0},{3,1},{4,2},{5,3},{6,4},{7,5},{8,14},{9,15},{10,... | collective-permute-start | bytes 196616 | tf_op jit(solution)/shard_map/ppermute | solution.py:426
  41.5 9.7 %collective-permute-start.8 = (bf16[32,2048]{1,0:T(8,128)(2,1)S(1)}, bf16[32,2048]{1,0:T(8,128)(2,1)S(1)}, u32[]{:S(2)}, u32[]{:S(2)}) collective-permute-start(bf16[32,2048]{1,0:T(8,128)(2,1)S(1)} %get-tuple-element.45), channel_id=1, source_target_pairs={{0,1},{1,2},{2,3},{3,4},{4,5},{5,6},{6,7},{7,0},{8,9},{9,10},{10,1... | collective-permute-start | bytes 393224 | tf_op jit(solution)/shard_map/ppermute | solution.py:426
  44.7 6.4 %collective-permute-start.9 = (bf16[32,2048]{1,0:T(8,128)(2,1)S(1)}, bf16[32,2048]{1,0:T(8,128)(2,1)S(1)}, u32[]{:S(2)}, u32[]{:S(2)}) collective-permute-start(bf16[32,2048]{1,0:T(8,128)(2,1)S(1)} %get-tuple-element.46), channel_id=1, source_target_pairs={{0,7},{1,0},{2,1},{3,2},{4,3},{5,4},{6,5},{7,6},{8,15},{9,8},{10,9... | collective-permute-start | bytes 393224 | tf_op jit(solution)/shard_map/ppermute | solution.py:426
  47.0 7.6 %collective-permute-start.14 = (bf16[32,2048]{1,0:T(8,128)(2,1)S(1)}, bf16[32,2048]{1,0:T(8,128)(2,1)S(1)}, u32[]{:S(2)}, u32[]{:S(2)}) collective-permute-start(bf16[32,2048]{1,0:T(8,128)(2,1)S(1)} %get-tuple-element.53), channel_id=1, source_target_pairs={{0,2},{1,3},{2,4},{3,5},{4,6},{5,7},{6,0},{7,1},{8,10},{9,11},{10,... | collective-permute-start | bytes 393224 | tf_op jit(solution)/shard_map/ppermute | solution.py:426
  49.3 7.0 %collective-permute-start.15 = (bf16[32,2048]{1,0:T(8,128)(2,1)S(1)}, bf16[32,2048]{1,0:T(8,128)(2,1)S(1)}, u32[]{:S(2)}, u32[]{:S(2)}) collective-permute-start(bf16[32,2048]{1,0:T(8,128)(2,1)S(1)} %get-tuple-element.54), channel_id=1, source_target_pairs={{0,6},{1,7},{2,0},{3,1},{4,2},{5,3},{6,4},{7,5},{8,14},{9,15},{10,... | collective-permute-start | bytes 393224 | tf_op jit(solution)/shard_map/ppermute | solution.py:426

commit v4 on v3

--- a/solution.py
+++ b/solution.py
@@ -131,10 +131,13 @@
     s2 = (r1 - s1.astype(F32)).astype(BF16)
     g = dot(s0, upper) + (dot(s1, upper) + dot(s2, upper))
     gram = []
+    flipped = []
     norms = []
     for p in range(NP):
         kp = part(k_ref, p)
-        kk = dot_nt(kp, kp)
+        kt = kp.T
+        flipped.append(kt)
+        kk = dot(kp, kt)
         gram.append(kk)
         norms.append(jnp.sum(jnp.where(eye, kk, 0.0), axis=0, keepdims=True))
     rn = 1.0 / jnp.sqrt(rows(*norms) + EPS)
@@ -185,13 +188,15 @@
         for p in range(NP):
             th, tl = parts[p]
             nh, nl = (odd_rows(a, size) for a in system[p])
-            out = dot(lanes(nh, nl), rows(lanes(th, tl), lanes(th, jnp.zeros_like(tl))))
-            mids.append(split(jnp.where(mask, out[:, :C] + out[:, C:], 0.0)))
+            out = dot(rows(nh, nl), th)
+            out = out[: C // 2] + out[C // 2 :] + dot(nh, tl)
+            mids.append(split(jnp.where(mask, out, 0.0)))
         for p in range(NP):
             th, tl = (odd_rows(a, size) for a in parts[p])
             mh, ml = (at_odd_rows(a, size) for a in mids[p])
-            out = dot(lanes(th, tl), rows(lanes(mh, ml), lanes(mh, jnp.zeros_like(ml))))
-            inverse[p] = minus_odd_rows(inverse[p], out[:, :C] + out[:, C:], size)
+            out = dot(rows(th, tl), mh)
+            out = out[: C // 2] + out[C // 2 :] + dot(th, ml)
+            inverse[p] = minus_odd_rows(inverse[p], out, size)
         size *= 2
     copies[3].wait()
     maps = []
@@ -205,7 +210,8 @@
         both = lanes(erase, write)
         wu_ref[p] = rows(*split(both))
         wh, wl = split(both * column(2, p))
-        out = dot_tn(rows(kp, kp), rows(wh, wl))
+        out = dot(flipped[p], lanes(wh, wl))
+        out = out[:, : 2 * HD] + out[:, 2 * HD :]
         decay = jnp.where(eye, jnp.exp(gend[p : p + 1, :]), 0.0)
         maps.append(lanes(decay - out[:, :HD], out[:, HD:]))
     whole = []

time: 57.1 us -> 56 us (0.981)
  Pallas kernels: 12.2 us -> 11 us
    pallas_call x10, Pallas kernels: 12.2 us -> 11 us  [call(): pl.pallas_call(kernel, out_shape=[jax.ShapeDtypeStruct(s, t) for s, t in...]
where the time goes in v4:
time: 56 us; the launch traced here: 55.9 us
  starting transfers between devices  25 us (45%)
  waiting for transfers between devices  19.6 us (35%)
  Pallas kernels  11 us (20%)
    ppermute x8, starting transfers between devices, along_z(): return lax.ppermute(a, 'tp', [(i, (i + d) % TP) for i in range(TP)])  16.5 us
    pallas_call x10, Pallas kernels, call(): pl.pallas_call(kernel, out_shape=[jax.ShapeDtypeStruct(s, t) for s, t in...  11 us
    ppermute x8, waiting for transfers between devices, along_z(): return lax.ppermute(a, 'tp', [(i, (i + d) % TP) for i in range(TP)])  8.51 us
    ppermute x3, waiting for transfers between devices, across_x(): lax.ppermute(a, 'ctx', [(i, (i // 8 ^ m) * 8 + i % 8) for i in range(n_ct...  4.93 us
    ppermute x3, waiting for transfers between devices, across_y(): return lax.ppermute(a, 'ctx', pairs)  4.43 us
    ppermute x3, starting transfers between devices, across_x(): lax.ppermute(a, 'ctx', [(i, (i // 8 ^ m) * 8 + i % 8) for i in range(n_ct...  4.18 us
    ppermute x3, starting transfers between devices, across_y(): return lax.ppermute(a, 'ctx', pairs)  4.18 us
    ppermute x2, waiting for transfers between devices, swap(): return lax.ppermute(a, 'ctx', [(i, i ^ 1) for i in range(n_ctx)])  1.75 us
  transfers between devices with their start and end apart: 16, of which 10 were waited for; matrix products, arithmetic and copies ran while one was open for 0% of the time, Pallas kernels for 6%

profile of v4, /device:TPU:24, one launch (start us, length us, event | category | flops | bytes accessed | tf_op | source)
XLA Modules:
  0.0 55.9 jit_solution(8573828543762640348)
XLA Ops:
  0.0 4.5 %shard_map.82 = (bf16[8,256,256]{2,1,0:T(8,128)(2,1)S(1)}, f32[64,128]{1,0:T(8,128)S(1)}, f32[128,64]{1,0:T(8,128)S(1)}, f32[4,128,256]{2,1,0:T(8,128)S(1)}, f32...) custom-call(bf16[256,512]{1,0:T(8,128)(2,1)} %k_ref.1, bf16[256,512]{1,0:T(8,128)(2,1)} %v_hbm.1, ...), custom_call_target="tpu_custom_call" | custom-call | flops 1000000000 | bytes 1048576 | tf_op jit(solution)/shard_map/pallas_call | solution.py:406
  4.6 1.3 %collective-permute-done.recv_ref = bf16[2,128,256]{2,1,0:T(8,128)(2,1)S(1)} collective-permute-done((bf16[2,128,256]{2,1,0:T(8,128)(2,1)S(1)}, bf16[2,128,256]{2,1,0:T(8,128)(2,1)S(1)}, u32[]{:S(2)}, u32[]{:S(2)}) %collective-permute-start) | collective-permute-done | bytes 131104 | tf_op jit(solution)/shard_map/ppermute | solution.py:422
  6.2 2.1 %collective-permute-start.3 = (bf16[2,128,256]{2,1,0:T(8,128)(2,1)S(1)}, bf16[2,128,256]{2,1,0:T(8,128)(2,1)S(1)}, u32[]{:S(2)}, u32[]{:S(2)}) collective-permute-start(bf16[2,128,256]{2,1,0:T(8,128)(2,1)S(1)} %get-tuple-element.32.m_ref), channel_id=1, source_target_pairs={{0,48},{8,56},{16,32},{24,40},{32,16},{40,24},{48,0},{56,8},{64,11... | collective-permute-start | bytes 393224 | tf_op jit(solution)/shard_map/ppermute | solution.py:426
  8.3 0.8 %collective-permute-start.2 = (bf16[2,128,256]{2,1,0:T(8,128)(2,1)S(1)}, bf16[2,128,256]{2,1,0:T(8,128)(2,1)S(1)}, u32[]{:S(2)}, u32[]{:S(2)}) collective-permute-start(bf16[2,128,256]{2,1,0:T(8,128)(2,1)S(1)} %get-tuple-element.32.m_ref), channel_id=1, source_target_pairs={{0,32},{8,40},{16,48},{24,56},{32,0},{40,8},{48,16},{56,24},{64,96... | collective-permute-start | bytes 393224 | tf_op jit(solution)/shard_map/ppermute | solution.py:426
  9.1 1.3 %collective-permute-start.1 = (bf16[2,128,256]{2,1,0:T(8,128)(2,1)S(1)}, bf16[2,128,256]{2,1,0:T(8,128)(2,1)S(1)}, u32[]{:S(2)}, u32[]{:S(2)}) collective-permute-start(bf16[2,128,256]{2,1,0:T(8,128)(2,1)S(1)} %get-tuple-element.32.m_ref), channel_id=1, source_target_pairs={{0,16},{8,24},{16,0},{24,8},{32,48},{40,56},{48,32},{56,40},{64,80... | collective-permute-start | bytes 393224 | tf_op jit(solution)/shard_map/ppermute | solution.py:426
  10.4 1.6 %shard_map.84 = (bf16[4,256,128]{2,1,0:T(8,128)(2,1)S(1)}, f32[4,256,128]{2,1,0:T(8,128)S(1)}) custom-call(bf16[256,512]{1,0:T(8,128)(2,1)S(1)} %copy-done.4, bf16[256,512]{1,0:T(8,128)(2,1)S(1)} %copy-done.3, bf16[8,256,256]{2,1,0:T(8,128)(2,1)S(1)} %get-tuple-element.33.wu_ref, f32[64,128]{1,0:T(8,128)S(1)} %get-tuple-element.34.vec_ref, ...), custom_call_target="tpu_custom_call" | custom-call | flops 1000000000 | bytes 1048576 | tf_op jit(solution)/shard_map/pallas_call | solution.py:406
  12.0 3.5 %collective-permute-done.3.r3_ref = bf16[2,128,256]{2,1,0:T(8,128)(2,1)S(1)} collective-permute-done((bf16[2,128,256]{2,1,0:T(8,128)(2,1)S(1)}, bf16[2,128,256]{2,1,0:T(8,128)(2,1)S(1)}, u32[]{:S(2)}, u32[]{:S(2)}) %collective-permute-start.3) | collective-permute-done | bytes 131104 | tf_op jit(solution)/shard_map/ppermute | solution.py:426
  17.0 2.8 %collective-permute-start.6 = (bf16[2,128,256]{2,1,0:T(8,128)(2,1)S(1)}, bf16[2,128,256]{2,1,0:T(8,128)(2,1)S(1)}, u32[]{:S(2)}, u32[]{:S(2)}) collective-permute-start(bf16[2,128,256]{2,1,0:T(8,128)(2,1)S(1)} %shard_map.85.m_ref), channel_id=1, source_target_pairs={{0,192},{8,200},{16,208},{24,216},{32,224},{40,232},{48,240},{56,2... | collective-permute-start | bytes 393224 | tf_op jit(solution)/shard_map/ppermute | solution.py:429
  19.8 0.8 %collective-permute-start.5 = (bf16[2,128,256]{2,1,0:T(8,128)(2,1)S(1)}, bf16[2,128,256]{2,1,0:T(8,128)(2,1)S(1)}, u32[]{:S(2)}, u32[]{:S(2)}) collective-permute-start(bf16[2,128,256]{2,1,0:T(8,128)(2,1)S(1)} %shard_map.85.m_ref), channel_id=1, source_target_pairs={{0,128},{8,136},{16,144},{24,152},{32,160},{40,168},{48,176},{56,1... | collective-permute-start | bytes 393224 | tf_op jit(solution)/shard_map/ppermute | solution.py:429
  21.2 0.9 %shard_map.86 = (f32[2,128,256]{2,1,0:T(8,128)S(1)}, f32[2,128,256]{2,1,0:T(8,128)S(1)}) custom-call(bf16[2,128,256]{2,1,0:T(8,128)(2,1)S(1)} %get-tuple-element.32.m_ref, bf16[2,128,256]{2,1,0:T(8,128)(2,1)S(1)} %collective-permute-done.1.r1_ref, bf16[2,128,256]{2,1,0:T(8,128)(2,1)S(1)} %collective-permute-done.2.r2_ref, ...), custom_call_target="tpu_custom_call" | custom-call | flops 100000000 | bytes 1048576 | tf_op jit(solution)/shard_map/pallas_call | solution.py:406
  22.0 2.6 %collective-permute-done.6.r3_ref = bf16[2,128,256]{2,1,0:T(8,128)(2,1)S(1)} collective-permute-done((bf16[2,128,256]{2,1,0:T(8,128)(2,1)S(1)}, bf16[2,128,256]{2,1,0:T(8,128)(2,1)S(1)}, u32[]{:S(2)}, u32[]{:S(2)}) %collective-permute-start.6) | collective-permute-done | bytes 131104 | tf_op jit(solution)/shard_map/ppermute | solution.py:429
  24.6 2.3 %collective-permute-done.5.r2_ref = bf16[2,128,256]{2,1,0:T(8,128)(2,1)S(1)} collective-permute-done((bf16[2,128,256]{2,1,0:T(8,128)(2,1)S(1)}, bf16[2,128,256]{2,1,0:T(8,128)(2,1)S(1)}, u32[]{:S(2)}, u32[]{:S(2)}) %collective-permute-start.5) | collective-permute-done | bytes 131104 | tf_op jit(solution)/shard_map/ppermute | solution.py:429
  27.0 0.9 %shard_map.87 = (bf16[2,128,256]{2,1,0:T(8,128)(2,1)S(1)}, bf16[2,128,128]{2,1,0:T(8,128)(2,1)S(1)}) custom-call(bf16[2,128,256]{2,1,0:T(8,128)(2,1)S(1)} %shard_map.85.m_ref, bf16[2,128,256]{2,1,0:T(8,128)(2,1)S(1)} %collective-permute-done.4.r1_ref, bf16[2,128,256]{2,1,0:T(8,128)(2,1)S(1)} %collective-permute-done.5.r2_ref, ...), custom_call_target="tpu_custom_call" | custom-call | flops 100000000 | bytes 1048576 | tf_op jit(solution)/shard_map/pallas_call | solution.py:406
  28.0 0.8 %shard_map.88.acc_ref = f32[256,2048]{1,0:T(8,128)S(1)} custom-call(bf16[2,128,256]{2,1,0:T(8,128)(2,1)S(1)} %get-tuple-element.42.state_ref, bf16[4,256,128]{2,1,0:T(8,128)(2,1)S(1)} %get-tuple-element.43.qeff_ref, f32[4,256,128]{2,1,0:T(8,128)S(1)} %get-tuple-element.37.after.local_ref, bf16[256,512]{1,0:T(8,128)(2,1)S(1)} %copy-done.1, ...), custom_call_target="tpu_custom_call" | custom-call | flops 1000000000 | bytes 1048576 | tf_op jit(solution)/shard_map/pallas_call | solution.py:406
  29.2 0.8 %shard_map.89 = (bf16[32,2048]{1,0:T(8,128)(2,1)S(1)}, bf16[32,2048]{1,0:T(8,128)(2,1)S(1)}, bf16[32,2048]{1,0:T(8,128)(2,1)S(1)}, bf16[32,2048]{1,0:T(8,128)(2,...) custom-call(bf16[2,128,128]{2,1,0:T(8,128)(2,1)S(1)} %collective-per, ...), custom_call_target="tpu_custom_call" | custom-call | flops 1000000000 | bytes 1048576 | tf_op jit(solution)/shard_map/pallas_call | solution.py:406
  30.0 2.0 %collective-permute-start.10 = (bf16[32,2048]{1,0:T(8,128)(2,1)S(1)}, bf16[32,2048]{1,0:T(8,128)(2,1)S(1)}, u32[]{:S(2)}, u32[]{:S(2)}) collective-permute-start(bf16[32,2048]{1,0:T(8,128)(2,1)S(1)} %get-tuple-element.48), channel_id=1, source_target_pairs={{0,1},{1,2},{2,3},{3,4},{4,5},{5,6},{6,7},{7,0},{8,9},{9,10},{10,1... | collective-permute-start | bytes 393224 | tf_op jit(solution)/shard_map/ppermute | solution.py:432
  32.0 4.2 %collective-permute-start.12 = (bf16[32,2048]{1,0:T(8,128)(2,1)S(1)}, bf16[32,2048]{1,0:T(8,128)(2,1)S(1)}, u32[]{:S(2)}, u32[]{:S(2)}) collective-permute-start(bf16[32,2048]{1,0:T(8,128)(2,1)S(1)} %get-tuple-element.51), channel_id=1, source_target_pairs={{0,7},{1,0},{2,1},{3,2},{4,3},{5,4},{6,5},{7,6},{8,15},{9,8},{10,9... | collective-permute-start | bytes 393224 | tf_op jit(solution)/shard_map/ppermute | solution.py:432
  36.2 4.1 %collective-permute-start.13 = (bf16[32,1024]{1,0:T(8,128)(2,1)S(1)}, bf16[32,1024]{1,0:T(8,128)(2,1)S(1)}, u32[]{:S(2)}, u32[]{:S(2)}) collective-permute-start(bf16[32,1024]{1,0:T(8,128)(2,1)S(1)} %get-tuple-element.52), channel_id=1, source_target_pairs={{0,6},{1,7},{2,0},{3,1},{4,2},{5,3},{6,4},{7,5},{8,14},{9,15},{10,... | collective-permute-start | bytes 196616 | tf_op jit(solution)/shard_map/ppermute | solution.py:432
  40.4 3.3 %collective-permute-done.11.a4_ref = bf16[32,1024]{1,0:T(8,128)(2,1)S(1)} collective-permute-done((bf16[32,1024]{1,0:T(8,128)(2,1)S(1)}, bf16[32,1024]{1,0:T(8,128)(2,1)S(1)}, u32[]{:S(2)}, u32[]{:S(2)}) %collective-permute-start.11) | collective-permute-done | bytes 65568 | tf_op jit(solution)/shard_map/ppermute | solution.py:432
  43.6 1.9 %collective-permute-start.9 = (bf16[32,2048]{1,0:T(8,128)(2,1)S(1)}, bf16[32,2048]{1,0:T(8,128)(2,1)S(1)}, u32[]{:S(2)}, u32[]{:S(2)}) collective-permute-start(bf16[32,2048]{1,0:T(8,128)(2,1)S(1)} %get-tuple-element.46), channel_id=1, source_target_pairs={{0,7},{1,0},{2,1},{3,2},{4,3},{5,4},{6,5},{7,6},{8,15},{9,8},{10,9... | collective-permute-start | bytes 393224 | tf_op jit(solution)/shard_map/ppermute | solution.py:432
  45.7 2.2 %collective-permute-start.14 = (bf16[32,2048]{1,0:T(8,128)(2,1)S(1)}, bf16[32,2048]{1,0:T(8,128)(2,1)S(1)}, u32[]{:S(2)}, u32[]{:S(2)}) collective-permute-start(bf16[32,2048]{1,0:T(8,128)(2,1)S(1)} %get-tuple-element.53), channel_id=1, source_target_pairs={{0,2},{1,3},{2,4},{3,5},{4,6},{5,7},{6,0},{7,1},{8,10},{9,11},{10,... | collective-permute-start | bytes 393224 | tf_op jit(solution)/shard_map/ppermute | solution.py:432
  47.9 2.0 %collective-permute-start.15 = (bf16[32,2048]{1,0:T(8,128)(2,1)S(1)}, bf16[32,2048]{1,0:T(8,128)(2,1)S(1)}, u32[]{:S(2)}, u32[]{:S(2)}) collective-permute-start(bf16[32,2048]{1,0:T(8,128)(2,1)S(1)} %get-tuple-element.54), channel_id=1, source_target_pairs={{0,6},{1,7},{2,0},{3,1},{4,2},{5,3},{6,4},{7,5},{8,14},{9,15},{10,... | collective-permute-start | bytes 393224 | tf_op jit(solution)/shard_map/ppermute | solution.py:432
  49.9 4.1 %collective-permute-done.14.refs_3_ = bf16[32,2048]{1,0:T(8,128)(2,1)S(1)} collective-permute-done((bf16[32,2048]{1,0:T(8,128)(2,1)S(1)}, bf16[32,2048]{1,0:T(8,128)(2,1)S(1)}, u32[]{:S(2)}, u32[]{:S(2)}) %collective-permute-start.14) | collective-permute-done | bytes 131104 | tf_op jit(solution)/shard_map/ppermute | solution.py:432
  54.0 1.1 %collective-permute-done.15.refs_4_ = bf16[32,2048]{1,0:T(8,128)(2,1)S(1)} collective-permute-done((bf16[32,2048]{1,0:T(8,128)(2,1)S(1)}, bf16[32,2048]{1,0:T(8,128)(2,1)S(1)}, u32[]{:S(2)}, u32[]{:S(2)}) %collective-permute-start.15) | collective-permute-done | bytes 131104 | tf_op jit(solution)/shard_map/ppermute | solution.py:432
  (28 shorter events, 3.7 us)
Async XLA Ops:
  0.0 10.4 %copy-start.3 = (bf16[256,512]{1,0:T(8,128)(2,1)S(1)}, bf16[256,512]{1,0:T(8,128)(2,1)}, u32[]{:S(2)}) copy-start(bf16[256,512]{1,0:T(8,128)(2,1)} %k_ref.1) | copy-start | bytes 786436
  0.0 10.4 %copy-start.4 = (bf16[256,512]{1,0:T(8,128)(2,1)S(1)}, bf16[256,512]{1,0:T(8,128)(2,1)}, u32[]{:S(2)}) copy-start(bf16[256,512]{1,0:T(8,128)(2,1)} %q_ref.1) | copy-start | bytes 786436
  4.5 1.4 %collective-permute-start = (bf16[2,128,256]{2,1,0:T(8,128)(2,1)S(1)}, bf16[2,128,256]{2,1,0:T(8,128)(2,1)S(1)}, u32[]{:S(2)}, u32[]{:S(2)}) collective-permute-start(bf16[2,128,256]{2,1,0:T(8,128)(2,1)S(1)} %get-tuple-element.31), channel_id=1, source_target_pairs={{0,8},{8,0},{16,24},{24,16},{32,40},{40,32},{48,56},{56,48},{64,72... | collective-permute-start | bytes 393224 | tf_op jit(solution)/shard_map/ppermute | solution.py:422
  6.2 9.4 %collective-permute-start.3 = (bf16[2,128,256]{2,1,0:T(8,128)(2,1)S(1)}, bf16[2,128,256]{2,1,0:T(8,128)(2,1)S(1)}, u32[]{:S(2)}, u32[]{:S(2)}) collective-permute-start(bf16[2,128,256]{2,1,0:T(8,128)(2,1)S(1)} %get-tuple-element.32.m_ref), channel_id=1, source_target_pairs={{0,48},{8,56},{16,32},{24,40},{32,16},{40,24},{48,0},{56,8},{64,11... | collective-permute-start | bytes 393224 | tf_op jit(solution)/shard_map/ppermute | solution.py:426
  8.3 7.9 %collective-permute-start.2 = (bf16[2,128,256]{2,1,0:T(8,128)(2,1)S(1)}, bf16[2,128,256]{2,1,0:T(8,128)(2,1)S(1)}, u32[]{:S(2)}, u32[]{:S(2)}) collective-permute-start(bf16[2,128,256]{2,1,0:T(8,128)(2,1)S(1)} %get-tuple-element.32.m_ref), channel_id=1, source_target_pairs={{0,32},{8,40},{16,48},{24,56},{32,0},{40,8},{48,16},{56,24},{64,96... | collective-permute-start | bytes 393224 | tf_op jit(solution)/shard_map/ppermute | solution.py:426
  9.1 7.4 %collective-permute-start.1 = (bf16[2,128,256]{2,1,0:T(8,128)(2,1)S(1)}, bf16[2,128,256]{2,1,0:T(8,128)(2,1)S(1)}, u32[]{:S(2)}, u32[]{:S(2)}) collective-permute-start(bf16[2,128,256]{2,1,0:T(8,128)(2,1)S(1)} %get-tuple-element.32.m_ref), channel_id=1, source_target_pairs={{0,16},{8,24},{16,0},{24,8},{32,48},{40,56},{48,32},{56,40},{64,80... | collective-permute-start | bytes 393224 | tf_op jit(solution)/shard_map/ppermute | solution.py:426
  12.0 16.0 %copy-start = (bf16[512,2048]{1,0:T(8,128)(2,1)S(1)}, bf16[512,2048]{1,0:T(8,128)(2,1)}, u32[]{:S(2)}) copy-start(bf16[512,2048]{1,0:T(8,128)(2,1)} %w_ref.3) | copy-start | bytes 6291460
  12.0 16.0 %copy-start.1 = (bf16[256,512]{1,0:T(8,128)(2,1)S(1)}, bf16[256,512]{1,0:T(8,128)(2,1)}, u32[]{:S(2)}) copy-start(bf16[256,512]{1,0:T(8,128)(2,1)} %gate_ref.3) | copy-start | bytes 786436
  12.0 16.0 %copy-start.2 = (f32[128]{0:T(128)S(1)}, f32[128]{0:T(128)}, u32[]{:S(2)}) copy-start(f32[128]{0:T(128)} %param.14) | copy-start | bytes 1540
  17.0 7.7 %collective-permute-start.6 = (bf16[2,128,256]{2,1,0:T(8,128)(2,1)S(1)}, bf16[2,128,256]{2,1,0:T(8,128)(2,1)S(1)}, u32[]{:S(2)}, u32[]{:S(2)}) collective-permute-start(bf16[2,128,256]{2,1,0:T(8,128)(2,1)S(1)} %shard_map.85.m_ref), channel_id=1, source_target_pairs={{0,192},{8,200},{16,208},{24,216},{32,224},{40,232},{48,240},{56,2... | collective-permute-start | bytes 393224 | tf_op jit(solution)/shard_map/ppermute | solution.py:429
  19.8 7.2 %collective-permute-start.5 = (bf16[2,128,256]{2,1,0:T(8,128)(2,1)S(1)}, bf16[2,128,256]{2,1,0:T(8,128)(2,1)S(1)}, u32[]{:S(2)}, u32[]{:S(2)}) collective-permute-start(bf16[2,128,256]{2,1,0:T(8,128)(2,1)S(1)} %shard_map.85.m_ref), channel_id=1, source_target_pairs={{0,128},{8,136},{16,144},{24,152},{32,160},{40,168},{48,176},{56,1... | collective-permute-start | bytes 393224 | tf_op jit(solution)/shard_map/ppermute | solution.py:429
  20.6 6.4 %collective-permute-start.4 = (bf16[2,128,256]{2,1,0:T(8,128)(2,1)S(1)}, bf16[2,128,256]{2,1,0:T(8,128)(2,1)S(1)}, u32[]{:S(2)}, u32[]{:S(2)}) collective-permute-start(bf16[2,128,256]{2,1,0:T(8,128)(2,1)S(1)} %shard_map.85.m_ref), channel_id=1, source_target_pairs={{0,64},{8,72},{16,80},{24,88},{32,96},{40,104},{48,112},{56,120},{... | collective-permute-start | bytes 393224 | tf_op jit(solution)/shard_map/ppermute | solution.py:429
  27.9 1.3 %collective-permute-start.7 = (bf16[2,128,128]{2,1,0:T(8,128)(2,1)S(1)}, bf16[2,128,128]{2,1,0:T(8,128)(2,1)S(1)}, u32[]{:S(2)}, u32[]{:S(2)}) collective-permute-start(bf16[2,128,128]{2,1,0:T(8,128)(2,1)S(1)} %get-tuple-element.41), channel_id=1, source_target_pairs={{0,8},{8,0},{16,24},{24,16},{32,40},{40,32},{48,56},{56,48},{64,72... | collective-permute-start | bytes 196616 | tf_op jit(solution)/shard_map/ppermute | solution.py:422
  30.0 15.5 %collective-permute-start.10 = (bf16[32,2048]{1,0:T(8,128)(2,1)S(1)}, bf16[32,2048]{1,0:T(8,128)(2,1)S(1)}, u32[]{:S(2)}, u32[]{:S(2)}) collective-permute-start(bf16[32,2048]{1,0:T(8,128)(2,1)S(1)} %get-tuple-element.48), channel_id=1, source_target_pairs={{0,1},{1,2},{2,3},{3,4},{4,5},{5,6},{6,7},{7,0},{8,9},{9,10},{10,1... | collective-permute-start | bytes 393224 | tf_op jit(solution)/shard_map/ppermute | solution.py:432
  32.0 13.6 %collective-permute-start.12 = (bf16[32,2048]{1,0:T(8,128)(2,1)S(1)}, bf16[32,2048]{1,0:T(8,128)(2,1)S(1)}, u32[]{:S(2)}, u32[]{:S(2)}) collective-permute-start(bf16[32,2048]{1,0:T(8,128)(2,1)S(1)} %get-tuple-element.51), channel_id=1, source_target_pairs={{0,7},{1,0},{2,1},{3,2},{4,3},{5,4},{6,5},{7,6},{8,15},{9,8},{10,9... | collective-permute-start | bytes 393224 | tf_op jit(solution)/shard_map/ppermute | solution.py:432
  36.2 7.4 %collective-permute-start.11 = (bf16[32,1024]{1,0:T(8,128)(2,1)S(1)}, bf16[32,1024]{1,0:T(8,128)(2,1)S(1)}, u32[]{:S(2)}, u32[]{:S(2)}) collective-permute-start(bf16[32,1024]{1,0:T(8,128)(2,1)S(1)} %get-tuple-element.49), channel_id=1, source_target_pairs={{0,2},{1,3},{2,4},{3,5},{4,6},{5,7},{6,0},{7,1},{8,10},{9,11},{10,... | collective-permute-start | bytes 196616 | tf_op jit(solution)/shard_map/ppermute | solution.py:432
  36.2 9.4 %collective-permute-start.13 = (bf16[32,1024]{1,0:T(8,128)(2,1)S(1)}, bf16[32,1024]{1,0:T(8,128)(2,1)S(1)}, u32[]{:S(2)}, u32[]{:S(2)}) collective-permute-start(bf16[32,1024]{1,0:T(8,128)(2,1)S(1)} %get-tuple-element.52), channel_id=1, source_target_pairs={{0,6},{1,7},{2,0},{3,1},{4,2},{5,3},{6,4},{7,5},{8,14},{9,15},{10,... | collective-permute-start | bytes 196616 | tf_op jit(solution)/shard_map/ppermute | solution.py:432
  40.4 9.5 %collective-permute-start.8 = (bf16[32,2048]{1,0:T(8,128)(2,1)S(1)}, bf16[32,2048]{1,0:T(8,128)(2,1)S(1)}, u32[]{:S(2)}, u32[]{:S(2)}) collective-permute-start(bf16[32,2048]{1,0:T(8,128)(2,1)S(1)} %get-tuple-element.45), channel_id=1, source_target_pairs={{0,1},{1,2},{2,3},{3,4},{4,5},{5,6},{6,7},{7,0},{8,9},{9,10},{10,1... | collective-permute-start | bytes 393224 | tf_op jit(solution)/shard_map/ppermute | solution.py:432
  43.6 6.3 %collective-permute-start.9 = (bf16[32,2048]{1,0:T(8,128)(2,1)S(1)}, bf16[32,2048]{1,0:T(8,128)(2,1)S(1)}, u32[]{:S(2)}, u32[]{:S(2)}) collective-permute-start(bf16[32,2048]{1,0:T(8,128)(2,1)S(1)} %get-tuple-element.46), channel_id=1, source_target_pairs={{0,7},{1,0},{2,1},{3,2},{4,3},{5,4},{6,5},{7,6},{8,15},{9,8},{10,9... | collective-permute-start | bytes 393224 | tf_op jit(solution)/shard_map/ppermute | solution.py:432
  45.7 8.4 %collective-permute-start.14 = (bf16[32,2048]{1,0:T(8,128)(2,1)S(1)}, bf16[32,2048]{1,0:T(8,128)(2,1)S(1)}, u32[]{:S(2)}, u32[]{:S(2)}) collective-permute-start(bf16[32,2048]{1,0:T(8,128)(2,1)S(1)} %get-tuple-element.53), channel_id=1, source_target_pairs={{0,2},{1,3},{2,4},{3,5},{4,6},{5,7},{6,0},{7,1},{8,10},{9,11},{10,... | collective-permute-start | bytes 393224 | tf_op jit(solution)/shard_map/ppermute | solution.py:432
  47.9 7.2 %collective-permute-start.15 = (bf16[32,2048]{1,0:T(8,128)(2,1)S(1)}, bf16[32,2048]{1,0:T(8,128)(2,1)S(1)}, u32[]{:S(2)}, u32[]{:S(2)}) collective-permute-start(bf16[32,2048]{1,0:T(8,128)(2,1)S(1)} %get-tuple-element.54), channel_id=1, source_target_pairs={{0,6},{1,7},{2,0},{3,1},{4,2},{5,3},{6,4},{7,5},{8,14},{9,15},{10,... | collective-permute-start | bytes 393224 | tf_op jit(solution)/shard_map/ppermute | solution.py:432

commit v5 on v4

--- a/solution.py
+++ b/solution.py
@@ -139,7 +139,8 @@
         flipped.append(kt)
         kk = dot(kp, kt)
         gram.append(kk)
-        norms.append(jnp.sum(jnp.where(eye, kk, 0.0), axis=0, keepdims=True))
+        kf = kt.astype(F32)
+        norms.append(jnp.sum(kf * kf, axis=0, keepdims=True))
     rn = 1.0 / jnp.sqrt(rows(*norms) + EPS)
     eg = jnp.exp(g)
     gend = g[:, C - 1 : C]
@@ -223,7 +224,8 @@
         send_ref[h] = jnp.where(core == 0, whole[OWN + h], whole[h]).astype(BF16)
 
 
-def pair_kernel(keep_ref, recv_ref, total_ref, early_ref):
+def pair_kernel(keep_ref, recv_ref, *refs):
+    *total_refs, early_ref = refs
     core = core_index()
     for h in range(OWN):
         mine = keep_ref[h]
@@ -231,10 +233,15 @@
         early = jnp.where(core == 0, mine, other)
         late = jnp.where(core == 0, other, mine)
         early_ref[h] = early
-        total_ref[h] = follow(late, early).astype(BF16)
-
-
-def reads_kernel(q_ref, k_ref, wu_ref, vec_ref, vect_ref, first_ref, qeff_ref, local_ref):
+        total = follow(late, early).astype(BF16)
+        for ref in total_refs:
+            ref[h] = total
+
+
+def reads_kernel(
+    q_ref, k_ref, wu_ref, vec_ref, vect_ref, first_ref, gate_ref, gain_ref,
+    qeff_ref, local_ref, factor_ref,
+):
     row = iota2((C, C), 0)
     col = iota2((C, C), 1)
     incl = row >= col
@@ -246,6 +253,9 @@
         i = kind * NP + p
         return vect[:, i : i + 1]
 
+    for h in range(HEADS):
+        gate = gate_ref[:, h * HD : h * HD + HD].astype(F32)
+        factor_ref[h] = gain_ref[...] * (gate / (1.0 + jnp.exp(-gate)))
     for p in range(NP):
         n, h = divmod(p, HEADS)
         qp = part(q_ref, p)
@@ -279,14 +289,17 @@
     return lanes(out[:, :HD], out[:, HD:] + later[:, HD:].astype(F32))
 
 
-def row_kernel(m_ref, r1_ref, r2_ref, r3_ref, after, total_ref, slots):
+def row_kernel(m_ref, r1_ref, r2_ref, r3_ref, after, *refs):
     del after
+    *total_refs, slots = refs
     y = y_index()
     for d, ref in enumerate((m_ref, r1_ref, r2_ref, r3_ref)):
         slots[jnp.bitwise_xor(y, d)] = ref[...]
     for h in range(OWN):
         m0, m1, m2, m3 = (slots[i, h] for i in range(4))
-        total_ref[h] = follow(follow_sent(m3, m2), follow_sent(m1, m0)).astype(BF16)
+        total = follow(follow_sent(m3, m2), follow_sent(m1, m0)).astype(BF16)
+        for ref in total_refs:
+            ref[h] = total
 
 
 def prefix_kernel(m_ref, r1_ref, r2_ref, r3_ref, early_ref, own_ref, other_ref, slots):
@@ -325,21 +338,19 @@
         send_ref[h] = (dot_sq(other[:, :HD], state) + other[:, HD:]).astype(BF16)
 
 
-def gated_rows(state, head, qeff_ref, local_ref, gate_ref, gain):
+def gated_rows(state, head, qeff_ref, local_ref, factor_ref):
     out = dot(qeff_ref[head], state)
     core_rows = local_ref[head] + out[:, :HD]
     if state.shape[1] > HD:
         core_rows = core_rows + out[:, HD:]
     mean = jnp.mean(core_rows * core_rows, axis=1, keepdims=True)
-    gate = gate_ref[:, pl.ds(pl.multiple_of(head * HD, HD), HD)].astype(F32)
-    silu = gate / (1.0 + jnp.exp(-gate))
-    return (core_rows / jnp.sqrt(mean + EPS) * gain * silu).astype(BF16)
-
-
-def gather_rows(state_ref, first, qeff_ref, local_ref, gate_ref, gain_ref, gs, lhs):
+    return (core_rows * (1.0 / jnp.sqrt(mean + EPS)) * factor_ref[head]).astype(BF16)
+
+
+def gather_rows(state_ref, first, qeff_ref, local_ref, factor_ref, gs, lhs):
     for h in range(OWN):
         gs[:, h * HD : h * HD + HD] = gated_rows(
-            state_ref[h], first + h, qeff_ref, local_ref, gate_ref, gain_ref[...]
+            state_ref[h], first + h, qeff_ref, local_ref, factor_ref
         )
     me = lax.axis_index("tp")
     chunk = gs.shape[0] // TP
@@ -354,22 +365,21 @@
 
 STEP = 512
 ORDER_Y = (1, 2, 3)
-
-
-def own_kernel(state_ref, qeff_ref, local_ref, gate_ref, gain_ref, w_ref, acc_ref, gs, lhs):
+ORDER_X = (1, 2, 3)
+
+
+def own_kernel(state_ref, qeff_ref, local_ref, factor_ref, w_ref, acc_ref, gs, lhs):
     first = OWN * core_index()
-    gather_rows(state_ref, first, qeff_ref, local_ref, gate_ref, gain_ref, gs, lhs)
+    gather_rows(state_ref, first, qeff_ref, local_ref, factor_ref, gs, lhs)
     for j in range(w_ref.shape[1] // STEP):
         s = slice(j * STEP, j * STEP + STEP)
         acc_ref[:, s] = dot(lhs[...], weight_rows(w_ref, first, s))
 
 
-def other_kernel(
-    state_ref, acc_ref, qeff_ref, local_ref, gate_ref, gain_ref, w_ref, *refs
-):
+def other_kernel(state_ref, acc_ref, qeff_ref, local_ref, factor_ref, w_ref, *refs):
     outs, (gs, lhs) = refs[:-2], refs[-2:]
     first = OWN * (1 - core_index())
-    gather_rows(state_ref, first, qeff_ref, local_ref, gate_ref, gain_ref, gs, lhs)
+    gather_rows(state_ref, first, qeff_ref, local_ref, factor_ref, gs, lhs)
     chunk = gs.shape[0] // TP
     for j in range(w_ref.shape[1] // STEP):
         s = slice(j * STEP, j * STEP + STEP)
@@ -456,18 +466,18 @@
         flops=10**9,
         vmem_mib=32,
     )
-    total, early = call(pair_kernel, [(pair, BF16), (pair, F32)], (keep, swap(send)))
-    around = [across_y(total, m) for m in ORDER_Y]
-    around = [around[ORDER_Y.index(m)] for m in (1, 2, 3)]
-    qeff, local = call(
+    *totals, early = call(pair_kernel, [(pair, BF16)] * 3 + [(pair, F32)], (keep, swap(send)))
+    total = totals[0]
+    around = [across_y(totals[ORDER_Y.index(m)], m) for m in (1, 2, 3)]
+    qeff, local, factor = call(
         reads_kernel,
-        [((HEADS, tokens, HD), BF16), ((HEADS, tokens, HD), F32)],
-        (q, k, wu, vec, vect, first),
+        [((HEADS, tokens, HD), BF16)] + [((HEADS, tokens, HD), F32)] * 2,
+        (q, k, wu, vec, vect, first, gate, gain.reshape(1, HD)),
         flops=10**9,
     )
-    (row_total,) = call(
+    row_totals = call(
         row_kernel,
-        [(pair, BF16)],
+        [(pair, BF16)] * 3,
         (total, *around, local),
         [pltpu.VMEM((4, *pair), BF16)],
         hbm={4: "any"},
@@ -478,21 +488,20 @@
         (total, *around, early),
         [pltpu.VMEM((4, *pair), BF16)],
     )
-    rows_around = [across_x(row_total, m) for m in (1, 2, 3)]
+    rows_around = [across_x(row_totals[ORDER_X.index(m)], m) for m in (1, 2, 3)]
     own_state, send_state = call(
         state_kernel,
         [(pair, BF16), ((OWN, HD, HD), BF16)],
-        (row_total, *rows_around, own, other),
+        (row_totals[0], *rows_around, own, other),
         [pltpu.VMEM((4, *pair), BF16)],
     )
     other_state = swap(send_state)
-    gain = gain.reshape(1, HD)
     rows_scratch = [pltpu.VMEM((tokens, OWN * HD), BF16)] * 2
     width = w.shape[1]
     (acc,) = call(
         own_kernel,
         [((tokens, width), F32)],
-        (own_state, qeff, local, gate, gain, w),
+        (own_state, qeff, local, factor, w),
         rows_scratch,
         flops=10**9,
     )
@@ -501,7 +510,7 @@
     p0, p1, p2, p3, p5, p6, p7, p4a, p4b = call(
         other_kernel,
         [block] * 7 + [((rows_here, width // 2), BF16)] * 2,
-        (other_state, acc, qeff, local, gate, gain, w),
+        (other_state, acc, qeff, local, factor, w),
         rows_scratch,
         flops=10**9,
     )

time: 56 us -> 55.5 us (level)
    ppermute x3, starting transfers between devices: 4.18 us -> 3.57 us  [across_y(): return lax.ppermute(a, 'ctx', pairs)]
where the time goes in v5:
time: 55.5 us; the launch traced here: 55.4 us
  starting transfers between devices  24.5 us (44%)
  waiting for transfers between devices  19.7 us (35%)
  Pallas kernels  11 us (20%)
    ppermute x8, starting transfers between devices, along_z(): return lax.ppermute(a, 'tp', [(i, (i + d) % TP) for i in range(TP)])  16.5 us
    pallas_call x10, Pallas kernels, call(): pl.pallas_call(kernel, out_shape=[jax.ShapeDtypeStruct(s, t) for s, t in...  11 us
    ppermute x8, waiting for transfers between devices, along_z(): return lax.ppermute(a, 'tp', [(i, (i + d) % TP) for i in range(TP)])  8.51 us
    ppermute x3, waiting for transfers between devices, across_x(): lax.ppermute(a, 'ctx', [(i, (i // 8 ^ m) * 8 + i % 8) for i in range(n_ct...  4.77 us
    ppermute x3, waiting for transfers between devices, across_y(): return lax.ppermute(a, 'ctx', pairs)  4.61 us
    ppermute x3, starting transfers between devices, across_x(): lax.ppermute(a, 'ctx', [(i, (i // 8 ^ m) * 8 + i % 8) for i in range(n_ct...  4.27 us
    ppermute x3, starting transfers between devices, across_y(): return lax.ppermute(a, 'ctx', pairs)  3.57 us
    ppermute x2, waiting for transfers between devices, swap(): return lax.ppermute(a, 'ctx', [(i, i ^ 1) for i in range(n_ctx)])  1.81 us
  transfers between devices with their start and end apart: 16, of which 10 were waited for; matrix products, arithmetic and copies ran while one was open for 0% of the time, Pallas kernels for 6%

profile of v5, /device:TPU:24, one launch (start us, length us, event | category | flops | bytes accessed | tf_op | source)
XLA Modules:
  0.0 55.4 jit_solution(18206924107195070324)
XLA Ops:
  0.0 4.4 %shard_map.82 = (bf16[8,256,256]{2,1,0:T(8,128)(2,1)S(1)}, f32[64,128]{1,0:T(8,128)S(1)}, f32[128,64]{1,0:T(8,128)S(1)}, f32[4,128,256]{2,1,0:T(8,128)S(1)}, f32...) custom-call(bf16[256,512]{1,0:T(8,128)(2,1)} %k_ref.1, bf16[256,512]{1,0:T(8,128)(2,1)} %v_hbm.1, ...), custom_call_target="tpu_custom_call" | custom-call | flops 1000000000 | bytes 1048576 | tf_op jit(solution)/shard_map/pallas_call | solution.py:416
  4.5 1.3 %collective-permute-done.recv_ref = bf16[2,128,256]{2,1,0:T(8,128)(2,1)S(1)} collective-permute-done((bf16[2,128,256]{2,1,0:T(8,128)(2,1)S(1)}, bf16[2,128,256]{2,1,0:T(8,128)(2,1)S(1)}, u32[]{:S(2)}, u32[]{:S(2)}) %collective-permute-start) | collective-permute-done | bytes 131104 | tf_op jit(solution)/shard_map/ppermute | solution.py:432
  6.2 1.3 %collective-permute-start.2 = (bf16[2,128,256]{2,1,0:T(8,128)(2,1)S(1)}, bf16[2,128,256]{2,1,0:T(8,128)(2,1)S(1)}, u32[]{:S(2)}, u32[]{:S(2)}) collective-permute-start(bf16[2,128,256]{2,1,0:T(8,128)(2,1)S(1)} %get-tuple-element.39), channel_id=1, source_target_pairs={{0,32},{8,40},{16,48},{24,56},{32,0},{40,8},{48,16},{56,24},{64,96... | collective-permute-start | bytes 393224 | tf_op jit(solution)/shard_map/ppermute | solution.py:436
  7.5 2.2 %collective-permute-start.3 = (bf16[2,128,256]{2,1,0:T(8,128)(2,1)S(1)}, bf16[2,128,256]{2,1,0:T(8,128)(2,1)S(1)}, u32[]{:S(2)}, u32[]{:S(2)}) collective-permute-start(bf16[2,128,256]{2,1,0:T(8,128)(2,1)S(1)} %get-tuple-element.40), channel_id=1, source_target_pairs={{0,48},{8,56},{16,32},{24,40},{32,16},{40,24},{48,0},{56,8},{64,11... | collective-permute-start | bytes 393224 | tf_op jit(solution)/shard_map/ppermute | solution.py:436
  9.7 1.7 %shard_map.84 = (bf16[4,256,128]{2,1,0:T(8,128)(2,1)S(1)}, f32[4,256,128]{2,1,0:T(8,128)S(1)}, f32[4,256,128]{2,1,0:T(8,128)S(1)}) custom-call(bf16[256,512]{1,0:T(8,128)(2,1)S(1)} %copy-done.2, bf16[256,512]{1,0:T(8,128)(2,1)S(1)} %copy-done.1, bf16[8,256,256]{2,1,0:T(8,128)(2,1)S(1)} %get-tuple-element.41.wu_ref, f32[64,128]{1,0:T(8,128)S(1)} %get-tuple-element.42.vec_ref, ...), custom_call_target="tpu_custom_call" | custom-call | flops 1000000000 | bytes 1048576 | tf_op jit(solution)/shard_map/pallas_call | solution.py:416
  11.5 2.6 %collective-permute-done.2.r2_ref = bf16[2,128,256]{2,1,0:T(8,128)(2,1)S(1)} collective-permute-done((bf16[2,128,256]{2,1,0:T(8,128)(2,1)S(1)}, bf16[2,128,256]{2,1,0:T(8,128)(2,1)S(1)}, u32[]{:S(2)}, u32[]{:S(2)}) %collective-permute-start.2) | collective-permute-done | bytes 131104 | tf_op jit(solution)/shard_map/ppermute | solution.py:436
  14.1 2.0 %collective-permute-done.3.r3_ref = bf16[2,128,256]{2,1,0:T(8,128)(2,1)S(1)} collective-permute-done((bf16[2,128,256]{2,1,0:T(8,128)(2,1)S(1)}, bf16[2,128,256]{2,1,0:T(8,128)(2,1)S(1)}, u32[]{:S(2)}, u32[]{:S(2)}) %collective-permute-start.3) | collective-permute-done | bytes 131104 | tf_op jit(solution)/shard_map/ppermute | solution.py:436
  16.6 3.1 %collective-permute-start.5 = (bf16[2,128,256]{2,1,0:T(8,128)(2,1)S(1)}, bf16[2,128,256]{2,1,0:T(8,128)(2,1)S(1)}, u32[]{:S(2)}, u32[]{:S(2)}) collective-permute-start(bf16[2,128,256]{2,1,0:T(8,128)(2,1)S(1)} %get-tuple-element.47), channel_id=1, source_target_pairs={{0,128},{8,136},{16,144},{24,152},{32,160},{40,168},{48,176},{56,1... | collective-permute-start | bytes 393224 | tf_op jit(solution)/shard_map/ppermute | solution.py:439
  19.8 1.1 %collective-permute-start.6 = (bf16[2,128,256]{2,1,0:T(8,128)(2,1)S(1)}, bf16[2,128,256]{2,1,0:T(8,128)(2,1)S(1)}, u32[]{:S(2)}, u32[]{:S(2)}) collective-permute-start(bf16[2,128,256]{2,1,0:T(8,128)(2,1)S(1)} %get-tuple-element.48), channel_id=1, source_target_pairs={{0,192},{8,200},{16,208},{24,216},{32,224},{40,232},{48,240},{56,2... | collective-permute-start | bytes 393224 | tf_op jit(solution)/shard_map/ppermute | solution.py:439
  20.9 0.9 %shard_map.86 = (f32[2,128,256]{2,1,0:T(8,128)S(1)}, f32[2,128,256]{2,1,0:T(8,128)S(1)}) custom-call(bf16[2,128,256]{2,1,0:T(8,128)(2,1)S(1)} %get-tuple-element.38.m_ref, bf16[2,128,256]{2,1,0:T(8,128)(2,1)S(1)} %collective-permute-done.1.r1_ref, bf16[2,128,256]{2,1,0:T(8,128)(2,1)S(1)} %collective-permute-done.2.r2_ref, ...), custom_call_target="tpu_custom_call" | custom-call | flops 100000000 | bytes 1048576 | tf_op jit(solution)/shard_map/pallas_call | solution.py:416
  21.8 1.9 %collective-permute-done.5.r2_ref = bf16[2,128,256]{2,1,0:T(8,128)(2,1)S(1)} collective-permute-done((bf16[2,128,256]{2,1,0:T(8,128)(2,1)S(1)}, bf16[2,128,256]{2,1,0:T(8,128)(2,1)S(1)}, u32[]{:S(2)}, u32[]{:S(2)}) %collective-permute-start.5) | collective-permute-done | bytes 131104 | tf_op jit(solution)/shard_map/ppermute | solution.py:439
  23.7 2.8 %collective-permute-done.6.r3_ref = bf16[2,128,256]{2,1,0:T(8,128)(2,1)S(1)} collective-permute-done((bf16[2,128,256]{2,1,0:T(8,128)(2,1)S(1)}, bf16[2,128,256]{2,1,0:T(8,128)(2,1)S(1)}, u32[]{:S(2)}, u32[]{:S(2)}) %collective-permute-start.6) | collective-permute-done | bytes 131104 | tf_op jit(solution)/shard_map/ppermute | solution.py:439
  26.5 0.9 %shard_map.87 = (bf16[2,128,256]{2,1,0:T(8,128)(2,1)S(1)}, bf16[2,128,128]{2,1,0:T(8,128)(2,1)S(1)}) custom-call(bf16[2,128,256]{2,1,0:T(8,128)(2,1)S(1)} %get-tuple-element.46.m_ref, bf16[2,128,256]{2,1,0:T(8,128)(2,1)S(1)} %collective-permute-done.4.r1_ref, bf16[2,128,256]{2,1,0:T(8,128)(2,1)S(1)} %collective-permute-done.5.r2_ref, ...), custom_call_target="tpu_custom_call" | custom-call | flops 100000000 | bytes 1048576 | tf_op jit(solution)/shard_map/pallas_call | solution.py:416
  27.6 0.8 %shard_map.88.acc_ref = f32[256,2048]{1,0:T(8,128)S(1)} custom-call(bf16[2,128,256]{2,1,0:T(8,128)(2,1)S(1)} %get-tuple-element.53.state_ref, bf16[4,256,128]{2,1,0:T(8,128)(2,1)S(1)} %get-tuple-element.54.qeff_ref, f32[4,256,128]{2,1,0:T(8,128)S(1)} %get-tuple-element.45.after.local_ref, f32[4,256,128]{2,1,0:T(8,128)S(1)} %get-tuple-element.55.factor_ref, ...), custom_call_target="tpu_custom_call" | custom-call | flops 1000000000 | bytes 1048576 | tf_op jit(solution)/shard_map/pallas_call | solution.py:416
  28.8 0.8 %shard_map.89 = (bf16[32,2048]{1,0:T(8,128)(2,1)S(1)}, bf16[32,2048]{1,0:T(8,128)(2,1)S(1)}, bf16[32,2048]{1,0:T(8,128)(2,1)S(1)}, bf16[32,2048]{1,0:T(8,128)(2,...) custom-call(bf16[2,128,128]{2,1,0:T(8,128)(2,1)S(1)} %collective-per, ...), custom_call_target="tpu_custom_call" | custom-call | flops 1000000000 | bytes 1048576 | tf_op jit(solution)/shard_map/pallas_call | solution.py:416
  29.6 2.0 %collective-permute-start.10 = (bf16[32,2048]{1,0:T(8,128)(2,1)S(1)}, bf16[32,2048]{1,0:T(8,128)(2,1)S(1)}, u32[]{:S(2)}, u32[]{:S(2)}) collective-permute-start(bf16[32,2048]{1,0:T(8,128)(2,1)S(1)} %get-tuple-element.60), channel_id=1, source_target_pairs={{0,1},{1,2},{2,3},{3,4},{4,5},{5,6},{6,7},{7,0},{8,9},{9,10},{10,1... | collective-permute-start | bytes 393224 | tf_op jit(solution)/shard_map/ppermute | solution.py:442
  31.6 4.2 %collective-permute-start.12 = (bf16[32,2048]{1,0:T(8,128)(2,1)S(1)}, bf16[32,2048]{1,0:T(8,128)(2,1)S(1)}, u32[]{:S(2)}, u32[]{:S(2)}) collective-permute-start(bf16[32,2048]{1,0:T(8,128)(2,1)S(1)} %get-tuple-element.63), channel_id=1, source_target_pairs={{0,7},{1,0},{2,1},{3,2},{4,3},{5,4},{6,5},{7,6},{8,15},{9,8},{10,9... | collective-permute-start | bytes 393224 | tf_op jit(solution)/shard_map/ppermute | solution.py:442
  35.8 4.1 %collective-permute-start.13 = (bf16[32,1024]{1,0:T(8,128)(2,1)S(1)}, bf16[32,1024]{1,0:T(8,128)(2,1)S(1)}, u32[]{:S(2)}, u32[]{:S(2)}) collective-permute-start(bf16[32,1024]{1,0:T(8,128)(2,1)S(1)} %get-tuple-element.64), channel_id=1, source_target_pairs={{0,6},{1,7},{2,0},{3,1},{4,2},{5,3},{6,4},{7,5},{8,14},{9,15},{10,... | collective-permute-start | bytes 196616 | tf_op jit(solution)/shard_map/ppermute | solution.py:442
  39.9 3.3 %collective-permute-done.11.a4_ref = bf16[32,1024]{1,0:T(8,128)(2,1)S(1)} collective-permute-done((bf16[32,1024]{1,0:T(8,128)(2,1)S(1)}, bf16[32,1024]{1,0:T(8,128)(2,1)S(1)}, u32[]{:S(2)}, u32[]{:S(2)}) %collective-permute-start.11) | collective-permute-done | bytes 65568 | tf_op jit(solution)/shard_map/ppermute | solution.py:442
  43.2 1.9 %collective-permute-start.9 = (bf16[32,2048]{1,0:T(8,128)(2,1)S(1)}, bf16[32,2048]{1,0:T(8,128)(2,1)S(1)}, u32[]{:S(2)}, u32[]{:S(2)}) collective-permute-start(bf16[32,2048]{1,0:T(8,128)(2,1)S(1)} %get-tuple-element.58), channel_id=1, source_target_pairs={{0,7},{1,0},{2,1},{3,2},{4,3},{5,4},{6,5},{7,6},{8,15},{9,8},{10,9... | collective-permute-start | bytes 393224 | tf_op jit(solution)/shard_map/ppermute | solution.py:442
  45.2 2.2 %collective-permute-start.14 = (bf16[32,2048]{1,0:T(8,128)(2,1)S(1)}, bf16[32,2048]{1,0:T(8,128)(2,1)S(1)}, u32[]{:S(2)}, u32[]{:S(2)}) collective-permute-start(bf16[32,2048]{1,0:T(8,128)(2,1)S(1)} %get-tuple-element.65), channel_id=1, source_target_pairs={{0,2},{1,3},{2,4},{3,5},{4,6},{5,7},{6,0},{7,1},{8,10},{9,11},{10,... | collective-permute-start | bytes 393224 | tf_op jit(solution)/shard_map/ppermute | solution.py:442
  47.4 2.0 %collective-permute-start.15 = (bf16[32,2048]{1,0:T(8,128)(2,1)S(1)}, bf16[32,2048]{1,0:T(8,128)(2,1)S(1)}, u32[]{:S(2)}, u32[]{:S(2)}) collective-permute-start(bf16[32,2048]{1,0:T(8,128)(2,1)S(1)} %get-tuple-element.66), channel_id=1, source_target_pairs={{0,6},{1,7},{2,0},{3,1},{4,2},{5,3},{6,4},{7,5},{8,14},{9,15},{10,... | collective-permute-start | bytes 393224 | tf_op jit(solution)/shard_map/ppermute | solution.py:442
  49.4 4.1 %collective-permute-done.14.refs_3_ = bf16[32,2048]{1,0:T(8,128)(2,1)S(1)} collective-permute-done((bf16[32,2048]{1,0:T(8,128)(2,1)S(1)}, bf16[32,2048]{1,0:T(8,128)(2,1)S(1)}, u32[]{:S(2)}, u32[]{:S(2)}) %collective-permute-start.14) | collective-permute-done | bytes 131104 | tf_op jit(solution)/shard_map/ppermute | solution.py:442
  53.6 1.1 %collective-permute-done.15.refs_4_ = bf16[32,2048]{1,0:T(8,128)(2,1)S(1)} collective-permute-done((bf16[32,2048]{1,0:T(8,128)(2,1)S(1)}, bf16[32,2048]{1,0:T(8,128)(2,1)S(1)}, u32[]{:S(2)}, u32[]{:S(2)}) %collective-permute-start.15) | collective-permute-done | bytes 131104 | tf_op jit(solution)/shard_map/ppermute | solution.py:442
  (28 shorter events, 2.5 us)
Async XLA Ops:
  0.0 9.7 %copy-start.1 = (bf16[256,512]{1,0:T(8,128)(2,1)S(1)}, bf16[256,512]{1,0:T(8,128)(2,1)}, u32[]{:S(2)}) copy-start(bf16[256,512]{1,0:T(8,128)(2,1)} %k_ref.1) | copy-start | bytes 786436
  0.0 9.7 %copy-start.4 = (f32[128]{0:T(128)S(1)}, f32[128]{0:T(128)}, u32[]{:S(2)}) copy-start(f32[128]{0:T(128)} %param.14) | copy-start | bytes 1540
  0.0 9.7 %copy-start.3 = (bf16[256,512]{1,0:T(8,128)(2,1)S(1)}, bf16[256,512]{1,0:T(8,128)(2,1)}, u32[]{:S(2)}) copy-start(bf16[256,512]{1,0:T(8,128)(2,1)} %gate_ref.1) | copy-start | bytes 786436
  0.0 9.7 %copy-start.2 = (bf16[256,512]{1,0:T(8,128)(2,1)S(1)}, bf16[256,512]{1,0:T(8,128)(2,1)}, u32[]{:S(2)}) copy-start(bf16[256,512]{1,0:T(8,128)(2,1)} %q_ref.1) | copy-start | bytes 786436
  4.4 1.4 %collective-permute-start = (bf16[2,128,256]{2,1,0:T(8,128)(2,1)S(1)}, bf16[2,128,256]{2,1,0:T(8,128)(2,1)S(1)}, u32[]{:S(2)}, u32[]{:S(2)}) collective-permute-start(bf16[2,128,256]{2,1,0:T(8,128)(2,1)S(1)} %get-tuple-element.37), channel_id=1, source_target_pairs={{0,8},{8,0},{16,24},{24,16},{32,40},{40,32},{48,56},{56,48},{64,72... | collective-permute-start | bytes 393224 | tf_op jit(solution)/shard_map/ppermute | solution.py:432
  6.2 7.9 %collective-permute-start.2 = (bf16[2,128,256]{2,1,0:T(8,128)(2,1)S(1)}, bf16[2,128,256]{2,1,0:T(8,128)(2,1)S(1)}, u32[]{:S(2)}, u32[]{:S(2)}) collective-permute-start(bf16[2,128,256]{2,1,0:T(8,128)(2,1)S(1)} %get-tuple-element.39), channel_id=1, source_target_pairs={{0,32},{8,40},{16,48},{24,56},{32,0},{40,8},{48,16},{56,24},{64,96... | collective-permute-start | bytes 393224 | tf_op jit(solution)/shard_map/ppermute | solution.py:436
  7.5 8.6 %collective-permute-start.3 = (bf16[2,128,256]{2,1,0:T(8,128)(2,1)S(1)}, bf16[2,128,256]{2,1,0:T(8,128)(2,1)S(1)}, u32[]{:S(2)}, u32[]{:S(2)}) collective-permute-start(bf16[2,128,256]{2,1,0:T(8,128)(2,1)S(1)} %get-tuple-element.40), channel_id=1, source_target_pairs={{0,48},{8,56},{16,32},{24,40},{32,16},{40,24},{48,0},{56,8},{64,11... | collective-permute-start | bytes 393224 | tf_op jit(solution)/shard_map/ppermute | solution.py:436
  9.7 6.4 %collective-permute-start.1 = (bf16[2,128,256]{2,1,0:T(8,128)(2,1)S(1)}, bf16[2,128,256]{2,1,0:T(8,128)(2,1)S(1)}, u32[]{:S(2)}, u32[]{:S(2)}) collective-permute-start(bf16[2,128,256]{2,1,0:T(8,128)(2,1)S(1)} %get-tuple-element.38.m_ref), channel_id=1, source_target_pairs={{0,16},{8,24},{16,0},{24,8},{32,48},{40,56},{48,32},{56,40},{64,80... | collective-permute-start | bytes 393224 | tf_op jit(solution)/shard_map/ppermute | solution.py:436
  11.5 16.1 %copy-start = (bf16[512,2048]{1,0:T(8,128)(2,1)S(1)}, bf16[512,2048]{1,0:T(8,128)(2,1)}, u32[]{:S(2)}) copy-start(bf16[512,2048]{1,0:T(8,128)(2,1)} %w_ref.3) | copy-start | bytes 6291460
  16.6 7.0 %collective-permute-start.5 = (bf16[2,128,256]{2,1,0:T(8,128)(2,1)S(1)}, bf16[2,128,256]{2,1,0:T(8,128)(2,1)S(1)}, u32[]{:S(2)}, u32[]{:S(2)}) collective-permute-start(bf16[2,128,256]{2,1,0:T(8,128)(2,1)S(1)} %get-tuple-element.47), channel_id=1, source_target_pairs={{0,128},{8,136},{16,144},{24,152},{32,160},{40,168},{48,176},{56,1... | collective-permute-start | bytes 393224 | tf_op jit(solution)/shard_map/ppermute | solution.py:439
  19.8 6.7 %collective-permute-start.6 = (bf16[2,128,256]{2,1,0:T(8,128)(2,1)S(1)}, bf16[2,128,256]{2,1,0:T(8,128)(2,1)S(1)}, u32[]{:S(2)}, u32[]{:S(2)}) collective-permute-start(bf16[2,128,256]{2,1,0:T(8,128)(2,1)S(1)} %get-tuple-element.48), channel_id=1, source_target_pairs={{0,192},{8,200},{16,208},{24,216},{32,224},{40,232},{48,240},{56,2... | collective-permute-start | bytes 393224 | tf_op jit(solution)/shard_map/ppermute | solution.py:439
  20.9 5.6 %collective-permute-start.4 = (bf16[2,128,256]{2,1,0:T(8,128)(2,1)S(1)}, bf16[2,128,256]{2,1,0:T(8,128)(2,1)S(1)}, u32[]{:S(2)}, u32[]{:S(2)}) collective-permute-start(bf16[2,128,256]{2,1,0:T(8,128)(2,1)S(1)} %get-tuple-element.46.m_ref), channel_id=1, source_target_pairs={{0,64},{8,72},{16,80},{24,88},{32,96},{40,104},{48,112},{56,120},{... | collective-permute-start | bytes 393224 | tf_op jit(solution)/shard_map/ppermute | solution.py:439
  27.5 1.3 %collective-permute-start.7 = (bf16[2,128,128]{2,1,0:T(8,128)(2,1)S(1)}, bf16[2,128,128]{2,1,0:T(8,128)(2,1)S(1)}, u32[]{:S(2)}, u32[]{:S(2)}) collective-permute-start(bf16[2,128,128]{2,1,0:T(8,128)(2,1)S(1)} %get-tuple-element.52), channel_id=1, source_target_pairs={{0,8},{8,0},{16,24},{24,16},{32,40},{40,32},{48,56},{56,48},{64,72... | collective-permute-start | bytes 196616 | tf_op jit(solution)/shard_map/ppermute | solution.py:432
  29.6 15.5 %collective-permute-start.10 = (bf16[32,2048]{1,0:T(8,128)(2,1)S(1)}, bf16[32,2048]{1,0:T(8,128)(2,1)S(1)}, u32[]{:S(2)}, u32[]{:S(2)}) collective-permute-start(bf16[32,2048]{1,0:T(8,128)(2,1)S(1)} %get-tuple-element.60), channel_id=1, source_target_pairs={{0,1},{1,2},{2,3},{3,4},{4,5},{5,6},{6,7},{7,0},{8,9},{9,10},{10,1... | collective-permute-start | bytes 393224 | tf_op jit(solution)/shard_map/ppermute | solution.py:442
  31.6 13.5 %collective-permute-start.12 = (bf16[32,2048]{1,0:T(8,128)(2,1)S(1)}, bf16[32,2048]{1,0:T(8,128)(2,1)S(1)}, u32[]{:S(2)}, u32[]{:S(2)}) collective-permute-start(bf16[32,2048]{1,0:T(8,128)(2,1)S(1)} %get-tuple-element.63), channel_id=1, source_target_pairs={{0,7},{1,0},{2,1},{3,2},{4,3},{5,4},{6,5},{7,6},{8,15},{9,8},{10,9... | collective-permute-start | bytes 393224 | tf_op jit(solution)/shard_map/ppermute | solution.py:442
  35.8 7.4 %collective-permute-start.11 = (bf16[32,1024]{1,0:T(8,128)(2,1)S(1)}, bf16[32,1024]{1,0:T(8,128)(2,1)S(1)}, u32[]{:S(2)}, u32[]{:S(2)}) collective-permute-start(bf16[32,1024]{1,0:T(8,128)(2,1)S(1)} %get-tuple-element.61), channel_id=1, source_target_pairs={{0,2},{1,3},{2,4},{3,5},{4,6},{5,7},{6,0},{7,1},{8,10},{9,11},{10,... | collective-permute-start | bytes 196616 | tf_op jit(solution)/shard_map/ppermute | solution.py:442
  35.8 9.3 %collective-permute-start.13 = (bf16[32,1024]{1,0:T(8,128)(2,1)S(1)}, bf16[32,1024]{1,0:T(8,128)(2,1)S(1)}, u32[]{:S(2)}, u32[]{:S(2)}) collective-permute-start(bf16[32,1024]{1,0:T(8,128)(2,1)S(1)} %get-tuple-element.64), channel_id=1, source_target_pairs={{0,6},{1,7},{2,0},{3,1},{4,2},{5,3},{6,4},{7,5},{8,14},{9,15},{10,... | collective-permute-start | bytes 196616 | tf_op jit(solution)/shard_map/ppermute | solution.py:442
  39.9 9.5 %collective-permute-start.8 = (bf16[32,2048]{1,0:T(8,128)(2,1)S(1)}, bf16[32,2048]{1,0:T(8,128)(2,1)S(1)}, u32[]{:S(2)}, u32[]{:S(2)}) collective-permute-start(bf16[32,2048]{1,0:T(8,128)(2,1)S(1)} %get-tuple-element.57), channel_id=1, source_target_pairs={{0,1},{1,2},{2,3},{3,4},{4,5},{5,6},{6,7},{7,0},{8,9},{9,10},{10,1... | collective-permute-start | bytes 393224 | tf_op jit(solution)/shard_map/ppermute | solution.py:442
  43.2 6.3 %collective-permute-start.9 = (bf16[32,2048]{1,0:T(8,128)(2,1)S(1)}, bf16[32,2048]{1,0:T(8,128)(2,1)S(1)}, u32[]{:S(2)}, u32[]{:S(2)}) collective-permute-start(bf16[32,2048]{1,0:T(8,128)(2,1)S(1)} %get-tuple-element.58), channel_id=1, source_target_pairs={{0,7},{1,0},{2,1},{3,2},{4,3},{5,4},{6,5},{7,6},{8,15},{9,8},{10,9... | collective-permute-start | bytes 393224 | tf_op jit(solution)/shard_map/ppermute | solution.py:442
  45.2 8.4 %collective-permute-start.14 = (bf16[32,2048]{1,0:T(8,128)(2,1)S(1)}, bf16[32,2048]{1,0:T(8,128)(2,1)S(1)}, u32[]{:S(2)}, u32[]{:S(2)}) collective-permute-start(bf16[32,2048]{1,0:T(8,128)(2,1)S(1)} %get-tuple-element.65), channel_id=1, source_target_pairs={{0,2},{1,3},{2,4},{3,5},{4,6},{5,7},{6,0},{7,1},{8,10},{9,11},{10,... | collective-permute-start | bytes 393224 | tf_op jit(solution)/shard_map/ppermute | solution.py:442
  47.4 7.2 %collective-permute-start.15 = (bf16[32,2048]{1,0:T(8,128)(2,1)S(1)}, bf16[32,2048]{1,0:T(8,128)(2,1)S(1)}, u32[]{:S(2)}, u32[]{:S(2)}) collective-permute-start(bf16[32,2048]{1,0:T(8,128)(2,1)S(1)} %get-tuple-element.66), channel_id=1, source_target_pairs={{0,6},{1,7},{2,0},{3,1},{4,2},{5,3},{6,4},{7,5},{8,14},{9,15},{10,... | collective-permute-start | bytes 393224 | tf_op jit(solution)/shard_map/ppermute | solution.py:442

commit v6 on v5

--- a/solution.py
+++ b/solution.py
@@ -327,11 +327,12 @@
     for d, ref in enumerate((m_ref, r1_ref, r2_ref, r3_ref)):
         slots[jnp.bitwise_xor(x, d)] = ref[...]
     for h in range(OWN):
-        state = jnp.where(x > 0, slots[0, h][:, HD:].astype(F32), 0.0)
-        for i in (1, 2):
-            m = slots[i, h]
-            step = dot_exact_left(m[:, :HD], state) + m[:, HD:].astype(F32)
-            state = jnp.where(x > i, step, state)
+        m0, m1, m2 = (slots[i, h] for i in range(3))
+        one = m0[:, HD:]
+        two = dot(m1[:, :HD], one) + m1[:, HD:].astype(F32)
+        three = dot_exact_left(m2[:, :HD], two) + m2[:, HD:].astype(F32)
+        state = jnp.where(x == 1, one.astype(F32), jnp.where(x == 2, two, three))
+        state = jnp.where(x > 0, state, 0.0)
         own, other = own_ref[h], other_ref[h]
         hi, lo = split(dot_sq(own[:, :HD], state) + own[:, HD:])
         keep_ref[h] = lanes(hi, lo)

time: 55.5 us -> 55.5 us (level)
  no operation moved by 1% of the time
where the time goes in v6:
time: 55.5 us; the launch traced here: 55.4 us
  starting transfers between devices  24.5 us (44%)
  waiting for transfers between devices  19.7 us (35%)
  Pallas kernels  11 us (20%)
    ppermute x8, starting transfers between devices, along_z(): return lax.ppermute(a, 'tp', [(i, (i + d) % TP) for i in range(TP)])  16.5 us
    pallas_call x10, Pallas kernels, call(): pl.pallas_call(kernel, out_shape=[jax.ShapeDtypeStruct(s, t) for s, t in...  11 us
    ppermute x8, waiting for transfers between devices, along_z(): return lax.ppermute(a, 'tp', [(i, (i + d) % TP) for i in range(TP)])  8.52 us
    ppermute x3, waiting for transfers between devices, across_x(): lax.ppermute(a, 'ctx', [(i, (i // 8 ^ m) * 8 + i % 8) for i in range(n_ct...  4.77 us
    ppermute x3, waiting for transfers between devices, across_y(): return lax.ppermute(a, 'ctx', pairs)  4.61 us
    ppermute x3, starting transfers between devices, across_x(): lax.ppermute(a, 'ctx', [(i, (i // 8 ^ m) * 8 + i % 8) for i in range(n_ct...  4.27 us
    ppermute x3, starting transfers between devices, across_y(): return lax.ppermute(a, 'ctx', pairs)  3.57 us
    ppermute x2, waiting for transfers between devices, swap(): return lax.ppermute(a, 'ctx', [(i, i ^ 1) for i in range(n_ctx)])  1.81 us
  transfers between devices with their start and end apart: 16, of which 10 were waited for; matrix products, arithmetic and copies ran while one was open for 0% of the time, Pallas kernels for 6%

profile of v6, /device:TPU:24, one launch (start us, length us, event | category | flops | bytes accessed | tf_op | source)
XLA Modules:
  0.0 55.4 jit_solution(1856978626411300177)
XLA Ops:
  0.0 4.4 %shard_map.82 = (bf16[8,256,256]{2,1,0:T(8,128)(2,1)S(1)}, f32[64,128]{1,0:T(8,128)S(1)}, f32[128,64]{1,0:T(8,128)S(1)}, f32[4,128,256]{2,1,0:T(8,128)S(1)}, f32...) custom-call(bf16[256,512]{1,0:T(8,128)(2,1)} %k_ref.1, bf16[256,512]{1,0:T(8,128)(2,1)} %v_hbm.1, ...), custom_call_target="tpu_custom_call" | custom-call | flops 1000000000 | bytes 1048576 | tf_op jit(solution)/shard_map/pallas_call | solution.py:417
  4.5 1.3 %collective-permute-done.recv_ref = bf16[2,128,256]{2,1,0:T(8,128)(2,1)S(1)} collective-permute-done((bf16[2,128,256]{2,1,0:T(8,128)(2,1)S(1)}, bf16[2,128,256]{2,1,0:T(8,128)(2,1)S(1)}, u32[]{:S(2)}, u32[]{:S(2)}) %collective-permute-start) | collective-permute-done | bytes 131104 | tf_op jit(solution)/shard_map/ppermute | solution.py:433
  6.2 1.3 %collective-permute-start.2 = (bf16[2,128,256]{2,1,0:T(8,128)(2,1)S(1)}, bf16[2,128,256]{2,1,0:T(8,128)(2,1)S(1)}, u32[]{:S(2)}, u32[]{:S(2)}) collective-permute-start(bf16[2,128,256]{2,1,0:T(8,128)(2,1)S(1)} %get-tuple-element.39), channel_id=1, source_target_pairs={{0,32},{8,40},{16,48},{24,56},{32,0},{40,8},{48,16},{56,24},{64,96... | collective-permute-start | bytes 393224 | tf_op jit(solution)/shard_map/ppermute | solution.py:437
  7.5 2.2 %collective-permute-start.3 = (bf16[2,128,256]{2,1,0:T(8,128)(2,1)S(1)}, bf16[2,128,256]{2,1,0:T(8,128)(2,1)S(1)}, u32[]{:S(2)}, u32[]{:S(2)}) collective-permute-start(bf16[2,128,256]{2,1,0:T(8,128)(2,1)S(1)} %get-tuple-element.40), channel_id=1, source_target_pairs={{0,48},{8,56},{16,32},{24,40},{32,16},{40,24},{48,0},{56,8},{64,11... | collective-permute-start | bytes 393224 | tf_op jit(solution)/shard_map/ppermute | solution.py:437
  9.7 1.7 %shard_map.84 = (bf16[4,256,128]{2,1,0:T(8,128)(2,1)S(1)}, f32[4,256,128]{2,1,0:T(8,128)S(1)}, f32[4,256,128]{2,1,0:T(8,128)S(1)}) custom-call(bf16[256,512]{1,0:T(8,128)(2,1)S(1)} %copy-done.2, bf16[256,512]{1,0:T(8,128)(2,1)S(1)} %copy-done.1, bf16[8,256,256]{2,1,0:T(8,128)(2,1)S(1)} %get-tuple-element.41.wu_ref, f32[64,128]{1,0:T(8,128)S(1)} %get-tuple-element.42.vec_ref, ...), custom_call_target="tpu_custom_call" | custom-call | flops 1000000000 | bytes 1048576 | tf_op jit(solution)/shard_map/pallas_call | solution.py:417
  11.5 2.6 %collective-permute-done.2.r2_ref = bf16[2,128,256]{2,1,0:T(8,128)(2,1)S(1)} collective-permute-done((bf16[2,128,256]{2,1,0:T(8,128)(2,1)S(1)}, bf16[2,128,256]{2,1,0:T(8,128)(2,1)S(1)}, u32[]{:S(2)}, u32[]{:S(2)}) %collective-permute-start.2) | collective-permute-done | bytes 131104 | tf_op jit(solution)/shard_map/ppermute | solution.py:437
  14.1 2.0 %collective-permute-done.3.r3_ref = bf16[2,128,256]{2,1,0:T(8,128)(2,1)S(1)} collective-permute-done((bf16[2,128,256]{2,1,0:T(8,128)(2,1)S(1)}, bf16[2,128,256]{2,1,0:T(8,128)(2,1)S(1)}, u32[]{:S(2)}, u32[]{:S(2)}) %collective-permute-start.3) | collective-permute-done | bytes 131104 | tf_op jit(solution)/shard_map/ppermute | solution.py:437
  16.6 3.1 %collective-permute-start.5 = (bf16[2,128,256]{2,1,0:T(8,128)(2,1)S(1)}, bf16[2,128,256]{2,1,0:T(8,128)(2,1)S(1)}, u32[]{:S(2)}, u32[]{:S(2)}) collective-permute-start(bf16[2,128,256]{2,1,0:T(8,128)(2,1)S(1)} %get-tuple-element.47), channel_id=1, source_target_pairs={{0,128},{8,136},{16,144},{24,152},{32,160},{40,168},{48,176},{56,1... | collective-permute-start | bytes 393224 | tf_op jit(solution)/shard_map/ppermute | solution.py:440
  19.8 1.1 %collective-permute-start.6 = (bf16[2,128,256]{2,1,0:T(8,128)(2,1)S(1)}, bf16[2,128,256]{2,1,0:T(8,128)(2,1)S(1)}, u32[]{:S(2)}, u32[]{:S(2)}) collective-permute-start(bf16[2,128,256]{2,1,0:T(8,128)(2,1)S(1)} %get-tuple-element.48), channel_id=1, source_target_pairs={{0,192},{8,200},{16,208},{24,216},{32,224},{40,232},{48,240},{56,2... | collective-permute-start | bytes 393224 | tf_op jit(solution)/shard_map/ppermute | solution.py:440
  20.9 0.9 %shard_map.86 = (f32[2,128,256]{2,1,0:T(8,128)S(1)}, f32[2,128,256]{2,1,0:T(8,128)S(1)}) custom-call(bf16[2,128,256]{2,1,0:T(8,128)(2,1)S(1)} %get-tuple-element.38.m_ref, bf16[2,128,256]{2,1,0:T(8,128)(2,1)S(1)} %collective-permute-done.1.r1_ref, bf16[2,128,256]{2,1,0:T(8,128)(2,1)S(1)} %collective-permute-done.2.r2_ref, ...), custom_call_target="tpu_custom_call" | custom-call | flops 100000000 | bytes 1048576 | tf_op jit(solution)/shard_map/pallas_call | solution.py:417
  21.8 1.9 %collective-permute-done.5.r2_ref = bf16[2,128,256]{2,1,0:T(8,128)(2,1)S(1)} collective-permute-done((bf16[2,128,256]{2,1,0:T(8,128)(2,1)S(1)}, bf16[2,128,256]{2,1,0:T(8,128)(2,1)S(1)}, u32[]{:S(2)}, u32[]{:S(2)}) %collective-permute-start.5) | collective-permute-done | bytes 131104 | tf_op jit(solution)/shard_map/ppermute | solution.py:440
  23.7 2.8 %collective-permute-done.6.r3_ref = bf16[2,128,256]{2,1,0:T(8,128)(2,1)S(1)} collective-permute-done((bf16[2,128,256]{2,1,0:T(8,128)(2,1)S(1)}, bf16[2,128,256]{2,1,0:T(8,128)(2,1)S(1)}, u32[]{:S(2)}, u32[]{:S(2)}) %collective-permute-start.6) | collective-permute-done | bytes 131104 | tf_op jit(solution)/shard_map/ppermute | solution.py:440
  26.5 0.9 %shard_map.87 = (bf16[2,128,256]{2,1,0:T(8,128)(2,1)S(1)}, bf16[2,128,128]{2,1,0:T(8,128)(2,1)S(1)}) custom-call(bf16[2,128,256]{2,1,0:T(8,128)(2,1)S(1)} %get-tuple-element.46.m_ref, bf16[2,128,256]{2,1,0:T(8,128)(2,1)S(1)} %collective-permute-done.4.r1_ref, bf16[2,128,256]{2,1,0:T(8,128)(2,1)S(1)} %collective-permute-done.5.r2_ref, ...), custom_call_target="tpu_custom_call" | custom-call | flops 100000000 | bytes 1048576 | tf_op jit(solution)/shard_map/pallas_call | solution.py:417
  27.5 0.8 %shard_map.88.acc_ref = f32[256,2048]{1,0:T(8,128)S(1)} custom-call(bf16[2,128,256]{2,1,0:T(8,128)(2,1)S(1)} %get-tuple-element.53.state_ref, bf16[4,256,128]{2,1,0:T(8,128)(2,1)S(1)} %get-tuple-element.54.qeff_ref, f32[4,256,128]{2,1,0:T(8,128)S(1)} %get-tuple-element.45.after.local_ref, f32[4,256,128]{2,1,0:T(8,128)S(1)} %get-tuple-element.55.factor_ref, ...), custom_call_target="tpu_custom_call" | custom-call | flops 1000000000 | bytes 1048576 | tf_op jit(solution)/shard_map/pallas_call | solution.py:417
  28.8 0.8 %shard_map.89 = (bf16[32,2048]{1,0:T(8,128)(2,1)S(1)}, bf16[32,2048]{1,0:T(8,128)(2,1)S(1)}, bf16[32,2048]{1,0:T(8,128)(2,1)S(1)}, bf16[32,2048]{1,0:T(8,128)(2,...) custom-call(bf16[2,128,128]{2,1,0:T(8,128)(2,1)S(1)} %collective-per, ...), custom_call_target="tpu_custom_call" | custom-call | flops 1000000000 | bytes 1048576 | tf_op jit(solution)/shard_map/pallas_call | solution.py:417
  29.5 2.0 %collective-permute-start.10 = (bf16[32,2048]{1,0:T(8,128)(2,1)S(1)}, bf16[32,2048]{1,0:T(8,128)(2,1)S(1)}, u32[]{:S(2)}, u32[]{:S(2)}) collective-permute-start(bf16[32,2048]{1,0:T(8,128)(2,1)S(1)} %get-tuple-element.60), channel_id=1, source_target_pairs={{0,1},{1,2},{2,3},{3,4},{4,5},{5,6},{6,7},{7,0},{8,9},{9,10},{10,1... | collective-permute-start | bytes 393224 | tf_op jit(solution)/shard_map/ppermute | solution.py:443
  31.5 4.2 %collective-permute-start.12 = (bf16[32,2048]{1,0:T(8,128)(2,1)S(1)}, bf16[32,2048]{1,0:T(8,128)(2,1)S(1)}, u32[]{:S(2)}, u32[]{:S(2)}) collective-permute-start(bf16[32,2048]{1,0:T(8,128)(2,1)S(1)} %get-tuple-element.63), channel_id=1, source_target_pairs={{0,7},{1,0},{2,1},{3,2},{4,3},{5,4},{6,5},{7,6},{8,15},{9,8},{10,9... | collective-permute-start | bytes 393224 | tf_op jit(solution)/shard_map/ppermute | solution.py:443
  35.7 4.1 %collective-permute-start.13 = (bf16[32,1024]{1,0:T(8,128)(2,1)S(1)}, bf16[32,1024]{1,0:T(8,128)(2,1)S(1)}, u32[]{:S(2)}, u32[]{:S(2)}) collective-permute-start(bf16[32,1024]{1,0:T(8,128)(2,1)S(1)} %get-tuple-element.64), channel_id=1, source_target_pairs={{0,6},{1,7},{2,0},{3,1},{4,2},{5,3},{6,4},{7,5},{8,14},{9,15},{10,... | collective-permute-start | bytes 196616 | tf_op jit(solution)/shard_map/ppermute | solution.py:443
  39.9 3.3 %collective-permute-done.11.a4_ref = bf16[32,1024]{1,0:T(8,128)(2,1)S(1)} collective-permute-done((bf16[32,1024]{1,0:T(8,128)(2,1)S(1)}, bf16[32,1024]{1,0:T(8,128)(2,1)S(1)}, u32[]{:S(2)}, u32[]{:S(2)}) %collective-permute-start.11) | collective-permute-done | bytes 65568 | tf_op jit(solution)/shard_map/ppermute | solution.py:443
  43.1 1.9 %collective-permute-start.9 = (bf16[32,2048]{1,0:T(8,128)(2,1)S(1)}, bf16[32,2048]{1,0:T(8,128)(2,1)S(1)}, u32[]{:S(2)}, u32[]{:S(2)}) collective-permute-start(bf16[32,2048]{1,0:T(8,128)(2,1)S(1)} %get-tuple-element.58), channel_id=1, source_target_pairs={{0,7},{1,0},{2,1},{3,2},{4,3},{5,4},{6,5},{7,6},{8,15},{9,8},{10,9... | collective-permute-start | bytes 393224 | tf_op jit(solution)/shard_map/ppermute | solution.py:443
  45.2 2.2 %collective-permute-start.14 = (bf16[32,2048]{1,0:T(8,128)(2,1)S(1)}, bf16[32,2048]{1,0:T(8,128)(2,1)S(1)}, u32[]{:S(2)}, u32[]{:S(2)}) collective-permute-start(bf16[32,2048]{1,0:T(8,128)(2,1)S(1)} %get-tuple-element.65), channel_id=1, source_target_pairs={{0,2},{1,3},{2,4},{3,5},{4,6},{5,7},{6,0},{7,1},{8,10},{9,11},{10,... | collective-permute-start | bytes 393224 | tf_op jit(solution)/shard_map/ppermute | solution.py:443
  47.4 2.0 %collective-permute-start.15 = (bf16[32,2048]{1,0:T(8,128)(2,1)S(1)}, bf16[32,2048]{1,0:T(8,128)(2,1)S(1)}, u32[]{:S(2)}, u32[]{:S(2)}) collective-permute-start(bf16[32,2048]{1,0:T(8,128)(2,1)S(1)} %get-tuple-element.66), channel_id=1, source_target_pairs={{0,6},{1,7},{2,0},{3,1},{4,2},{5,3},{6,4},{7,5},{8,14},{9,15},{10,... | collective-permute-start | bytes 393224 | tf_op jit(solution)/shard_map/ppermute | solution.py:443
  49.4 4.1 %collective-permute-done.14.refs_3_ = bf16[32,2048]{1,0:T(8,128)(2,1)S(1)} collective-permute-done((bf16[32,2048]{1,0:T(8,128)(2,1)S(1)}, bf16[32,2048]{1,0:T(8,128)(2,1)S(1)}, u32[]{:S(2)}, u32[]{:S(2)}) %collective-permute-start.14) | collective-permute-done | bytes 131104 | tf_op jit(solution)/shard_map/ppermute | solution.py:443
  53.5 1.1 %collective-permute-done.15.refs_4_ = bf16[32,2048]{1,0:T(8,128)(2,1)S(1)} collective-permute-done((bf16[32,2048]{1,0:T(8,128)(2,1)S(1)}, bf16[32,2048]{1,0:T(8,128)(2,1)S(1)}, u32[]{:S(2)}, u32[]{:S(2)}) %collective-permute-start.15) | collective-permute-done | bytes 131104 | tf_op jit(solution)/shard_map/ppermute | solution.py:443
  (28 shorter events, 2.5 us)
Async XLA Ops:
  0.0 9.7 %copy-start.1 = (bf16[256,512]{1,0:T(8,128)(2,1)S(1)}, bf16[256,512]{1,0:T(8,128)(2,1)}, u32[]{:S(2)}) copy-start(bf16[256,512]{1,0:T(8,128)(2,1)} %k_ref.1) | copy-start | bytes 786436
  0.0 9.7 %copy-start.4 = (f32[128]{0:T(128)S(1)}, f32[128]{0:T(128)}, u32[]{:S(2)}) copy-start(f32[128]{0:T(128)} %param.14) | copy-start | bytes 1540
  0.0 9.7 %copy-start.3 = (bf16[256,512]{1,0:T(8,128)(2,1)S(1)}, bf16[256,512]{1,0:T(8,128)(2,1)}, u32[]{:S(2)}) copy-start(bf16[256,512]{1,0:T(8,128)(2,1)} %gate_ref.1) | copy-start | bytes 786436
  0.0 9.7 %copy-start.2 = (bf16[256,512]{1,0:T(8,128)(2,1)S(1)}, bf16[256,512]{1,0:T(8,128)(2,1)}, u32[]{:S(2)}) copy-start(bf16[256,512]{1,0:T(8,128)(2,1)} %q_ref.1) | copy-start | bytes 786436
  4.4 1.4 %collective-permute-start = (bf16[2,128,256]{2,1,0:T(8,128)(2,1)S(1)}, bf16[2,128,256]{2,1,0:T(8,128)(2,1)S(1)}, u32[]{:S(2)}, u32[]{:S(2)}) collective-permute-start(bf16[2,128,256]{2,1,0:T(8,128)(2,1)S(1)} %get-tuple-element.37), channel_id=1, source_target_pairs={{0,8},{8,0},{16,24},{24,16},{32,40},{40,32},{48,56},{56,48},{64,72... | collective-permute-start | bytes 393224 | tf_op jit(solution)/shard_map/ppermute | solution.py:433
  6.2 7.9 %collective-permute-start.2 = (bf16[2,128,256]{2,1,0:T(8,128)(2,1)S(1)}, bf16[2,128,256]{2,1,0:T(8,128)(2,1)S(1)}, u32[]{:S(2)}, u32[]{:S(2)}) collective-permute-start(bf16[2,128,256]{2,1,0:T(8,128)(2,1)S(1)} %get-tuple-element.39), channel_id=1, source_target_pairs={{0,32},{8,40},{16,48},{24,56},{32,0},{40,8},{48,16},{56,24},{64,96... | collective-permute-start | bytes 393224 | tf_op jit(solution)/shard_map/ppermute | solution.py:437
  7.5 8.6 %collective-permute-start.3 = (bf16[2,128,256]{2,1,0:T(8,128)(2,1)S(1)}, bf16[2,128,256]{2,1,0:T(8,128)(2,1)S(1)}, u32[]{:S(2)}, u32[]{:S(2)}) collective-permute-start(bf16[2,128,256]{2,1,0:T(8,128)(2,1)S(1)} %get-tuple-element.40), channel_id=1, source_target_pairs={{0,48},{8,56},{16,32},{24,40},{32,16},{40,24},{48,0},{56,8},{64,11... | collective-permute-start | bytes 393224 | tf_op jit(solution)/shard_map/ppermute | solution.py:437
  9.7 6.4 %collective-permute-start.1 = (bf16[2,128,256]{2,1,0:T(8,128)(2,1)S(1)}, bf16[2,128,256]{2,1,0:T(8,128)(2,1)S(1)}, u32[]{:S(2)}, u32[]{:S(2)}) collective-permute-start(bf16[2,128,256]{2,1,0:T(8,128)(2,1)S(1)} %get-tuple-element.38.m_ref), channel_id=1, source_target_pairs={{0,16},{8,24},{16,0},{24,8},{32,48},{40,56},{48,32},{56,40},{64,80... | collective-permute-start | bytes 393224 | tf_op jit(solution)/shard_map/ppermute | solution.py:437
  11.5 16.0 %copy-start = (bf16[512,2048]{1,0:T(8,128)(2,1)S(1)}, bf16[512,2048]{1,0:T(8,128)(2,1)}, u32[]{:S(2)}) copy-start(bf16[512,2048]{1,0:T(8,128)(2,1)} %w_ref.3) | copy-start | bytes 6291460
  16.6 7.0 %collective-permute-start.5 = (bf16[2,128,256]{2,1,0:T(8,128)(2,1)S(1)}, bf16[2,128,256]{2,1,0:T(8,128)(2,1)S(1)}, u32[]{:S(2)}, u32[]{:S(2)}) collective-permute-start(bf16[2,128,256]{2,1,0:T(8,128)(2,1)S(1)} %get-tuple-element.47), channel_id=1, source_target_pairs={{0,128},{8,136},{16,144},{24,152},{32,160},{40,168},{48,176},{56,1... | collective-permute-start | bytes 393224 | tf_op jit(solution)/shard_map/ppermute | solution.py:440
  19.8 6.7 %collective-permute-start.6 = (bf16[2,128,256]{2,1,0:T(8,128)(2,1)S(1)}, bf16[2,128,256]{2,1,0:T(8,128)(2,1)S(1)}, u32[]{:S(2)}, u32[]{:S(2)}) collective-permute-start(bf16[2,128,256]{2,1,0:T(8,128)(2,1)S(1)} %get-tuple-element.48), channel_id=1, source_target_pairs={{0,192},{8,200},{16,208},{24,216},{32,224},{40,232},{48,240},{56,2... | collective-permute-start | bytes 393224 | tf_op jit(solution)/shard_map/ppermute | solution.py:440
  20.9 5.6 %collective-permute-start.4 = (bf16[2,128,256]{2,1,0:T(8,128)(2,1)S(1)}, bf16[2,128,256]{2,1,0:T(8,128)(2,1)S(1)}, u32[]{:S(2)}, u32[]{:S(2)}) collective-permute-start(bf16[2,128,256]{2,1,0:T(8,128)(2,1)S(1)} %get-tuple-element.46.m_ref), channel_id=1, source_target_pairs={{0,64},{8,72},{16,80},{24,88},{32,96},{40,104},{48,112},{56,120},{... | collective-permute-start | bytes 393224 | tf_op jit(solution)/shard_map/ppermute | solution.py:440
  27.4 1.3 %collective-permute-start.7 = (bf16[2,128,128]{2,1,0:T(8,128)(2,1)S(1)}, bf16[2,128,128]{2,1,0:T(8,128)(2,1)S(1)}, u32[]{:S(2)}, u32[]{:S(2)}) collective-permute-start(bf16[2,128,128]{2,1,0:T(8,128)(2,1)S(1)} %get-tuple-element.52), channel_id=1, source_target_pairs={{0,8},{8,0},{16,24},{24,16},{32,40},{40,32},{48,56},{56,48},{64,72... | collective-permute-start | bytes 196616 | tf_op jit(solution)/shard_map/ppermute | solution.py:433
  29.5 15.6 %collective-permute-start.10 = (bf16[32,2048]{1,0:T(8,128)(2,1)S(1)}, bf16[32,2048]{1,0:T(8,128)(2,1)S(1)}, u32[]{:S(2)}, u32[]{:S(2)}) collective-permute-start(bf16[32,2048]{1,0:T(8,128)(2,1)S(1)} %get-tuple-element.60), channel_id=1, source_target_pairs={{0,1},{1,2},{2,3},{3,4},{4,5},{5,6},{6,7},{7,0},{8,9},{9,10},{10,1... | collective-permute-start | bytes 393224 | tf_op jit(solution)/shard_map/ppermute | solution.py:443
  31.5 13.5 %collective-permute-start.12 = (bf16[32,2048]{1,0:T(8,128)(2,1)S(1)}, bf16[32,2048]{1,0:T(8,128)(2,1)S(1)}, u32[]{:S(2)}, u32[]{:S(2)}) collective-permute-start(bf16[32,2048]{1,0:T(8,128)(2,1)S(1)} %get-tuple-element.63), channel_id=1, source_target_pairs={{0,7},{1,0},{2,1},{3,2},{4,3},{5,4},{6,5},{7,6},{8,15},{9,8},{10,9... | collective-permute-start | bytes 393224 | tf_op jit(solution)/shard_map/ppermute | solution.py:443
  35.7 7.4 %collective-permute-start.11 = (bf16[32,1024]{1,0:T(8,128)(2,1)S(1)}, bf16[32,1024]{1,0:T(8,128)(2,1)S(1)}, u32[]{:S(2)}, u32[]{:S(2)}) collective-permute-start(bf16[32,1024]{1,0:T(8,128)(2,1)S(1)} %get-tuple-element.61), channel_id=1, source_target_pairs={{0,2},{1,3},{2,4},{3,5},{4,6},{5,7},{6,0},{7,1},{8,10},{9,11},{10,... | collective-permute-start | bytes 196616 | tf_op jit(solution)/shard_map/ppermute | solution.py:443
  35.7 9.4 %collective-permute-start.13 = (bf16[32,1024]{1,0:T(8,128)(2,1)S(1)}, bf16[32,1024]{1,0:T(8,128)(2,1)S(1)}, u32[]{:S(2)}, u32[]{:S(2)}) collective-permute-start(bf16[32,1024]{1,0:T(8,128)(2,1)S(1)} %get-tuple-element.64), channel_id=1, source_target_pairs={{0,6},{1,7},{2,0},{3,1},{4,2},{5,3},{6,4},{7,5},{8,14},{9,15},{10,... | collective-permute-start | bytes 196616 | tf_op jit(solution)/shard_map/ppermute | solution.py:443
  39.9 9.5 %collective-permute-start.8 = (bf16[32,2048]{1,0:T(8,128)(2,1)S(1)}, bf16[32,2048]{1,0:T(8,128)(2,1)S(1)}, u32[]{:S(2)}, u32[]{:S(2)}) collective-permute-start(bf16[32,2048]{1,0:T(8,128)(2,1)S(1)} %get-tuple-element.57), channel_id=1, source_target_pairs={{0,1},{1,2},{2,3},{3,4},{4,5},{5,6},{6,7},{7,0},{8,9},{9,10},{10,1... | collective-permute-start | bytes 393224 | tf_op jit(solution)/shard_map/ppermute | solution.py:443
  43.1 6.3 %collective-permute-start.9 = (bf16[32,2048]{1,0:T(8,128)(2,1)S(1)}, bf16[32,2048]{1,0:T(8,128)(2,1)S(1)}, u32[]{:S(2)}, u32[]{:S(2)}) collective-permute-start(bf16[32,2048]{1,0:T(8,128)(2,1)S(1)} %get-tuple-element.58), channel_id=1, source_target_pairs={{0,7},{1,0},{2,1},{3,2},{4,3},{5,4},{6,5},{7,6},{8,15},{9,8},{10,9... | collective-permute-start | bytes 393224 | tf_op jit(solution)/shard_map/ppermute | solution.py:443
  45.2 8.3 %collective-permute-start.14 = (bf16[32,2048]{1,0:T(8,128)(2,1)S(1)}, bf16[32,2048]{1,0:T(8,128)(2,1)S(1)}, u32[]{:S(2)}, u32[]{:S(2)}) collective-permute-start(bf16[32,2048]{1,0:T(8,128)(2,1)S(1)} %get-tuple-element.65), channel_id=1, source_target_pairs={{0,2},{1,3},{2,4},{3,5},{4,6},{5,7},{6,0},{7,1},{8,10},{9,11},{10,... | collective-permute-start | bytes 393224 | tf_op jit(solution)/shard_map/ppermute | solution.py:443
  47.4 7.2 %collective-permute-start.15 = (bf16[32,2048]{1,0:T(8,128)(2,1)S(1)}, bf16[32,2048]{1,0:T(8,128)(2,1)S(1)}, u32[]{:S(2)}, u32[]{:S(2)}) collective-permute-start(bf16[32,2048]{1,0:T(8,128)(2,1)S(1)} %get-tuple-element.66), channel_id=1, source_target_pairs={{0,6},{1,7},{2,0},{3,1},{4,2},{5,3},{6,4},{7,5},{8,14},{9,15},{10,... | collective-permute-start | bytes 393224 | tf_op jit(solution)/shard_map/ppermute | solution.py:443
